TPU v7x, 256 devices: a whole 4x4x8 slice. The times are simulated.
256 devices in a mesh: img: 32 (over y, z_lo, core), txt: 8 (over x, z_hi).
Axes of the slice: x: 4, y: 4, z: 8 (z_hi: 2, z_lo: 4; z = z_hi * 4 + z_lo), core: 2. Of those that a mesh axis runs over, the one named last changes fastest.
Arguments:
- images: bfloat16 [16384, 1152], P(('img', 'txt')), may hold values from -6 to 6
- texts: bfloat16 [16384, 1152], P(('img', 'txt')), may hold values from -6 to 6
- log_scale: float32 [], replicated, may hold values from 2 to 3
- bias: float32 [], replicated, may hold values from -3 to -1
Outputs:
- mean_loss: float32 [], replicated
- grad_images: float32 [16384, 1152], P(('img', 'txt'))
- grad_texts: float32 [16384, 1152], P(('img', 'txt'))
- grad_log_scale: float32 [], replicated
- grad_bias: float32 [], replicated
All inputs are finite; a program needn't handle non-finite values.
Results may differ from a plain program's by a relative error of at most 0.0009.
The roundings to bfloat16 on the way count: a program that leaves them out, or rounds other values in their place, can miss the bound.
Values may be sent and summed in bfloat16 or wider, within the bound.
No kernel may reach another device: no remote copies, remote signals or barrier semaphores. Data moves between devices by JAX's collectives and lax.ppermute only.
A program may use at most 64 MiB of HBM per device.

v0:
```python
import jax
import jax.numpy as jnp
from jax import lax
from jax.sharding import PartitionSpec as P

tiny_eps = 1e-06


def unit_rows(values):
    wide = values.astype(jnp.float32)
    lengths = jnp.sqrt(jnp.sum(wide * wide, axis=-1, keepdims=True) + tiny_eps)
    return (wide / lengths, lengths)


def project_back(unit, direction, lengths):
    along = jnp.sum(unit * direction, axis=-1, keepdims=True)
    return (direction - unit * along) / lengths


def shards(images, texts, log_scale, bias):
    pairs = images.shape[0]
    img_pos = lax.axis_index("img")
    txt_pos = lax.axis_index("txt")
    unit_img, img_len = unit_rows(images)
    unit_txt, txt_len = unit_rows(texts)
    img_block = lax.all_gather(unit_img.astype(jnp.bfloat16), "txt", axis=0, tiled=True)
    txt_block = lax.all_gather(unit_txt.astype(jnp.bfloat16), "img", axis=0, tiled=True)
    scale = jnp.exp(log_scale)
    dots = lax.dot_general(
        img_block, txt_block, (((1,), (1,)), ((), ())), preferred_element_type=jnp.float32
    )
    logits = scale * dots + bias
    rows = jnp.arange(img_block.shape[0], dtype=jnp.int32)[:, None]
    columns = jnp.arange(txt_block.shape[0], dtype=jnp.int32)[None, :]
    positive = jnp.logical_and(
        columns // pairs == img_pos, rows == txt_pos * pairs + columns % pairs
    )
    sign = jnp.where(positive, jnp.float32(1.0), jnp.float32(-1.0))
    losses = -jax.nn.log_sigmoid(sign * logits)
    slopes = -sign * jax.nn.sigmoid(-sign * logits)
    weights = (scale * slopes).astype(jnp.bfloat16)
    image_term = jnp.dot(weights, txt_block, preferred_element_type=jnp.float32)
    img_dir = lax.psum_scatter(image_term, "txt", scatter_dimension=0, tiled=True)
    text_term = lax.dot_general(
        weights, img_block, (((0,), (0,)), ((), ())), preferred_element_type=jnp.float32
    )
    text_dir = lax.psum_scatter(text_term, "img", scatter_dimension=0, tiled=True)
    loss_sum, slope_sum, curve_sum = lax.psum(
        (jnp.sum(losses), jnp.sum(slopes), jnp.sum(slopes * dots)), ("img", "txt")
    )
    total = float(pairs * lax.axis_size("img") * lax.axis_size("txt"))
    count = total * total
    grad_images = project_back(unit_img, img_dir, img_len)
    grad_texts = project_back(unit_txt, text_dir, txt_len)
    mean_loss = loss_sum / count
    grad_log_scale = scale * curve_sum / count
    grad_bias = slope_sum / count
    return (mean_loss, grad_images, grad_texts, grad_log_scale, grad_bias)


def solution(mesh):
    return jax.shard_map(
        shards,
        mesh=mesh,
        in_specs=(P(("img", "txt"), None), P(("img", "txt"), None), P(), P()),
        out_specs=(P(), P(("img", "txt"), None), P(("img", "txt"), None), P(), P()),
        check_vma=False,
    )
```

profile of v0, /device:TPU:1, one launch (start us, length us, event | category | flops | bytes accessed | tf_op | source)
XLA Modules:
  0.0 430.6 jit_solution(1660601261387753566)
XLA Ops:
  7.2 0.0 all-gather.3.cloned.1.call-start
  7.2 1.0 fusion.11
  8.3 1.7 fusion.22
  9.9 0.0 all-gather.3.cloned.1.call-update
  10.0 0.0 all-gather.5.cloned.1.call-start
  10.0 1.0 fusion.12
  11.1 1.7 fusion.23
  12.8 0.0 all-gather.5.cloned.1.call-update
  12.8 0.0 reduce-scatter.3.cloned.1.call-start
  14.2 63.1 %all-gather.3.cloned.1.call-done = bf16[512,1152]{1,0:T(8,128)(2,1)} async-done(((bf16[64,1152]{1,0:T(8,128)(2,1)}), bf16[512,1152]{1,0:T(8,128)(2,1)}) %all-gather.3.cloned.1.call-update) | async-done | bytes 1179664 | tf_op jit(solution)/shard_map/all_gather | solution.py:26
  77.3 64.0 %all-gather.5.cloned.1.call-done = bf16[2048,1152]{1,0:T(8,128)(2,1)} async-done(((bf16[64,1152]{1,0:T(8,128)(2,1)}), bf16[2048,1152]{1,0:T(8,128)(2,1)}) %all-gather.5.cloned.1.call-update) | async-done | bytes 4718608 | tf_op jit(solution)/shard_map/all_gather | solution.py:27
  141.4 10.4 %fusion.25 = (f32[]{:T(128)}, f32[]{:T(128)}, f32[]{:T(128)}, f32[512,2048]{1,0:T(8,128)S(1)}) fusion(f32[]{:T(128)S(6)} %copy.10, f32[]{:T(128)S(6)} %exp.11, s32[2048]{0:T(1024)S(1)} %fusion.20, pred[2048]{0:T(1024)(128)(4,1)S(1)} %fusion.19, bf16[512,1152]{1,0:T(8,128)(2,1)} %all-gather.3.cloned.1.call-done, ...), kind=kOutput, calls=%fused_computation.45 | convolution fusion | flops 2440036352 | bytes 10102804 | tf_op jit(solution)/shard_map/dot_general | solution.py:29
  151.8 2.1 copy-done.4
  153.9 6.1 %fusion.10 = f32[512,1152]{1,0:T(8,128)} fusion(bf16[2048,1152]{1,0:T(8,128)(2,1)S(1)} %copy-done.2, f32[]{:T(128)S(6)} %exp.11, f32[512,2048]{1,0:T(8,128)S(1)} %get-tuple-element.11, f32[]{:T(128)S(6)} %copy.10, s32[2048]{0:T(1024)S(1)} %fusion.20, pred[2048]{0:T(1024)(128)(4,1)S(1)} %fusion.19), kind=kOutput, calls=%fused_computation.17 | convolution fusion | flops 2429550592 | bytes 11282440 | tf_op jit(solution)/shard_map/dot_general | solution.py:42
  159.9 0.0 reduce-scatter.3.cloned.1.call-update
  160.0 0.2 reduce-scatter.5.cloned.1.call-start
  160.2 10.4 %fusion.9 = f32[2048,1152]{1,0:T(8,128)} fusion(bf16[512,1152]{1,0:T(8,128)(2,1)S(1)} %copy-done.3, f32[]{:T(128)S(6)} %exp.11, f32[512,2048]{1,0:T(8,128)} %copy-done.4, f32[]{:T(128)S(6)} %copy.10, s32[2048]{0:T(1024)S(1)} %fusion.20, pred[2048]{0:T(1024)(128)(4,1)S(1)} %fusion.19), kind=kOutput, calls=%fused_computation.16 | convolution fusion | flops 2429550592 | bytes 14821384 | tf_op jit(solution)/shard_map/dot_general | solution.py:44
  170.6 81.1 %all-reduce = (f32[]{:T(128)}, f32[]{:T(128)}, f32[]{:T(128)}) all-reduce(f32[]{:T(128)} %get-tuple-element.7, f32[]{:T(128)} %get-tuple-element.6, f32[]{:T(128)} %get-tuple-element.5), channel_id=1, replica_groups=mesh['img'=32,'txt'=8] {'img','txt'}, use_global_device_ids=true, to_apply=%region_3.4 | all-reduce | flops 3 | bytes 24 | tf_op jit(solution)/shard_map/psum | solution.py:48
  253.6 3.4 reduce-scatter.3.cloned.1.call-done
  257.0 1.2 multiply_reduce_fusion.2
  258.1 1.8 subtract_divide_fusion.1
  260.0 157.7 %reduce-scatter.5.cloned.1.call-done = f32[64,1152]{1,0:T(8,128)} async-done(((f32[2048,1152]{1,0:T(8,128)}), f32[64,1152]{1,0:T(8,128)}) %reduce-scatter.5.cloned.1.call-update) | async-done | bytes 294928 | tf_op jit(solution)/shard_map/reduce_scatter | solution.py:47
  417.7 1.2 multiply_reduce_fusion.1
  418.8 1.8 subtract_divide_fusion
  (14 shorter events, 0.1 us)
Async XLA Ops:
  7.2 70.2 %all-gather.3.cloned.1.call-start = ((), (), s32[]{:S(2)}) async-start(), calls=%async_computation.2 | async-start | bytes 1327104 | tf_op jit(solution)/shard_map/all_gather | solution.py:26
  10.0 131.4 %all-gather.5.cloned.1.call-start = ((), (), s32[]{:S(2)}) async-start(), calls=%async_computation.3 | async-start | bytes 4866048 | tf_op jit(solution)/shard_map/all_gather | solution.py:27
  12.8 244.2 %reduce-scatter.3.cloned.1.call-start = ((), (), s32[]{:S(2)}) async-start(), calls=%async_computation.4 | async-start | bytes 2654208 | tf_op jit(solution)/shard_map/reduce_scatter | solution.py:43
  141.4 12.5 %copy-start.2 = (bf16[2048,1152]{1,0:T(8,128)(2,1)S(1)}, bf16[2048,1152]{1,0:T(8,128)(2,1)}, u32[]{:S(2)}) copy-start(bf16[2048,1152]{1,0:T(8,128)(2,1)} %all-gather.5.cloned.1.call-done) | copy-start | bytes 14155780
  151.8 2.1 copy-start.4
  153.9 6.3 %copy-start.3 = (bf16[512,1152]{1,0:T(8,128)(2,1)S(1)}, bf16[512,1152]{1,0:T(8,128)(2,1)}, u32[]{:S(2)}) copy-start(bf16[512,1152]{1,0:T(8,128)(2,1)} %all-gather.3.cloned.1.call-done) | copy-start | bytes 3538948
  160.0 257.7 %reduce-scatter.5.cloned.1.call-start = ((), (), s32[]{:S(2)}) async-start(), calls=%async_computation.5 | async-start | bytes 9732096 | tf_op jit(solution)/shard_map/reduce_scatter | solution.py:47
  170.6 86.4 %copy-start = (bf16[64,1152]{1,0:T(8,128)(2,1)S(1)}, bf16[64,1152]{1,0:T(8,128)(2,1)}, u32[]{:S(2)}) copy-start(bf16[64,1152]{1,0:T(8,128)(2,1)} %param.4) | copy-start | bytes 442372
  170.6 247.1 %copy-start.1 = (bf16[64,1152]{1,0:T(8,128)(2,1)S(1)}, bf16[64,1152]{1,0:T(8,128)(2,1)}, u32[]{:S(2)}) copy-start(bf16[64,1152]{1,0:T(8,128)(2,1)} %param.5) | copy-start | bytes 442372
Sparse Core Ops, SparseCore 0:
  11.2 66.1 all-gather.2
  79.8 61.5 all-gather.4
  160.1 96.8 reduce-scatter.2
  259.6 158.0 reduce-scatter.4
where the time goes:
time: 435 us; the launch traced here: 431 us
  waiting for transfers between devices  288 us (66%)
  blocking collectives  81.1 us (19%)
  matrix products  26.9 us (6%)
  between operations  20.5 us (5%)
  other arithmetic  11.4 us (3%)
    reduce_scatter x1, waiting for transfers between devices, shards(): lax.psum_scatter(text_term, 'img', scatter_dimension=0, tiled=True)  158 us
    psum x1, blocking collectives, shards(): lax.psum((jnp.sum(losses), jnp.sum(slopes), jnp.sum(slopes * dots)), ('im...  81.1 us
    all_gather x1, waiting for transfers between devices, shards(): lax.all_gather(unit_txt.astype(jnp.bfloat16), 'img', axis=0, tiled=True)  64 us
    all_gather x1, waiting for transfers between devices, shards(): lax.all_gather(unit_img.astype(jnp.bfloat16), 'txt', axis=0, tiled=True)  63.1 us
    dot_general x1, matrix products, shards(): lax.dot_general(img_block, txt_block, (((1,), (1,)), ((), ())), preferred...  10.4 us
    dot_general x1, matrix products, shards(): lax.dot_general(weights, img_block, (((0,), (0,)), ((), ())), preferred_e...  10.4 us
  transfers between devices with their start and end apart: 4, of which 4 were waited for; matrix products, arithmetic and copies ran while one was open for 4% of the time, Pallas kernels for 0%

commit v1 on v0

v1 whole, which is shorter than its diff:
```python
import itertools

import jax
import jax.numpy as jnp
from jax import lax
from jax.experimental import pallas as pl
from jax.experimental.pallas import tpu as pltpu
from jax.sharding import Mesh, PartitionSpec as P

tiny_eps = 1e-06
LOG2E = 1.4426950408889634
LN2 = 0.6931471805599453
F32, BF16, F16 = jnp.float32, jnp.bfloat16, jnp.float16
DOWN, UP = 0.125, 8.0

AXES = ("y", "zl", "c", "x", "zh")
SIZES = (4, 4, 2, 4, 2)
COORDS = list(itertools.product(*[range(s) for s in SIZES]))
PLACE = {coord: n for n, coord in enumerate(COORDS)}


def place(y, z, c, x):
    return PLACE[(y % 4, z % 4, c, x % 4, (z % 8) // 4)]


def permute(move, value):
    pairs = []
    for y, zl, c, x, zh in COORDS:
        z = zh * 4 + zl
        pairs.append((place(y, z, c, x), place(*move(y, z, c, x))))
    return lax.ppermute(value, AXES, pairs)


def first(k, v):
    return permute(lambda y, z, c, x: (y, z, c, x + k) if c == 0 else (y + k, z, c, x), v)


def second(k, v):
    return permute(lambda y, z, c, x: (y + k, z, c, x) if c == 0 else (y, z, c, x + k), v)


def along_z(k, v):
    return permute(lambda y, z, c, x: (y, z + k, c, x) if c == 0 else (y, z - k, c, x), v)


def sibling(v):
    return permute(lambda y, z, c, x: (y, z, 1 - c, x), v)


def low(sums):
    return (sums * DOWN).astype(F16)


def normalise_kernel(images, texts, img_low, txt_low):
    for src, dst in ((images, img_low), (texts, txt_low)):
        wide = src[...].astype(F32)
        length = jnp.sqrt(jnp.sum(wide * wide, axis=-1, keepdims=True) + tiny_eps)
        dst[...] = (wide / length).astype(BF16)


def fold_rows(value):
    rows, cols = value.shape
    return jnp.sum(value.reshape(rows // 8, 8, cols), axis=0)


def product_rows(value):
    while value.shape[0] > 8:
        half = value.shape[0] // 2
        value = value[:half] * value[half:]
    return value


def pair_kernel(sc, *refs):
    imgs, txts = refs[:9], refs[9:13]
    w_ref, keep, send, sums, x_ref, y_ref = refs[13:]
    at = 0
    for r in imgs:
        x_ref[at : at + r.shape[0], :] = r[...]
        at += r.shape[0]
    at = 0
    for r in txts:
        y_ref[at : at + r.shape[0], :] = r[...]
        at += r.shape[0]
    scale = sc[0]
    bias = sc[1]
    lift = jnp.zeros((8, 256), F32)
    logs = jnp.zeros((8, 256), F32)
    slope_acc = jnp.zeros((8, 256), F32)
    curve_acc = jnp.zeros((8, 256), F32)
    for i in range(4):
        for j in range(4):
            dots = lax.dot_general(
                x_ref[i * 256 : i * 256 + 256, :],
                y_ref[j * 256 : j * 256 + 256, :],
                (((1,), (1,)), ((), ())),
                preferred_element_type=F32,
            )
            z = (scale * dots + bias) * LOG2E
            if i == 0 and j == 0:
                row = lax.broadcasted_iota(jnp.int32, (256, 256), 0)
                col = lax.broadcasted_iota(jnp.int32, (256, 256), 1)
                positive = jnp.logical_and(row == col, row < 64)
                z = jnp.where(positive, -z, z)
            e = jnp.exp2(-jnp.abs(z))
            whole = 1.0 + e
            r = 1.0 / whole
            slope = jnp.where(z >= 0.0, r, e * r)
            if i == 0 and j == 0:
                slope = jnp.where(positive, -slope, slope)
            lift += fold_rows(jnp.maximum(z, 0.0))
            logs += jnp.log(product_rows(whole))
            slope_acc += fold_rows(slope)
            curve_acc += fold_rows(slope * dots)
            w_ref[i * 256 : i * 256 + 256, j * 256 : j * 256 + 256] = (scale * slope).astype(BF16)
    loss = LN2 * jnp.sum(lift) + jnp.sum(logs)
    row = lax.broadcasted_iota(jnp.int32, (8, 128), 0)
    sums[...] = jnp.where(
        row == 0, loss, jnp.where(row == 1, jnp.sum(slope_acc), jnp.where(row == 2, jnp.sum(curve_acc), 0.0))
    )
    for lo, hi in ((576, 800), (800, 1024)):
        part = jnp.dot(w_ref[lo:hi, :], y_ref[...], preferred_element_type=F32)
        send[lo - 576 : hi - 576, :] = part
    for lo, hi in ((0, 192), (192, 384), (384, 576)):
        keep[lo:hi, :] = jnp.dot(w_ref[lo:hi, :], y_ref[...], preferred_element_type=F32)


def text_kernel(w_ref, *refs):
    imgs = refs[:9]
    own, back, fore, over, x_ref = refs[9:]
    at = 0
    for r in imgs:
        x_ref[at : at + r.shape[0], :] = r[...]
        at += r.shape[0]
    for j, out in ((1, back), (2, fore), (3, over), (0, own)):
        part = lax.dot_general(
            w_ref[:, j * 256 : j * 256 + 256],
            x_ref[...],
            (((0,), (0,)), ((), ())),
            preferred_element_type=F32,
        )
        out[...] = part


def project_kernel(images, texts, img_dir, txt_dir, grad_images, grad_texts):
    for src, sums, dst in ((images, img_dir, grad_images), (texts, txt_dir, grad_texts)):
        direction = sums[...]
        wide = src[...].astype(F32)
        length = jnp.sqrt(jnp.sum(wide * wide, axis=-1, keepdims=True) + tiny_eps)
        unit = wide / length
        along = jnp.sum(unit * direction, axis=-1, keepdims=True)
        dst[...] = (direction - unit * along) / length


def shards(images, texts, log_scale, bias):
    rows, d = images.shape
    arr = jax.ShapeDtypeStruct
    img_low, txt_low = pl.pallas_call(
        normalise_kernel, out_shape=(arr((rows, d), BF16), arr((rows, d), BF16)), name="normalise"
    )(images, texts)
    scale = jnp.exp(log_scale)
    scalars = jnp.stack([scale, bias])

    pair = jnp.concatenate([img_low, sibling(img_low)], axis=0)
    r1 = along_z(1, pair)
    r2 = along_z(2, pair)
    a, b, c = first(1, txt_low), first(-1, txt_low), first(2, txt_low)
    block = jnp.concatenate([txt_low, a, b, c], axis=0)
    r3 = along_z(1, r2)
    r4 = along_z(2, r2[:64])
    ta, tb, tc = second(1, block), second(-1, block), second(2, block)
    imgs = (pair, r1, r2, r3, r4, sibling(r1), sibling(r2), sibling(r3), sibling(r4))
    txts = (block, ta, tb, tc)

    vmem = pl.BlockSpec(memory_space=pltpu.VMEM)
    w, keep, send, sums = pl.pallas_call(
        pair_kernel,
        in_specs=[pl.BlockSpec(memory_space=pltpu.SMEM)] + [vmem] * 13,
        out_specs=[vmem] * 4,
        out_shape=(arr((1024, 1024), BF16), arr((576, d), F32), arr((448, d), F32), arr((8, 128), F32)),
        scratch_shapes=[pltpu.VMEM((1024, d), BF16), pltpu.VMEM((1024, d), BF16)],
        compiler_params=pltpu.CompilerParams(vmem_limit_bytes=48 * 1024 * 1024),
        cost_estimate=pl.CostEstimate(flops=4 * 1024 * 1024 * 1152, bytes_accessed=12_000_000, transcendentals=2 * 1024 * 1024),
        name="pairs",
    )(scalars, *imgs, *txts)
    got = sibling(low(send))

    t_own, t_back, t_fore, t_over = pl.pallas_call(
        text_kernel,
        in_specs=[vmem] * 10,
        out_specs=[vmem] * 4,
        out_shape=(arr((256, d), F32),) * 4,
        scratch_shapes=[pltpu.VMEM((1024, d), BF16)],
        compiler_params=pltpu.CompilerParams(vmem_limit_bytes=48 * 1024 * 1024),
        cost_estimate=pl.CostEstimate(flops=2 * 1024 * 1024 * 1152, bytes_accessed=8_000_000, transcendentals=0),
        name="texts",
    )(w, *imgs)

    chain = keep[128:] * DOWN + got.astype(F32)
    g3 = along_z(-1, chain[256:384].astype(F16))
    g4 = along_z(-2, chain[384:448].astype(F16))
    c2 = chain[128:256] + g3.astype(F32) + jnp.pad(g4.astype(F32), ((0, 64), (0, 0)))
    g1 = along_z(-1, chain[0:128].astype(F16))
    g2 = along_z(-2, c2.astype(F16))
    mine = keep[:128] + (g1.astype(F32) + g2.astype(F32)) * UP
    img_dir = mine[:64] + sibling(mine[64:])

    s1, s2, s3 = second(-1, low(t_back)), second(1, low(t_fore)), second(2, low(t_over))
    t_sum = t_own + (s1.astype(F32) + s2.astype(F32) + s3.astype(F32)) * UP
    t_low = low(t_sum[64:])
    f1, f2, f3 = first(-1, t_low[0:64]), first(1, t_low[64:128]), first(2, t_low[128:192])
    txt_dir = t_sum[:64] + (f1.astype(F32) + f2.astype(F32) + f3.astype(F32)) * UP

    grad_images, grad_texts = pl.pallas_call(
        project_kernel, out_shape=(arr((rows, d), F32), arr((rows, d), F32)), name="project"
    )(images, texts, img_dir, txt_dir)

    sums = sums + sibling(sums)
    for bit in (1, 2, 4):
        sums = sums + permute(lambda y, z, c, x: (y, z ^ bit, c, x), sums)
    for bit in (1, 2):
        sums = sums + permute(lambda y, z, c, x: (y ^ bit, z, c, x), sums)
        sums = sums + permute(lambda y, z, c, x: (y, z, c, x ^ bit), sums)
    total = float(rows * 256)
    count = total * total
    return (sums[0, 0] / count, grad_images, grad_texts, scale * sums[2, 0] / count, sums[1, 0] / count)


def solution(mesh):
    fine = Mesh(mesh.devices.reshape(SIZES), AXES)
    rows = P(AXES, None)
    return jax.shard_map(
        shards,
        mesh=fine,
        in_specs=(rows, rows, P(), P()),
        out_specs=(P(), rows, rows, P(), P()),
        check_vma=False,
    )
```

time: 435 us -> 151 us (0.35)
  waiting for transfers between devices: 288 us -> 46.8 us
  blocking collectives: 81.1 us -> 0 us
  starting transfers between devices: 0.34 us -> 61.2 us
  matrix products: 26.9 us -> 0 us
  Pallas kernels: 0 us -> 20.5 us
  between operations: 20.5 us -> 7.47 us
    reduce_scatter x2 -> x0, waiting for transfers between devices: 161 us -> none  [the longest x1 158 us: shards(): lax.psum_scatter(text_term, 'img', scatter_dimension=0, tiled=True)]
    all_gather x2 -> x0, waiting for transfers between devices: 127 us -> none  [the longest x1 64 us: shards(): lax.all_gather(unit_txt.astype(jnp.bfloat16), 'img', axis=0, tiled=True)]
    psum x1 -> x0, blocking collectives: 81.1 us -> none  [shards(): lax.psum((jnp.sum(losses), jnp.sum(slopes), jnp.sum(slopes * dots)), ('im...]
    ppermute x0 -> x35, starting transfers between devices: none -> 61.2 us  [permute(): return lax.ppermute(value, AXES, pairs)]
    ppermute x0 -> x35, waiting for transfers between devices: none -> 46.8 us  [permute(): return lax.ppermute(value, AXES, pairs)]
    dot_general x3 -> x0, matrix products: 26.9 us -> none  [the longest x1 10.4 us: shards(): lax.dot_general(img_block, txt_block, (((1,), (1,)), ((), ())), preferred...]
    pallas_call x0 -> x4, Pallas kernels: none -> 20.5 us  [the longest x1 11.2 us: shards(): pl.pallas_call(pair_kernel, in_specs=[pl.BlockSpec(memory_space=pltpu.SME...]
    reduce_sum x4 -> x0, other arithmetic: 4.42 us -> none  [the longest x2 2.34 us: project_back(): along = jnp.sum(unit * direction, axis=-1, keepdims=True)]
  transfers between devices with their start and end apart: 4 -> 35, of which waited for: 4 -> 19; matrix products, arithmetic and copies ran while one was open for 4% -> 4% of each run, Pallas kernels for 0% -> 0%
where the time goes in v1:
time: 151 us; the launch traced here: 149 us
  starting transfers between devices  61.2 us (41%)
  waiting for transfers between devices  46.8 us (31%)
  Pallas kernels  20.5 us (14%)
  between operations  7.47 us (5%)
  other arithmetic  7.12 us (5%)
  local copies, waits for them, and re-layouts  6.17 us (4%)
    ppermute x35, starting transfers between devices, permute(): return lax.ppermute(value, AXES, pairs)  61.2 us
    ppermute x35, waiting for transfers between devices, permute(): return lax.ppermute(value, AXES, pairs)  46.8 us
    pallas_call x1, Pallas kernels, shards(): pl.pallas_call(pair_kernel, in_specs=[pl.BlockSpec(memory_space=pltpu.SME...  11.2 us
    unnamed x22, local copies, waits for them, and re-layouts  5.37 us
    pallas_call x1, Pallas kernels, shards(): pl.pallas_call(text_kernel, in_specs=[vmem] * 10, out_specs=[vmem] * 4, o...  5.22 us
    convert_element_type x5, other arithmetic, low(): return (sums * DOWN).astype(F16)  3.08 us
  transfers between devices with their start and end apart: 35, of which 19 were waited for; matrix products, arithmetic and copies ran while one was open for 4% of the time, Pallas kernels for 0%

profile of v1, /device:TPU:1, one launch (start us, length us, event | category | flops | bytes accessed | tf_op | source)
XLA Modules:
  0.0 149.3 jit_solution(7132928626059990032)
XLA Ops:
  2.5 3.7 %collective-permute-start.11 = (bf16[64,1152]{1,0:T(8,128)(2,1)}, bf16[64,1152]{1,0:T(8,128)(2,1)S(1)}, u32[]{:S(2)}, u32[]{:S(2)}) collective-permute-start(bf16[64,1152]{1,0:T(8,128)(2,1)} %get-tuple-element.18), channel_id=1, source_target_pairs={{0,4},{1,5},{2,6},{3,7},{4,0},{5,1},{6,2},{7,3},{8,136},{9,137},{1... | collective-permute-start | bytes 442376 | tf_op jit(solution)/shard_map/ppermute | solution.py:31
  10.2 6.1 %collective-permute-start.2 = (bf16[128,1152]{1,0:T(8,128)(2,1)S(1)}, bf16[128,1152]{1,0:T(8,128)(2,1)S(1)}, u32[]{:S(2)}, u32[]{:S(2)}) collective-permute-start(bf16[128,1152]{1,0:T(8,128)(2,1)S(1)} %constant_dynamic-update-slice_fusion.refs_0_), channel_id=1, source_target_pairs={{0,32},{1,33},{2,34},{3,35},{4,36},{5,37},{6,38},{7,39},{8,41},{9,... | collective-permute-start | bytes 884744 | tf_op jit(solution)/shard_map/ppermute | solution.py:31
  18.1 5.1 %collective-permute-done.2.refs_2_ = bf16[128,1152]{1,0:T(8,128)(2,1)S(1)} collective-permute-done((bf16[128,1152]{1,0:T(8,128)(2,1)S(1)}, bf16[128,1152]{1,0:T(8,128)(2,1)S(1)}, u32[]{:S(2)}, u32[]{:S(2)}) %collective-permute-start.2) | collective-permute-done | bytes 294944 | tf_op jit(solution)/shard_map/ppermute | solution.py:31
  23.2 4.2 %collective-permute-start.4 = (bf16[64,1152]{1,0:T(8,128)(2,1)S(1)}, bf16[64,1152]{1,0:T(8,128)(2,1)S(1)}, u32[]{:S(2)}, u32[]{:S(2)}) collective-permute-start(bf16[64,1152]{1,0:T(8,128)(2,1)S(1)} %slice.71), channel_id=1, source_target_pairs={{0,32},{1,33},{2,34},{3,35},{4,36},{5,37},{6,38},{7,39},{8,41},{9,... | collective-permute-start | bytes 442376 | tf_op jit(solution)/shard_map/ppermute | solution.py:31
  27.4 3.5 %collective-permute-done.4.refs_4_ = bf16[64,1152]{1,0:T(8,128)(2,1)S(1)} collective-permute-done((bf16[64,1152]{1,0:T(8,128)(2,1)S(1)}, bf16[64,1152]{1,0:T(8,128)(2,1)S(1)}, u32[]{:S(2)}, u32[]{:S(2)}) %collective-permute-start.4) | collective-permute-done | bytes 147488 | tf_op jit(solution)/shard_map/ppermute | solution.py:31
  36.8 2.4 %collective-permute-start.3 = (bf16[128,1152]{1,0:T(8,128)(2,1)S(1)}, bf16[128,1152]{1,0:T(8,128)(2,1)}, u32[]{:S(2)}, u32[]{:S(2)}) collective-permute-start(bf16[128,1152]{1,0:T(8,128)(2,1)S(1)} %collective-permute-done.2.refs_2_), channel_id=1, source_target_pairs={{0,16},{1,17},{2,18},{3,19},{4,20},{5,21},{6,22},{7,23},{8,57},{9,... | collective-permute-start | bytes 884744 | tf_op jit(solution)/shard_map/ppermute | solution.py:31
  40.2 3.6 %collective-permute-done.3.refs_3_ = bf16[128,1152]{1,0:T(8,128)(2,1)} collective-permute-done((bf16[128,1152]{1,0:T(8,128)(2,1)S(1)}, bf16[128,1152]{1,0:T(8,128)(2,1)}, u32[]{:S(2)}, u32[]{:S(2)}) %collective-permute-start.3) | collective-permute-done | bytes 294944 | tf_op jit(solution)/shard_map/ppermute | solution.py:31
  50.0 11.2 %pairs.1 = (bf16[1024,1024]{1,0:T(8,128)(2,1)}, f32[576,1152]{1,0:T(8,128)}, f32[448,1152]{1,0:T(8,128)}, f32[8,128]{1,0:T(8,128)S(1)}) custom-call(f32[2]{0:T(128)S(1)} %pad_maximum_fusion.sc, bf16[128,1152]{1,0:T(8,128)(2,1)S(1)} %constant_dynamic-update-slice_fusion.refs_0_, bf16[128,1152]{1,0:T(8,128)(2,1)S(1)} %collective-permute-done.1.refs_1_, ...), custom_call_target="tpu_custom_call" | custom-call | flops 4831838208 | bytes 12000000 | tf_op jit(solution)/shard_map/pairs/pallas_call | solution.py:175
  61.2 5.2 %texts.4 = (f32[256,1152]{1,0:T(8,128)S(1)}, f32[256,1152]{1,0:T(8,128)S(1)}, f32[256,1152]{1,0:T(8,128)S(1)}, f32[256,1152]{1,0:T(8,128)}) custom-call(bf16[1024,1024]{1,0:T(8,128)(2,1)} %get-tuple-element.22.w_ref, bf16[128,1152]{1,0:T(8,128)(2,1)S(1)} %constant_dynamic-update-slice_fusion.refs_0_, bf16[128,1152]{1,0:T(8,128)(2,1)S(1)} %collective-permute-done.1.refs_1_, ...), custom_call_target="tpu_custom_call" | custom-call | flops 2415919104 | bytes 8000000 | tf_op jit(solution)/shard_map/texts/pallas_call | solution.py:187
  74.2 3.6 %collective-permute-start.23 = (f16[448,1152]{1,0:T(8,128)(2,1)S(1)}, f16[448,1152]{1,0:T(8,128)(2,1)S(1)}, u32[]{:S(2)}, u32[]{:S(2)}) collective-permute-start(f16[448,1152]{1,0:T(8,128)(2,1)S(1)} %multiply_convert_fusion), channel_id=1, source_target_pairs={{0,8},{1,9},{2,10},{3,11},{4,12},{5,13},{6,14},{7,15},{8,0},{9,1},... | collective-permute-start | bytes 3096584 | tf_op jit(solution)/shard_map/ppermute | solution.py:31
  77.9 2.2 %collective-permute-done.15 = f32[8,128]{1,0:T(8,128)S(1)} collective-permute-done((f32[8,128]{1,0:T(8,128)S(1)}, f32[8,128]{1,0:T(8,128)S(1)}, u32[]{:S(2)}, u32[]{:S(2)}) %collective-permute-start.15) | collective-permute-done | bytes 4128 | tf_op jit(solution)/shard_map/ppermute | solution.py:31
  80.1 2.5 %collective-permute-start.16 = (f32[8,128]{1,0:T(8,128)S(1)}, f32[8,128]{1,0:T(8,128)S(1)}, u32[]{:S(2)}, u32[]{:S(2)}) collective-permute-start(f32[8,128]{1,0:T(8,128)S(1)} %add.62), channel_id=1, source_target_pairs={{0,16},{1,17},{2,18},{3,19},{4,20},{5,21},{6,22},{7,23},{8,24},{9,... | collective-permute-start | bytes 12296 | tf_op jit(solution)/shard_map/ppermute | solution.py:31
  84.4 3.3 %collective-permute-done.17 = f32[8,128]{1,0:T(8,128)S(1)} collective-permute-done((f32[8,128]{1,0:T(8,128)S(1)}, f32[8,128]{1,0:T(8,128)S(1)}, u32[]{:S(2)}, u32[]{:S(2)}) %collective-permute-start.17) | collective-permute-done | bytes 4128 | tf_op jit(solution)/shard_map/ppermute | solution.py:31
  87.7 4.5 %collective-permute-start.18 = (f32[8,128]{1,0:T(8,128)S(1)}, f32[8,128]{1,0:T(8,128)S(1)}, u32[]{:S(2)}, u32[]{:S(2)}) collective-permute-start(f32[8,128]{1,0:T(8,128)S(1)} %add.64), channel_id=1, source_target_pairs={{0,1},{1,0},{2,3},{3,2},{4,5},{5,4},{6,7},{7,6},{8,9},{9,8},{10,11... | collective-permute-start | bytes 12296 | tf_op jit(solution)/shard_map/ppermute | solution.py:31
  94.1 2.5 %collective-permute-done.19 = f32[8,128]{1,0:T(8,128)S(1)} collective-permute-done((f32[8,128]{1,0:T(8,128)S(1)}, f32[8,128]{1,0:T(8,128)S(1)}, u32[]{:S(2)}, u32[]{:S(2)}) %collective-permute-start.19) | collective-permute-done | bytes 4128 | tf_op jit(solution)/shard_map/ppermute | solution.py:31
  96.9 2.1 %collective-permute-done.20 = f32[8,128]{1,0:T(8,128)S(1)} collective-permute-done((f32[8,128]{1,0:T(8,128)S(1)}, f32[8,128]{1,0:T(8,128)S(1)}, u32[]{:S(2)}, u32[]{:S(2)}) %collective-permute-start.20) | collective-permute-done | bytes 4128 | tf_op jit(solution)/shard_map/ppermute | solution.py:31
  99.0 4.0 %collective-permute-done.21 = f32[8,128]{1,0:T(8,128)S(1)} collective-permute-done((f32[8,128]{1,0:T(8,128)S(1)}, f32[8,128]{1,0:T(8,128)S(1)}, u32[]{:S(2)}, u32[]{:S(2)}) %collective-permute-start.21) | collective-permute-done | bytes 4128 | tf_op jit(solution)/shard_map/ppermute | solution.py:31
  104.8 2.2 %collective-permute-done.22 = f32[8,128]{1,0:T(8,128)S(1)} collective-permute-done((f32[8,128]{1,0:T(8,128)S(1)}, f32[8,128]{1,0:T(8,128)S(1)}, u32[]{:S(2)}, u32[]{:S(2)}) %collective-permute-start.22) | collective-permute-done | bytes 4128 | tf_op jit(solution)/shard_map/ppermute | solution.py:31
  114.1 3.6 %collective-permute-start.24 = (f16[128,1152]{1,0:T(8,128)(2,1)S(1)}, f16[128,1152]{1,0:T(8,128)(2,1)S(1)}, u32[]{:S(2)}, u32[]{:S(2)}) collective-permute-start(f16[128,1152]{1,0:T(8,128)(2,1)S(1)} %get-tuple-element.31), channel_id=1, source_target_pairs={{0,49},{1,48},{2,51},{3,50},{4,53},{5,52},{6,55},{7,54},{8,24},{9,... | collective-permute-start | bytes 884744 | tf_op jit(solution)/shard_map/ppermute | solution.py:31
  117.7 2.2 %collective-permute-done.26 = f16[64,1152]{1,0:T(8,128)(2,1)S(1)} collective-permute-done((f16[64,1152]{1,0:T(8,128)(2,1)S(1)}, f16[64,1152]{1,0:T(8,128)(2,1)S(1)}, u32[]{:S(2)}, u32[]{:S(2)}) %collective-permute-start.26) | collective-permute-done | bytes 147488 | tf_op jit(solution)/shard_map/ppermute | solution.py:31
  119.9 3.3 %collective-permute-done.25 = f16[128,1152]{1,0:T(8,128)(2,1)S(1)} collective-permute-done((f16[128,1152]{1,0:T(8,128)(2,1)S(1)}, f16[128,1152]{1,0:T(8,128)(2,1)S(1)}, u32[]{:S(2)}, u32[]{:S(2)}) %collective-permute-start.25) | collective-permute-done | bytes 294944 | tf_op jit(solution)/shard_map/ppermute | solution.py:31
  126.5 6.6 %collective-permute-done.27 = f16[128,1152]{1,0:T(8,128)(2,1)S(1)} collective-permute-done((f16[128,1152]{1,0:T(8,128)(2,1)S(1)}, f16[128,1152]{1,0:T(8,128)(2,1)S(1)}, u32[]{:S(2)}, u32[]{:S(2)}) %collective-permute-start.27) | collective-permute-done | bytes 294944 | tf_op jit(solution)/shard_map/ppermute | solution.py:31
  133.2 8.5 %collective-permute-start.28 = (f32[64,1152]{1,0:T(8,128)S(1)}, f32[64,1152]{1,0:T(8,128)S(1)}, u32[]{:S(2)}, u32[]{:S(2)}) collective-permute-start(f32[64,1152]{1,0:T(8,128)S(1)} %slice.77), channel_id=1, source_target_pairs={{0,8},{1,9},{2,10},{3,11},{4,12},{5,13},{6,14},{7,15},{8,0},{9,1},... | collective-permute-start | bytes 884744 | tf_op jit(solution)/shard_map/ppermute | solution.py:31
  143.6 2.2 %project.1 = (f32[64,1152]{1,0:T(8,128)}, f32[64,1152]{1,0:T(8,128)}) custom-call(bf16[64,1152]{1,0:T(8,128)(2,1)} %images.3, bf16[64,1152]{1,0:T(8,128)(2,1)} %texts.5, f32[64,1152]{1,0:T(8,128)} %slice_add_fusion.2.img_dir, f32[64,1152]{1,0:T(8,128)} %slice_add_fusion.1.txt_dir), custom_call_target="tpu_custom_call" | custom-call | tf_op jit(solution)/shard_map/project/pallas_call | solution.py:213
  (100 shorter events, 43.7 us)
Async XLA Ops:
  2.5 28.8 %collective-permute-start.11 = (bf16[64,1152]{1,0:T(8,128)(2,1)}, bf16[64,1152]{1,0:T(8,128)(2,1)S(1)}, u32[]{:S(2)}, u32[]{:S(2)}) collective-permute-start(bf16[64,1152]{1,0:T(8,128)(2,1)} %get-tuple-element.18), channel_id=1, source_target_pairs={{0,4},{1,5},{2,6},{3,7},{4,0},{5,1},{6,2},{7,3},{8,136},{9,137},{1... | collective-permute-start | bytes 442376 | tf_op jit(solution)/shard_map/ppermute | solution.py:31
  6.2 21.2 %collective-permute-start.10 = (bf16[64,1152]{1,0:T(8,128)(2,1)}, bf16[64,1152]{1,0:T(8,128)(2,1)S(1)}, u32[]{:S(2)}, u32[]{:S(2)}) collective-permute-start(bf16[64,1152]{1,0:T(8,128)(2,1)} %get-tuple-element.18), channel_id=1, source_target_pairs={{0,6},{1,7},{2,0},{3,1},{4,2},{5,3},{6,4},{7,5},{8,200},{9,201},{1... | collective-permute-start | bytes 442376 | tf_op jit(solution)/shard_map/ppermute | solution.py:31
  7.0 11.1 %collective-permute-start.9 = (bf16[64,1152]{1,0:T(8,128)(2,1)}, bf16[64,1152]{1,0:T(8,128)(2,1)S(1)}, u32[]{:S(2)}, u32[]{:S(2)}) collective-permute-start(bf16[64,1152]{1,0:T(8,128)(2,1)} %get-tuple-element.18), channel_id=1, source_target_pairs={{0,2},{1,3},{2,4},{3,5},{4,6},{5,7},{6,0},{7,1},{8,72},{9,73},{10,... | collective-permute-start | bytes 442376 | tf_op jit(solution)/shard_map/ppermute | solution.py:31
  10.2 12.9 %collective-permute-start.2 = (bf16[128,1152]{1,0:T(8,128)(2,1)S(1)}, bf16[128,1152]{1,0:T(8,128)(2,1)S(1)}, u32[]{:S(2)}, u32[]{:S(2)}) collective-permute-start(bf16[128,1152]{1,0:T(8,128)(2,1)S(1)} %constant_dynamic-update-slice_fusion.refs_0_), channel_id=1, source_target_pairs={{0,32},{1,33},{2,34},{3,35},{4,36},{5,37},{6,38},{7,39},{8,41},{9,... | collective-permute-start | bytes 884744 | tf_op jit(solution)/shard_map/ppermute | solution.py:31
  17.3 18.6 %collective-permute-start.1 = (bf16[128,1152]{1,0:T(8,128)(2,1)S(1)}, bf16[128,1152]{1,0:T(8,128)(2,1)S(1)}, u32[]{:S(2)}, u32[]{:S(2)}) collective-permute-start(bf16[128,1152]{1,0:T(8,128)(2,1)S(1)} %constant_dynamic-update-slice_fusion.refs_0_), channel_id=1, source_target_pairs={{0,16},{1,17},{2,18},{3,19},{4,20},{5,21},{6,22},{7,23},{8,57},{9,... | collective-permute-start | bytes 884744 | tf_op jit(solution)/shard_map/ppermute | solution.py:31
  23.2 7.8 %collective-permute-start.4 = (bf16[64,1152]{1,0:T(8,128)(2,1)S(1)}, bf16[64,1152]{1,0:T(8,128)(2,1)S(1)}, u32[]{:S(2)}, u32[]{:S(2)}) collective-permute-start(bf16[64,1152]{1,0:T(8,128)(2,1)S(1)} %slice.71), channel_id=1, source_target_pairs={{0,32},{1,33},{2,34},{3,35},{4,36},{5,37},{6,38},{7,39},{8,41},{9,... | collective-permute-start | bytes 442376 | tf_op jit(solution)/shard_map/ppermute | solution.py:31
  31.3 15.7 %collective-permute-start.14 = (bf16[256,1152]{1,0:T(8,128)(2,1)S(1)}, bf16[256,1152]{1,0:T(8,128)(2,1)S(1)}, u32[]{:S(2)}, u32[]{:S(2)}) collective-permute-start(bf16[256,1152]{1,0:T(8,128)(2,1)S(1)} %constant_dynamic-update-slice_fusion.2.refs_9_), channel_id=1, source_target_pairs={{0,128},{1,129},{2,130},{3,131},{4,132},{5,133},{6,134},{7,135},{8... | collective-permute-start | bytes 1769480 | tf_op jit(solution)/shard_map/ppermute | solution.py:31
  32.9 15.0 %collective-permute-start.13 = (bf16[256,1152]{1,0:T(8,128)(2,1)S(1)}, bf16[256,1152]{1,0:T(8,128)(2,1)S(1)}, u32[]{:S(2)}, u32[]{:S(2)}) collective-permute-start(bf16[256,1152]{1,0:T(8,128)(2,1)S(1)} %constant_dynamic-update-slice_fusion.2.refs_9_), channel_id=1, source_target_pairs={{0,192},{1,193},{2,194},{3,195},{4,196},{5,197},{6,198},{7,199},{8... | collective-permute-start | bytes 1769480 | tf_op jit(solution)/shard_map/ppermute | solution.py:31
  35.8 12.4 %collective-permute-start.12 = (bf16[256,1152]{1,0:T(8,128)(2,1)S(1)}, bf16[256,1152]{1,0:T(8,128)(2,1)S(1)}, u32[]{:S(2)}, u32[]{:S(2)}) collective-permute-start(bf16[256,1152]{1,0:T(8,128)(2,1)S(1)} %constant_dynamic-update-slice_fusion.2.refs_9_), channel_id=1, source_target_pairs={{0,64},{1,65},{2,66},{3,67},{4,68},{5,69},{6,70},{7,71},{8,10},{9,... | collective-permute-start | bytes 1769480 | tf_op jit(solution)/shard_map/ppermute | solution.py:31
  36.8 7.0 %collective-permute-start.3 = (bf16[128,1152]{1,0:T(8,128)(2,1)S(1)}, bf16[128,1152]{1,0:T(8,128)(2,1)}, u32[]{:S(2)}, u32[]{:S(2)}) collective-permute-start(bf16[128,1152]{1,0:T(8,128)(2,1)S(1)} %collective-permute-done.2.refs_2_), channel_id=1, source_target_pairs={{0,16},{1,17},{2,18},{3,19},{4,20},{5,21},{6,22},{7,23},{8,57},{9,... | collective-permute-start | bytes 884744 | tf_op jit(solution)/shard_map/ppermute | solution.py:31
  39.2 7.7 %collective-permute-start.5 = (bf16[128,1152]{1,0:T(8,128)(2,1)S(1)}, bf16[128,1152]{1,0:T(8,128)(2,1)}, u32[]{:S(2)}, u32[]{:S(2)}) collective-permute-start(bf16[128,1152]{1,0:T(8,128)(2,1)S(1)} %collective-permute-done.1.refs_1_), channel_id=1, source_target_pairs={{0,8},{1,9},{2,10},{3,11},{4,12},{5,13},{6,14},{7,15},{8,0},{9,1},... | collective-permute-start | bytes 884744 | tf_op jit(solution)/shard_map/ppermute | solution.py:31
  69.8 39.6 %collective-permute-start.31 = (f16[256,1152]{1,0:T(8,128)(2,1)}, f16[256,1152]{1,0:T(8,128)(2,1)}, u32[]{:S(2)}, u32[]{:S(2)}) collective-permute-start(f16[256,1152]{1,0:T(8,128)(2,1)} %multiply_convert_fusion.1), channel_id=1, source_target_pairs={{0,128},{1,129},{2,130},{3,131},{4,132},{5,133},{6,134},{7,135},{8... | collective-permute-start | bytes 1769480 | tf_op jit(solution)/shard_map/ppermute | solution.py:31
  71.4 38.1 %collective-permute-start.30 = (f16[256,1152]{1,0:T(8,128)(2,1)}, f16[256,1152]{1,0:T(8,128)(2,1)}, u32[]{:S(2)}, u32[]{:S(2)}) collective-permute-start(f16[256,1152]{1,0:T(8,128)(2,1)} %multiply_convert_fusion.2), channel_id=1, source_target_pairs={{0,64},{1,65},{2,66},{3,67},{4,68},{5,69},{6,70},{7,71},{8,10},{9,... | collective-permute-start | bytes 1769480 | tf_op jit(solution)/shard_map/ppermute | solution.py:31
  72.5 37.0 %collective-permute-start.29 = (f16[256,1152]{1,0:T(8,128)(2,1)}, f16[256,1152]{1,0:T(8,128)(2,1)}, u32[]{:S(2)}, u32[]{:S(2)}) collective-permute-start(f16[256,1152]{1,0:T(8,128)(2,1)} %multiply_convert_fusion.3), channel_id=1, source_target_pairs={{0,192},{1,193},{2,194},{3,195},{4,196},{5,197},{6,198},{7,199},{8... | collective-permute-start | bytes 1769480 | tf_op jit(solution)/shard_map/ppermute | solution.py:31
  74.2 37.1 %collective-permute-start.23 = (f16[448,1152]{1,0:T(8,128)(2,1)S(1)}, f16[448,1152]{1,0:T(8,128)(2,1)S(1)}, u32[]{:S(2)}, u32[]{:S(2)}) collective-permute-start(f16[448,1152]{1,0:T(8,128)(2,1)S(1)} %multiply_convert_fusion), channel_id=1, source_target_pairs={{0,8},{1,9},{2,10},{3,11},{4,12},{5,13},{6,14},{7,15},{8,0},{9,1},... | collective-permute-start | bytes 3096584 | tf_op jit(solution)/shard_map/ppermute | solution.py:31
  87.7 6.4 %collective-permute-start.18 = (f32[8,128]{1,0:T(8,128)S(1)}, f32[8,128]{1,0:T(8,128)S(1)}, u32[]{:S(2)}, u32[]{:S(2)}) collective-permute-start(f32[8,128]{1,0:T(8,128)S(1)} %add.64), channel_id=1, source_target_pairs={{0,1},{1,0},{2,3},{3,2},{4,5},{5,4},{6,7},{7,6},{8,9},{9,8},{10,11... | collective-permute-start | bytes 12296 | tf_op jit(solution)/shard_map/ppermute | solution.py:31
  112.2 7.7 %collective-permute-start.26 = (f16[64,1152]{1,0:T(8,128)(2,1)S(1)}, f16[64,1152]{1,0:T(8,128)(2,1)S(1)}, u32[]{:S(2)}, u32[]{:S(2)}) collective-permute-start(f16[64,1152]{1,0:T(8,128)(2,1)S(1)} %slice.75), channel_id=1, source_target_pairs={{0,33},{1,32},{2,35},{3,34},{4,37},{5,36},{6,39},{7,38},{8,40},{9,... | collective-permute-start | bytes 442376 | tf_op jit(solution)/shard_map/ppermute | solution.py:31
  113.0 10.2 %collective-permute-start.25 = (f16[128,1152]{1,0:T(8,128)(2,1)S(1)}, f16[128,1152]{1,0:T(8,128)(2,1)S(1)}, u32[]{:S(2)}, u32[]{:S(2)}) collective-permute-start(f16[128,1152]{1,0:T(8,128)(2,1)S(1)} %get-tuple-element.32), channel_id=1, source_target_pairs={{0,49},{1,48},{2,51},{3,50},{4,53},{5,52},{6,55},{7,54},{8,24},{9,... | collective-permute-start | bytes 884744 | tf_op jit(solution)/shard_map/ppermute | solution.py:31
  114.1 12.4 %collective-permute-start.24 = (f16[128,1152]{1,0:T(8,128)(2,1)S(1)}, f16[128,1152]{1,0:T(8,128)(2,1)S(1)}, u32[]{:S(2)}, u32[]{:S(2)}) collective-permute-start(f16[128,1152]{1,0:T(8,128)(2,1)S(1)} %get-tuple-element.31), channel_id=1, source_target_pairs={{0,49},{1,48},{2,51},{3,50},{4,53},{5,52},{6,55},{7,54},{8,24},{9,... | collective-permute-start | bytes 884744 | tf_op jit(solution)/shard_map/ppermute | solution.py:31
  123.3 9.8 %collective-permute-start.27 = (f16[128,1152]{1,0:T(8,128)(2,1)S(1)}, f16[128,1152]{1,0:T(8,128)(2,1)S(1)}, u32[]{:S(2)}, u32[]{:S(2)}) collective-permute-start(f16[128,1152]{1,0:T(8,128)(2,1)S(1)} %fusion.2), channel_id=1, source_target_pairs={{0,33},{1,32},{2,35},{3,34},{4,37},{5,36},{6,39},{7,38},{8,40},{9,... | collective-permute-start | bytes 884744 | tf_op jit(solution)/shard_map/ppermute | solution.py:31
  123.6 18.1 %collective-permute-start.32 = (f16[64,1152]{1,0:T(8,128)(2,1)S(1)}, f16[64,1152]{1,0:T(8,128)(2,1)S(1)}, u32[]{:S(2)}, u32[]{:S(2)}) collective-permute-start(f16[64,1152]{1,0:T(8,128)(2,1)S(1)} %get-tuple-element.33), channel_id=1, source_target_pairs={{0,6},{1,7},{2,0},{3,1},{4,2},{5,3},{6,4},{7,5},{8,200},{9,201},{1... | collective-permute-start | bytes 442376 | tf_op jit(solution)/shard_map/ppermute | solution.py:31
  123.7 18.0 %collective-permute-start.34 = (f16[64,1152]{1,0:T(8,128)(2,1)S(1)}, f16[64,1152]{1,0:T(8,128)(2,1)S(1)}, u32[]{:S(2)}, u32[]{:S(2)}) collective-permute-start(f16[64,1152]{1,0:T(8,128)(2,1)S(1)} %get-tuple-element.34), channel_id=1, source_target_pairs={{0,4},{1,5},{2,6},{3,7},{4,0},{5,1},{6,2},{7,3},{8,136},{9,137},{1... | collective-permute-start | bytes 442376 | tf_op jit(solution)/shard_map/ppermute | solution.py:31
  125.3 16.4 %collective-permute-start.33 = (f16[64,1152]{1,0:T(8,128)(2,1)S(1)}, f16[64,1152]{1,0:T(8,128)(2,1)S(1)}, u32[]{:S(2)}, u32[]{:S(2)}) collective-permute-start(f16[64,1152]{1,0:T(8,128)(2,1)S(1)} %get-tuple-element.35), channel_id=1, source_target_pairs={{0,2},{1,3},{2,4},{3,5},{4,6},{5,7},{6,0},{7,1},{8,72},{9,73},{10,... | collective-permute-start | bytes 442376 | tf_op jit(solution)/shard_map/ppermute | solution.py:31
  133.2 9.7 %collective-permute-start.28 = (f32[64,1152]{1,0:T(8,128)S(1)}, f32[64,1152]{1,0:T(8,128)S(1)}, u32[]{:S(2)}, u32[]{:S(2)}) collective-permute-start(f32[64,1152]{1,0:T(8,128)S(1)} %slice.77), channel_id=1, source_target_pairs={{0,8},{1,9},{2,10},{3,11},{4,12},{5,13},{6,14},{7,15},{8,0},{9,1},... | collective-permute-start | bytes 884744 | tf_op jit(solution)/shard_map/ppermute | solution.py:31
  (20 other events, 88.2 us)

commit v2 on v1

--- a/solution.py
+++ b/solution.py
@@ -11,6 +11,7 @@
 LOG2E = 1.4426950408889634
 LN2 = 0.6931471805599453
 F32, BF16, F16 = jnp.float32, jnp.bfloat16, jnp.float16
+SHRINK = 2.0**-20
 DOWN, UP = 0.125, 8.0
 
 AXES = ("y", "zl", "c", "x", "zh")
@@ -47,6 +48,28 @@
     return permute(lambda y, z, c, x: (y, z, 1 - c, x), v)
 
 
+def flip_z(bit, v):
+    return permute(lambda y, z, c, x: (y, z ^ bit, c, x), v)
+
+
+def flip_second(bit, v):
+    return permute(lambda y, z, c, x: (y ^ bit, z, c, x) if c == 0 else (y, z, c, x ^ bit), v)
+
+
+def split(sums):
+    value = sums * SHRINK
+    terms = []
+    for _ in range(3):
+        term = lax.reduce_precision(value, 5, 10)
+        terms.append(term.astype(F16))
+        value = (value - term) * 2048.0
+    return jnp.pad(jnp.concatenate(terms, axis=1), ((0, 0), (0, 768)))
+
+
+def join(codes):
+    return (codes[:, :128] + codes[:, 128:256] / 2048.0 + codes[:, 256:384] / 2048.0**2) / SHRINK
+
+
 def low(sums):
     return (sums * DOWN).astype(F16)
 
@@ -70,25 +93,26 @@
     return value
 
 
+def lay(pieces, dst):
+    at = 0
+    for piece in pieces:
+        dst[at : at + piece.shape[0], :] = piece[...]
+        at += piece.shape[0]
+
+
 def pair_kernel(sc, *refs):
     imgs, txts = refs[:9], refs[9:13]
-    w_ref, keep, send, sums, x_ref, y_ref = refs[13:]
-    at = 0
-    for r in imgs:
-        x_ref[at : at + r.shape[0], :] = r[...]
-        at += r.shape[0]
-    at = 0
-    for r in txts:
-        y_ref[at : at + r.shape[0], :] = r[...]
-        at += r.shape[0]
+    w_ref, x_ref, y_ref, sums = refs[13:]
+    lay(imgs, x_ref)
+    lay(txts, y_ref)
     scale = sc[0]
     bias = sc[1]
     lift = jnp.zeros((8, 256), F32)
     logs = jnp.zeros((8, 256), F32)
     slope_acc = jnp.zeros((8, 256), F32)
     curve_acc = jnp.zeros((8, 256), F32)
-    for i in range(4):
-        for j in range(4):
+    for j in range(4):
+        for i in range(4):
             dots = lax.dot_general(
                 x_ref[i * 256 : i * 256 + 256, :],
                 y_ref[j * 256 : j * 256 + 256, :],
@@ -117,28 +141,20 @@
     sums[...] = jnp.where(
         row == 0, loss, jnp.where(row == 1, jnp.sum(slope_acc), jnp.where(row == 2, jnp.sum(curve_acc), 0.0))
     )
+
+
+def image_kernel(w_ref, y_ref, keep, send):
     for lo, hi in ((576, 800), (800, 1024)):
-        part = jnp.dot(w_ref[lo:hi, :], y_ref[...], preferred_element_type=F32)
-        send[lo - 576 : hi - 576, :] = part
-    for lo, hi in ((0, 192), (192, 384), (384, 576)):
+        send[lo - 576 : hi - 576, :] = jnp.dot(w_ref[lo:hi, :], y_ref[...], preferred_element_type=F32)
+    for lo, hi in ((0, 288), (288, 576)):
         keep[lo:hi, :] = jnp.dot(w_ref[lo:hi, :], y_ref[...], preferred_element_type=F32)
 
 
-def text_kernel(w_ref, *refs):
-    imgs = refs[:9]
-    own, back, fore, over, x_ref = refs[9:]
-    at = 0
-    for r in imgs:
-        x_ref[at : at + r.shape[0], :] = r[...]
-        at += r.shape[0]
+def text_kernel(w_ref, x_ref, own, back, fore, over):
     for j, out in ((1, back), (2, fore), (3, over), (0, own)):
-        part = lax.dot_general(
-            w_ref[:, j * 256 : j * 256 + 256],
-            x_ref[...],
-            (((0,), (0,)), ((), ())),
-            preferred_element_type=F32,
+        out[...] = lax.dot_general(
+            w_ref[:, j * 256 : j * 256 + 256], x_ref[...], (((0,), (0,)), ((), ())), preferred_element_type=F32
         )
-        out[...] = part
 
 
 def project_kernel(images, texts, img_dir, txt_dir, grad_images, grad_texts):
@@ -165,61 +181,80 @@
     r2 = along_z(2, pair)
     a, b, c = first(1, txt_low), first(-1, txt_low), first(2, txt_low)
     block = jnp.concatenate([txt_low, a, b, c], axis=0)
+    block, pair = lax.optimization_barrier((block, pair))
+    ta, tb, tc = second(1, block), second(-1, block), second(2, block)
+    q1, q2 = sibling(r1), sibling(r2)
+    r2, q1, q2 = lax.optimization_barrier((r2, q1, q2))
     r3 = along_z(1, r2)
     r4 = along_z(2, r2[:64])
-    ta, tb, tc = second(1, block), second(-1, block), second(2, block)
-    imgs = (pair, r1, r2, r3, r4, sibling(r1), sibling(r2), sibling(r3), sibling(r4))
+    imgs = (pair, r1, r2, r3, r4, q1, q2, sibling(r3), sibling(r4))
     txts = (block, ta, tb, tc)
 
     vmem = pl.BlockSpec(memory_space=pltpu.VMEM)
-    w, keep, send, sums = pl.pallas_call(
+    limit = pltpu.CompilerParams(vmem_limit_bytes=16 * 1024 * 1024)
+    cost = pl.CostEstimate(flops=2 * 1024 * 1024 * 1152, bytes_accessed=7_000_000, transcendentals=2 * 1024 * 1024)
+    w, x, y, sums = pl.pallas_call(
         pair_kernel,
         in_specs=[pl.BlockSpec(memory_space=pltpu.SMEM)] + [vmem] * 13,
         out_specs=[vmem] * 4,
-        out_shape=(arr((1024, 1024), BF16), arr((576, d), F32), arr((448, d), F32), arr((8, 128), F32)),
-        scratch_shapes=[pltpu.VMEM((1024, d), BF16), pltpu.VMEM((1024, d), BF16)],
-        compiler_params=pltpu.CompilerParams(vmem_limit_bytes=48 * 1024 * 1024),
-        cost_estimate=pl.CostEstimate(flops=4 * 1024 * 1024 * 1152, bytes_accessed=12_000_000, transcendentals=2 * 1024 * 1024),
+        out_shape=(arr((1024, 1024), BF16), arr((1024, d), BF16), arr((1024, d), BF16), arr((8, 128), F32)),
+        compiler_params=limit,
+        cost_estimate=cost,
         name="pairs",
     )(scalars, *imgs, *txts)
-    got = sibling(low(send))
+    sums = sums + sibling(sums)
+    w, sums = lax.optimization_barrier((w, sums))
+
+    keep, send = pl.pallas_call(
+        image_kernel,
+        in_specs=[vmem] * 2,
+        out_specs=[vmem] * 2,
+        out_shape=(arr((576, d), F32), arr((448, d), F32)),
+        compiler_params=limit,
+        cost_estimate=cost,
+        name="images",
+    )(w, y)
+    sums = sums + flip_z(1, sums)
+    got = sibling(send)
+    w, sums, keep = lax.optimization_barrier((w, sums, keep))
 
     t_own, t_back, t_fore, t_over = pl.pallas_call(
         text_kernel,
-        in_specs=[vmem] * 10,
+        in_specs=[vmem] * 2,
         out_specs=[vmem] * 4,
         out_shape=(arr((256, d), F32),) * 4,
-        scratch_shapes=[pltpu.VMEM((1024, d), BF16)],
-        compiler_params=pltpu.CompilerParams(vmem_limit_bytes=48 * 1024 * 1024),
-        cost_estimate=pl.CostEstimate(flops=2 * 1024 * 1024 * 1152, bytes_accessed=8_000_000, transcendentals=0),
+        compiler_params=limit,
+        cost_estimate=cost,
         name="texts",
-    )(w, *imgs)
-
-    chain = keep[128:] * DOWN + got.astype(F32)
-    g3 = along_z(-1, chain[256:384].astype(F16))
-    g4 = along_z(-2, chain[384:448].astype(F16))
-    c2 = chain[128:256] + g3.astype(F32) + jnp.pad(g4.astype(F32), ((0, 64), (0, 0)))
-    g1 = along_z(-1, chain[0:128].astype(F16))
-    g2 = along_z(-2, c2.astype(F16))
+    )(w, x)
+    sums = sums + flip_z(2, sums) + flip_z(4, sums) + flip_z(6, sums)
+
+    chain = keep[128:] + got
+    g3 = along_z(-1, low(chain[256:384]))
+    g4 = along_z(-2, low(chain[384:448]))
+
+    codes = split(sums)
+    out = [jnp.concatenate([low(v), codes], axis=0) for v in (t_back, t_fore, t_over)]
+    back = [second(k, v).astype(F32) for k, v in zip((-1, 1, 2), out)]
+    c2 = chain[128:256] + (g3.astype(F32) + jnp.pad(g4.astype(F32), ((0, 64), (0, 0)))) * UP
+    c2, back[0], back[1], back[2] = lax.optimization_barrier((c2, *back))
+    t_sum = t_own + (back[0][:256] + back[1][:256] + back[2][:256]) * UP
+    sums = sums + sum(join(v[256:]) for v in back)
+    codes = split(sums)
+    out = [jnp.concatenate([low(t_sum[k * 64 : k * 64 + 64]), codes], axis=0) for k in (1, 2, 3)]
+    back = [first(k, v).astype(F32) for k, v in zip((-1, 1, 2), out)]
+    txt_dir = t_sum[:64] + (back[0][:64] + back[1][:64] + back[2][:64]) * UP
+    sums = sums + sum(join(v[64:]) for v in back)
+
+    g1 = along_z(-1, low(chain[0:128]))
+    g2 = along_z(-2, low(c2))
     mine = keep[:128] + (g1.astype(F32) + g2.astype(F32)) * UP
     img_dir = mine[:64] + sibling(mine[64:])
-
-    s1, s2, s3 = second(-1, low(t_back)), second(1, low(t_fore)), second(2, low(t_over))
-    t_sum = t_own + (s1.astype(F32) + s2.astype(F32) + s3.astype(F32)) * UP
-    t_low = low(t_sum[64:])
-    f1, f2, f3 = first(-1, t_low[0:64]), first(1, t_low[64:128]), first(2, t_low[128:192])
-    txt_dir = t_sum[:64] + (f1.astype(F32) + f2.astype(F32) + f3.astype(F32)) * UP
 
     grad_images, grad_texts = pl.pallas_call(
         project_kernel, out_shape=(arr((rows, d), F32), arr((rows, d), F32)), name="project"
     )(images, texts, img_dir, txt_dir)
 
-    sums = sums + sibling(sums)
-    for bit in (1, 2, 4):
-        sums = sums + permute(lambda y, z, c, x: (y, z ^ bit, c, x), sums)
-    for bit in (1, 2):
-        sums = sums + permute(lambda y, z, c, x: (y ^ bit, z, c, x), sums)
-        sums = sums + permute(lambda y, z, c, x: (y, z, c, x ^ bit), sums)
     total = float(rows * 256)
     count = total * total
     return (sums[0, 0] / count, grad_images, grad_texts, scale * sums[2, 0] / count, sums[1, 0] / count)

time: 151 us -> 117 us (0.77)
  waiting for transfers between devices: 46.8 us -> 27.1 us
  starting transfers between devices: 61.2 us -> 53.6 us
  Pallas kernels: 20.5 us -> 16.3 us
  local copies, waits for them, and re-layouts: 6.17 us -> 3.25 us
    ppermute x35 -> x32, waiting for transfers between devices: 46.8 us -> 27.1 us  [permute(): return lax.ppermute(value, AXES, pairs)]
    ppermute x35 -> x32, starting transfers between devices: 61.2 us -> 53.6 us  [permute(): return lax.ppermute(value, AXES, pairs)]
    pallas_call x1, Pallas kernels: 11.2 us -> 6.38 us  [shards(): pl.pallas_call(pair_kernel, in_specs=[pl.BlockSpec(memory_space=pltpu.SME...]
    unnamed x22 -> x11, local copies, waits for them, and re-layouts: 5.37 us -> 2.65 us
    concatenate x0 -> x5, other arithmetic: none -> 1.52 us  [the longest x1 0.96 us: shards(): block = jnp.concatenate([txt_low, a, b, c], axis=0)]
    convert_element_type x5 -> x6, other arithmetic: 3.08 us -> 2 us  [low(): return (sums * DOWN).astype(F16)]
    pallas_call x1 -> x2, Pallas kernels: 5.22 us -> 5.83 us  [the longest x1 2.92 us: shards(): pl.pallas_call(image_kernel, in_specs=[vmem] * 2, out_specs=[vmem] * 2, o...]
  transfers between devices with their start and end apart: 35 -> 32, of which waited for: 19 -> 11; matrix products, arithmetic and copies ran while one was open for 4% -> 7% of each run, Pallas kernels for 0% -> 5%
where the time goes in v2:
time: 117 us; the launch traced here: 116 us
  starting transfers between devices  53.6 us (46%)
  waiting for transfers between devices  27.1 us (23%)
  Pallas kernels  16.3 us (14%)
  other arithmetic  8.44 us (7%)
  between operations  7.57 us (6%)
  local copies, waits for them, and re-layouts  3.25 us (3%)
    ppermute x32, starting transfers between devices, permute(): return lax.ppermute(value, AXES, pairs)  53.6 us
    ppermute x32, waiting for transfers between devices, permute(): return lax.ppermute(value, AXES, pairs)  27.1 us
    pallas_call x1, Pallas kernels, shards(): pl.pallas_call(pair_kernel, in_specs=[pl.BlockSpec(memory_space=pltpu.SME...  6.38 us
    pallas_call x1, Pallas kernels, shards(): pl.pallas_call(image_kernel, in_specs=[vmem] * 2, out_specs=[vmem] * 2, o...  2.92 us
    pallas_call x1, Pallas kernels, shards(): pl.pallas_call(text_kernel, in_specs=[vmem] * 2, out_specs=[vmem] * 4, ou...  2.91 us
    unnamed x11, local copies, waits for them, and re-layouts  2.65 us
  transfers between devices with their start and end apart: 32, of which 11 were waited for; matrix products, arithmetic and copies ran while one was open for 7% of the time, Pallas kernels for 5%

profile of v2, /device:TPU:1, one launch (start us, length us, event | category | flops | bytes accessed | tf_op | source)
XLA Modules:
  0.0 116.2 jit_solution(4767133805466186264)
XLA Ops:
  0.6 1.8 %normalise.1 = (bf16[64,1152]{1,0:T(8,128)(2,1)}, bf16[64,1152]{1,0:T(8,128)(2,1)}) custom-call(bf16[64,1152]{1,0:T(8,128)(2,1)} %images.5, bf16[64,1152]{1,0:T(8,128)(2,1)} %texts.5), custom_call_target="tpu_custom_call" | custom-call | tf_op jit(solution)/shard_map/normalise/pallas_call | solution.py:173
  2.5 3.2 %collective-permute-start.3 = (bf16[64,1152]{1,0:T(8,128)(2,1)}, bf16[64,1152]{1,0:T(8,128)(2,1)S(1)}, u32[]{:S(2)}, u32[]{:S(2)}) collective-permute-start(bf16[64,1152]{1,0:T(8,128)(2,1)} %get-tuple-element.34), channel_id=1, source_target_pairs={{0,8},{1,9},{2,10},{3,11},{4,12},{5,13},{6,14},{7,15},{8,0},{9,1},... | collective-permute-start | bytes 442376 | tf_op jit(solution)/shard_map/ppermute | solution.py:32
  6.9 3.9 %collective-permute-start.4 = (bf16[128,1152]{1,0:T(8,128)(2,1)S(1)}, bf16[128,1152]{1,0:T(8,128)(2,1)S(1)}, u32[]{:S(2)}, u32[]{:S(2)}) collective-permute-start(bf16[128,1152]{1,0:T(8,128)(2,1)S(1)} %constant_dynamic-update-slice_fusion.refs_0_), channel_id=1, source_target_pairs={{0,16},{1,17},{2,18},{3,19},{4,20},{5,21},{6,22},{7,23},{8,57},{9,... | collective-permute-start | bytes 884744 | tf_op jit(solution)/shard_map/ppermute | solution.py:32
  12.0 2.9 %collective-permute-start.2 = (bf16[64,1152]{1,0:T(8,128)(2,1)}, bf16[64,1152]{1,0:T(8,128)(2,1)S(1)}, u32[]{:S(2)}, u32[]{:S(2)}) collective-permute-start(bf16[64,1152]{1,0:T(8,128)(2,1)} %get-tuple-element.33), channel_id=1, source_target_pairs={{0,4},{1,5},{2,6},{3,7},{4,0},{5,1},{6,2},{7,3},{8,136},{9,137},{1... | collective-permute-start | bytes 442376 | tf_op jit(solution)/shard_map/ppermute | solution.py:32
  17.3 3.6 %collective-permute-done.5.refs_2_ = bf16[128,1152]{1,0:T(8,128)(2,1)S(1)} collective-permute-done((bf16[128,1152]{1,0:T(8,128)(2,1)S(1)}, bf16[128,1152]{1,0:T(8,128)(2,1)S(1)}, u32[]{:S(2)}, u32[]{:S(2)}) %collective-permute-start.5) | collective-permute-done | bytes 294944 | tf_op jit(solution)/shard_map/ppermute | solution.py:32
  26.6 3.4 %collective-permute-start.8 = (bf16[128,1152]{1,0:T(8,128)(2,1)S(1)}, bf16[128,1152]{1,0:T(8,128)(2,1)}, u32[]{:S(2)}, u32[]{:S(2)}) collective-permute-start(bf16[128,1152]{1,0:T(8,128)(2,1)S(1)} %collective-permute-done.5.refs_2_), channel_id=1, source_target_pairs={{0,16},{1,17},{2,18},{3,19},{4,20},{5,21},{6,22},{7,23},{8,57},{9,... | collective-permute-start | bytes 884744 | tf_op jit(solution)/shard_map/ppermute | solution.py:32
  30.1 2.5 %collective-permute-start.9 = (bf16[64,1152]{1,0:T(8,128)(2,1)S(1)}, bf16[64,1152]{1,0:T(8,128)(2,1)}, u32[]{:S(2)}, u32[]{:S(2)}) collective-permute-start(bf16[64,1152]{1,0:T(8,128)(2,1)S(1)} %slice.144), channel_id=1, source_target_pairs={{0,32},{1,33},{2,34},{3,35},{4,36},{5,37},{6,38},{7,39},{8,41},{9,... | collective-permute-start | bytes 442376 | tf_op jit(solution)/shard_map/ppermute | solution.py:32
  32.5 2.8 %collective-permute-done.8.refs_3_ = bf16[128,1152]{1,0:T(8,128)(2,1)} collective-permute-done((bf16[128,1152]{1,0:T(8,128)(2,1)S(1)}, bf16[128,1152]{1,0:T(8,128)(2,1)}, u32[]{:S(2)}, u32[]{:S(2)}) %collective-permute-start.8) | collective-permute-done | bytes 294944 | tf_op jit(solution)/shard_map/ppermute | solution.py:32
  36.2 1.7 %collective-permute-done.9.refs_4_ = bf16[64,1152]{1,0:T(8,128)(2,1)} collective-permute-done((bf16[64,1152]{1,0:T(8,128)(2,1)S(1)}, bf16[64,1152]{1,0:T(8,128)(2,1)}, u32[]{:S(2)}, u32[]{:S(2)}) %collective-permute-start.9) | collective-permute-done | bytes 147488 | tf_op jit(solution)/shard_map/ppermute | solution.py:32
  37.9 2.9 %collective-permute-start.11 = (bf16[64,1152]{1,0:T(8,128)(2,1)}, bf16[64,1152]{1,0:T(8,128)(2,1)}, u32[]{:S(2)}, u32[]{:S(2)}) collective-permute-start(bf16[64,1152]{1,0:T(8,128)(2,1)} %collective-permute-done.9.refs_4_), channel_id=1, source_target_pairs={{0,8},{1,9},{2,10},{3,11},{4,12},{5,13},{6,14},{7,15},{8,0},{9,1},... | collective-permute-start | bytes 442376 | tf_op jit(solution)/shard_map/ppermute | solution.py:32
  43.2 6.4 %pairs.1 = (bf16[1024,1024]{1,0:T(8,128)(2,1)S(1)}, bf16[1024,1152]{1,0:T(8,128)(2,1)S(1)}, bf16[1024,1152]{1,0:T(8,128)(2,1)S(1)}, f32[8,128]{1,0:T(8,128)S(1)}) custom-call(f32[2]{0:T(128)S(1)} %pad_maximum_fusion.7.sc, bf16[128,1152]{1,0:T(8,128)(2,1)S(1)} %constant_dynamic-update-slice_fusion.refs_0_, ...), custom_call_target="tpu_custom_call" | custom-call | flops 2415919104 | bytes 7000000 | tf_op jit(solution)/shard_map/pairs/pallas_call | solution.py:196
  52.4 2.9 %images.4 = (f32[576,1152]{1,0:T(8,128)S(1)}, f32[448,1152]{1,0:T(8,128)S(1)}) custom-call(bf16[1024,1024]{1,0:T(8,128)(2,1)S(1)} %get-tuple-element.49.w_ref, bf16[1024,1152]{1,0:T(8,128)(2,1)S(1)} %get-tuple-element.44.y_ref), custom_call_target="tpu_custom_call" | custom-call | flops 2415919104 | bytes 7000000 | tf_op jit(solution)/shard_map/images/pallas_call | solution.py:208
  57.6 2.9 %collective-permute-start.18 = (f32[8,128]{1,0:T(8,128)S(1)}, f32[8,128]{1,0:T(8,128)S(1)}, u32[]{:S(2)}, u32[]{:S(2)}) collective-permute-start(f32[8,128]{1,0:T(8,128)S(1)} %add.116), channel_id=1, source_target_pairs={{0,1},{1,0},{2,3},{3,2},{4,5},{5,4},{6,7},{7,6},{8,9},{9,8},{10,11... | collective-permute-start | bytes 12296 | tf_op jit(solution)/shard_map/ppermute | solution.py:32
  61.7 2.9 %texts.4 = (f32[256,1152]{1,0:T(8,128)S(1)}, f32[256,1152]{1,0:T(8,128)S(1)}, f32[256,1152]{1,0:T(8,128)S(1)}, f32[256,1152]{1,0:T(8,128)S(1)}) custom-call(bf16[1024,1024]{1,0:T(8,128)(2,1)S(1)} %get-tuple-element.49.w_ref, bf16[1024,1152]{1,0:T(8,128)(2,1)S(1)} %get-tuple-element.50.x_ref), custom_call_target="tpu_custom_call" | custom-call | flops 2415919104 | bytes 7000000 | tf_op jit(solution)/shard_map/texts/pallas_call | solution.py:221
  65.5 1.9 %collective-permute-start.23 = (f16[264,1152]{1,0:T(8,128)(2,1)S(1)}, f16[264,1152]{1,0:T(8,128)(2,1)S(1)}, u32[]{:S(2)}, u32[]{:S(2)}) collective-permute-start(f16[264,1152]{1,0:T(8,128)(2,1)S(1)} %get-tuple-element.75), channel_id=1, source_target_pairs={{0,192},{1,193},{2,194},{3,195},{4,196},{5,197},{6,198},{7,199},{8... | collective-permute-start | bytes 1824776 | tf_op jit(solution)/shard_map/ppermute | solution.py:32
  67.3 1.8 %collective-permute-start.25 = (f16[264,1152]{1,0:T(8,128)(2,1)S(1)}, f16[264,1152]{1,0:T(8,128)(2,1)S(1)}, u32[]{:S(2)}, u32[]{:S(2)}) collective-permute-start(f16[264,1152]{1,0:T(8,128)(2,1)S(1)} %get-tuple-element.73), channel_id=1, source_target_pairs={{0,128},{1,129},{2,130},{3,131},{4,132},{5,133},{6,134},{7,135},{8... | collective-permute-start | bytes 1824776 | tf_op jit(solution)/shard_map/ppermute | solution.py:32
  72.2 8.7 %collective-permute-done.23 = f16[264,1152]{1,0:T(8,128)(2,1)S(1)} collective-permute-done((f16[264,1152]{1,0:T(8,128)(2,1)S(1)}, f16[264,1152]{1,0:T(8,128)(2,1)S(1)}, u32[]{:S(2)}, u32[]{:S(2)}) %collective-permute-start.23) | collective-permute-done | bytes 608288 | tf_op jit(solution)/shard_map/ppermute | solution.py:32
  81.0 3.3 %collective-permute-done.24 = f16[264,1152]{1,0:T(8,128)(2,1)S(1)} collective-permute-done((f16[264,1152]{1,0:T(8,128)(2,1)S(1)}, f16[264,1152]{1,0:T(8,128)(2,1)S(1)}, u32[]{:S(2)}, u32[]{:S(2)}) %collective-permute-start.24) | collective-permute-done | bytes 608288 | tf_op jit(solution)/shard_map/ppermute | solution.py:32
  88.1 1.7 %collective-permute-start.26 = (f16[72,1152]{1,0:T(8,128)(2,1)S(1)}, f16[72,1152]{1,0:T(8,128)(2,1)S(1)}, u32[]{:S(2)}, u32[]{:S(2)}) collective-permute-start(f16[72,1152]{1,0:T(8,128)(2,1)S(1)} %get-tuple-element.70), channel_id=1, source_target_pairs={{0,6},{1,7},{2,0},{3,1},{4,2},{5,3},{6,4},{7,5},{8,200},{9,201},{1... | collective-permute-start | bytes 497672 | tf_op jit(solution)/shard_map/ppermute | solution.py:32
  91.9 1.6 %collective-permute-done.27 = f16[72,1152]{1,0:T(8,128)(2,1)S(1)} collective-permute-done((f16[72,1152]{1,0:T(8,128)(2,1)S(1)}, f16[72,1152]{1,0:T(8,128)(2,1)S(1)}, u32[]{:S(2)}, u32[]{:S(2)}) %collective-permute-start.27) | collective-permute-done | bytes 165920 | tf_op jit(solution)/shard_map/ppermute | solution.py:32
  96.9 3.1 %collective-permute-done.30 = f16[128,1152]{1,0:T(8,128)(2,1)} collective-permute-done((f16[128,1152]{1,0:T(8,128)(2,1)}, f16[128,1152]{1,0:T(8,128)(2,1)}, u32[]{:S(2)}, u32[]{:S(2)}) %collective-permute-start.30) | collective-permute-done | bytes 294944 | tf_op jit(solution)/shard_map/ppermute | solution.py:32
  101.2 6.9 %collective-permute-start.31 = (f32[64,1152]{1,0:T(8,128)S(1)}, f32[64,1152]{1,0:T(8,128)S(1)}, u32[]{:S(2)}, u32[]{:S(2)}) collective-permute-start(f32[64,1152]{1,0:T(8,128)S(1)} %slice.201), channel_id=1, source_target_pairs={{0,8},{1,9},{2,10},{3,11},{4,12},{5,13},{6,14},{7,15},{8,0},{9,1},... | collective-permute-start | bytes 884744 | tf_op jit(solution)/shard_map/ppermute | solution.py:32
  108.0 1.8 %fusion.3.txt_dir = f32[64,1152]{1,0:T(8,128)} fusion(f32[72,1152]{1,0:T(8,128)S(1)} %convert_element_type.101, f32[72,1152]{1,0:T(8,128)S(1)} %convert_element_type.99, f32[72,1152]{1,0:T(8,128)S(1)} %copy-done.4, f32[256,1152]{1,0:T(8,128)} %copy-done.2), kind=kLoop, calls=%fused_computation.18 | loop fusion | flops 294912 | bytes 1474560 | tf_op jit(solution)/shard_map/add | solution.py:246
  110.5 2.2 %project.1 = (f32[64,1152]{1,0:T(8,128)}, f32[64,1152]{1,0:T(8,128)}) custom-call(bf16[64,1152]{1,0:T(8,128)(2,1)} %images.5, bf16[64,1152]{1,0:T(8,128)(2,1)} %texts.5, f32[64,1152]{1,0:T(8,128)} %slice_add_fusion.4.img_dir, f32[64,1152]{1,0:T(8,128)} %fusion.3.txt_dir), custom_call_target="tpu_custom_call" | custom-call | tf_op jit(solution)/shard_map/project/pallas_call | solution.py:254
  (91 shorter events, 31.8 us)
Async XLA Ops:
  6.9 10.3 %collective-permute-start.4 = (bf16[128,1152]{1,0:T(8,128)(2,1)S(1)}, bf16[128,1152]{1,0:T(8,128)(2,1)S(1)}, u32[]{:S(2)}, u32[]{:S(2)}) collective-permute-start(bf16[128,1152]{1,0:T(8,128)(2,1)S(1)} %constant_dynamic-update-slice_fusion.refs_0_), channel_id=1, source_target_pairs={{0,16},{1,17},{2,18},{3,19},{4,20},{5,21},{6,22},{7,23},{8,57},{9,... | collective-permute-start | bytes 884744 | tf_op jit(solution)/shard_map/ppermute | solution.py:32
  10.8 10.0 %collective-permute-start.5 = (bf16[128,1152]{1,0:T(8,128)(2,1)S(1)}, bf16[128,1152]{1,0:T(8,128)(2,1)S(1)}, u32[]{:S(2)}, u32[]{:S(2)}) collective-permute-start(bf16[128,1152]{1,0:T(8,128)(2,1)S(1)} %constant_dynamic-update-slice_fusion.refs_0_), channel_id=1, source_target_pairs={{0,32},{1,33},{2,34},{3,35},{4,36},{5,37},{6,38},{7,39},{8,41},{9,... | collective-permute-start | bytes 884744 | tf_op jit(solution)/shard_map/ppermute | solution.py:32
  12.0 9.3 %collective-permute-start.2 = (bf16[64,1152]{1,0:T(8,128)(2,1)}, bf16[64,1152]{1,0:T(8,128)(2,1)S(1)}, u32[]{:S(2)}, u32[]{:S(2)}) collective-permute-start(bf16[64,1152]{1,0:T(8,128)(2,1)} %get-tuple-element.33), channel_id=1, source_target_pairs={{0,4},{1,5},{2,6},{3,7},{4,0},{5,1},{6,2},{7,3},{8,136},{9,137},{1... | collective-permute-start | bytes 442376 | tf_op jit(solution)/shard_map/ppermute | solution.py:32
  14.9 6.4 %collective-permute-start.1 = (bf16[64,1152]{1,0:T(8,128)(2,1)}, bf16[64,1152]{1,0:T(8,128)(2,1)S(1)}, u32[]{:S(2)}, u32[]{:S(2)}) collective-permute-start(bf16[64,1152]{1,0:T(8,128)(2,1)} %get-tuple-element.33), channel_id=1, source_target_pairs={{0,6},{1,7},{2,0},{3,1},{4,2},{5,3},{6,4},{7,5},{8,200},{9,201},{1... | collective-permute-start | bytes 442376 | tf_op jit(solution)/shard_map/ppermute | solution.py:32
  17.3 9.4 %collective-permute-start.6 = (bf16[128,1152]{1,0:T(8,128)(2,1)S(1)}, bf16[128,1152]{1,0:T(8,128)(2,1)S(1)}, u32[]{:S(2)}, u32[]{:S(2)}) collective-permute-start(bf16[128,1152]{1,0:T(8,128)(2,1)S(1)} %collective-permute-done.4.refs_1_), channel_id=1, source_target_pairs={{0,8},{1,9},{2,10},{3,11},{4,12},{5,13},{6,14},{7,15},{8,0},{9,1},... | collective-permute-start | bytes 884744 | tf_op jit(solution)/shard_map/ppermute | solution.py:32
  22.3 19.9 %collective-permute-start.12 = (bf16[256,1152]{1,0:T(8,128)(2,1)S(1)}, bf16[256,1152]{1,0:T(8,128)(2,1)S(1)}, u32[]{:S(2)}, u32[]{:S(2)}) collective-permute-start(bf16[256,1152]{1,0:T(8,128)(2,1)S(1)} %pad_maximum_fusion.3.refs_9_), channel_id=1, source_target_pairs={{0,64},{1,65},{2,66},{3,67},{4,68},{5,69},{6,70},{7,71},{8,10},{9,... | collective-permute-start | bytes 1769480 | tf_op jit(solution)/shard_map/ppermute | solution.py:32
  23.6 18.6 %collective-permute-start.13 = (bf16[256,1152]{1,0:T(8,128)(2,1)S(1)}, bf16[256,1152]{1,0:T(8,128)(2,1)S(1)}, u32[]{:S(2)}, u32[]{:S(2)}) collective-permute-start(bf16[256,1152]{1,0:T(8,128)(2,1)S(1)} %pad_maximum_fusion.3.refs_9_), channel_id=1, source_target_pairs={{0,192},{1,193},{2,194},{3,195},{4,196},{5,197},{6,198},{7,199},{8... | collective-permute-start | bytes 1769480 | tf_op jit(solution)/shard_map/ppermute | solution.py:32
  25.1 17.1 %collective-permute-start.14 = (bf16[256,1152]{1,0:T(8,128)(2,1)S(1)}, bf16[256,1152]{1,0:T(8,128)(2,1)S(1)}, u32[]{:S(2)}, u32[]{:S(2)}) collective-permute-start(bf16[256,1152]{1,0:T(8,128)(2,1)S(1)} %pad_maximum_fusion.3.refs_9_), channel_id=1, source_target_pairs={{0,128},{1,129},{2,130},{3,131},{4,132},{5,133},{6,134},{7,135},{8... | collective-permute-start | bytes 1769480 | tf_op jit(solution)/shard_map/ppermute | solution.py:32
  26.6 8.7 %collective-permute-start.8 = (bf16[128,1152]{1,0:T(8,128)(2,1)S(1)}, bf16[128,1152]{1,0:T(8,128)(2,1)}, u32[]{:S(2)}, u32[]{:S(2)}) collective-permute-start(bf16[128,1152]{1,0:T(8,128)(2,1)S(1)} %collective-permute-done.5.refs_2_), channel_id=1, source_target_pairs={{0,16},{1,17},{2,18},{3,19},{4,20},{5,21},{6,22},{7,23},{8,57},{9,... | collective-permute-start | bytes 884744 | tf_op jit(solution)/shard_map/ppermute | solution.py:32
  30.1 7.8 %collective-permute-start.9 = (bf16[64,1152]{1,0:T(8,128)(2,1)S(1)}, bf16[64,1152]{1,0:T(8,128)(2,1)}, u32[]{:S(2)}, u32[]{:S(2)}) collective-permute-start(bf16[64,1152]{1,0:T(8,128)(2,1)S(1)} %slice.144), channel_id=1, source_target_pairs={{0,32},{1,33},{2,34},{3,35},{4,36},{5,37},{6,38},{7,39},{8,41},{9,... | collective-permute-start | bytes 442376 | tf_op jit(solution)/shard_map/ppermute | solution.py:32
  35.3 6.9 %collective-permute-start.10 = (bf16[128,1152]{1,0:T(8,128)(2,1)}, bf16[128,1152]{1,0:T(8,128)(2,1)}, u32[]{:S(2)}, u32[]{:S(2)}) collective-permute-start(bf16[128,1152]{1,0:T(8,128)(2,1)} %collective-permute-done.8.refs_3_), channel_id=1, source_target_pairs={{0,8},{1,9},{2,10},{3,11},{4,12},{5,13},{6,14},{7,15},{8,0},{9,1},... | collective-permute-start | bytes 884744 | tf_op jit(solution)/shard_map/ppermute | solution.py:32
  55.3 13.8 %collective-permute-start.20 = (f32[448,1152]{1,0:T(8,128)S(1)}, f32[448,1152]{1,0:T(8,128)S(1)}, u32[]{:S(2)}, u32[]{:S(2)}) collective-permute-start(f32[448,1152]{1,0:T(8,128)S(1)} %get-tuple-element.48), channel_id=1, source_target_pairs={{0,8},{1,9},{2,10},{3,11},{4,12},{5,13},{6,14},{7,15},{8,0},{9,1},... | collective-permute-start | bytes 6193160 | tf_op jit(solution)/shard_map/ppermute | solution.py:32
  56.0 8.9 %collective-permute-start.19 = (f32[8,128]{1,0:T(8,128)S(1)}, f32[8,128]{1,0:T(8,128)S(1)}, u32[]{:S(2)}, u32[]{:S(2)}) collective-permute-start(f32[8,128]{1,0:T(8,128)S(1)} %add.116), channel_id=1, source_target_pairs={{0,33},{1,32},{2,35},{3,34},{4,37},{5,36},{6,39},{7,38},{8,41},{9,... | collective-permute-start | bytes 12296 | tf_op jit(solution)/shard_map/ppermute | solution.py:32
  57.6 7.4 %collective-permute-start.18 = (f32[8,128]{1,0:T(8,128)S(1)}, f32[8,128]{1,0:T(8,128)S(1)}, u32[]{:S(2)}, u32[]{:S(2)}) collective-permute-start(f32[8,128]{1,0:T(8,128)S(1)} %add.116), channel_id=1, source_target_pairs={{0,1},{1,0},{2,3},{3,2},{4,5},{5,4},{6,7},{7,6},{8,9},{9,8},{10,11... | collective-permute-start | bytes 12296 | tf_op jit(solution)/shard_map/ppermute | solution.py:32
  65.5 15.4 %collective-permute-start.23 = (f16[264,1152]{1,0:T(8,128)(2,1)S(1)}, f16[264,1152]{1,0:T(8,128)(2,1)S(1)}, u32[]{:S(2)}, u32[]{:S(2)}) collective-permute-start(f16[264,1152]{1,0:T(8,128)(2,1)S(1)} %get-tuple-element.75), channel_id=1, source_target_pairs={{0,192},{1,193},{2,194},{3,195},{4,196},{5,197},{6,198},{7,199},{8... | collective-permute-start | bytes 1824776 | tf_op jit(solution)/shard_map/ppermute | solution.py:32
  67.3 17.0 %collective-permute-start.24 = (f16[264,1152]{1,0:T(8,128)(2,1)S(1)}, f16[264,1152]{1,0:T(8,128)(2,1)S(1)}, u32[]{:S(2)}, u32[]{:S(2)}) collective-permute-start(f16[264,1152]{1,0:T(8,128)(2,1)S(1)} %get-tuple-element.74), channel_id=1, source_target_pairs={{0,64},{1,65},{2,66},{3,67},{4,68},{5,69},{6,70},{7,71},{8,10},{9,... | collective-permute-start | bytes 1824776 | tf_op jit(solution)/shard_map/ppermute | solution.py:32
  67.3 17.0 %collective-permute-start.25 = (f16[264,1152]{1,0:T(8,128)(2,1)S(1)}, f16[264,1152]{1,0:T(8,128)(2,1)S(1)}, u32[]{:S(2)}, u32[]{:S(2)}) collective-permute-start(f16[264,1152]{1,0:T(8,128)(2,1)S(1)} %get-tuple-element.73), channel_id=1, source_target_pairs={{0,128},{1,129},{2,130},{3,131},{4,132},{5,133},{6,134},{7,135},{8... | collective-permute-start | bytes 1824776 | tf_op jit(solution)/shard_map/ppermute | solution.py:32
  70.1 15.0 %collective-permute-start.21 = (f16[128,1152]{1,0:T(8,128)(2,1)S(1)}, f16[128,1152]{1,0:T(8,128)(2,1)S(1)}, u32[]{:S(2)}, u32[]{:S(2)}) collective-permute-start(f16[128,1152]{1,0:T(8,128)(2,1)S(1)} %get-tuple-element.66), channel_id=1, source_target_pairs={{0,49},{1,48},{2,51},{3,50},{4,53},{5,52},{6,55},{7,54},{8,24},{9,... | collective-permute-start | bytes 884744 | tf_op jit(solution)/shard_map/ppermute | solution.py:32
  70.7 14.4 %collective-permute-start.22 = (f16[64,1152]{1,0:T(8,128)(2,1)S(1)}, f16[64,1152]{1,0:T(8,128)(2,1)S(1)}, u32[]{:S(2)}, u32[]{:S(2)}) collective-permute-start(f16[64,1152]{1,0:T(8,128)(2,1)S(1)} %fusion.7), channel_id=1, source_target_pairs={{0,33},{1,32},{2,35},{3,34},{4,37},{5,36},{6,39},{7,38},{8,40},{9,... | collective-permute-start | bytes 442376 | tf_op jit(solution)/shard_map/ppermute | solution.py:32
  84.5 12.4 %collective-permute-start.29 = (f16[128,1152]{1,0:T(8,128)(2,1)}, f16[128,1152]{1,0:T(8,128)(2,1)}, u32[]{:S(2)}, u32[]{:S(2)}) collective-permute-start(f16[128,1152]{1,0:T(8,128)(2,1)} %get-tuple-element.65), channel_id=1, source_target_pairs={{0,49},{1,48},{2,51},{3,50},{4,53},{5,52},{6,55},{7,54},{8,24},{9,... | collective-permute-start | bytes 884744 | tf_op jit(solution)/shard_map/ppermute | solution.py:32
  85.9 5.9 %collective-permute-start.28 = (f16[72,1152]{1,0:T(8,128)(2,1)S(1)}, f16[72,1152]{1,0:T(8,128)(2,1)S(1)}, u32[]{:S(2)}, u32[]{:S(2)}) collective-permute-start(f16[72,1152]{1,0:T(8,128)(2,1)S(1)} %get-tuple-element.72), channel_id=1, source_target_pairs={{0,4},{1,5},{2,6},{3,7},{4,0},{5,1},{6,2},{7,3},{8,136},{9,137},{1... | collective-permute-start | bytes 497672 | tf_op jit(solution)/shard_map/ppermute | solution.py:32
  87.1 6.4 %collective-permute-start.27 = (f16[72,1152]{1,0:T(8,128)(2,1)S(1)}, f16[72,1152]{1,0:T(8,128)(2,1)S(1)}, u32[]{:S(2)}, u32[]{:S(2)}) collective-permute-start(f16[72,1152]{1,0:T(8,128)(2,1)S(1)} %get-tuple-element.71), channel_id=1, source_target_pairs={{0,2},{1,3},{2,4},{3,5},{4,6},{5,7},{6,0},{7,1},{8,72},{9,73},{10,... | collective-permute-start | bytes 497672 | tf_op jit(solution)/shard_map/ppermute | solution.py:32
  90.5 9.4 %collective-permute-start.30 = (f16[128,1152]{1,0:T(8,128)(2,1)}, f16[128,1152]{1,0:T(8,128)(2,1)}, u32[]{:S(2)}, u32[]{:S(2)}) collective-permute-start(f16[128,1152]{1,0:T(8,128)(2,1)} %multiply_convert_fusion.3), channel_id=1, source_target_pairs={{0,33},{1,32},{2,35},{3,34},{4,37},{5,36},{6,39},{7,38},{8,40},{9,... | collective-permute-start | bytes 884744 | tf_op jit(solution)/shard_map/ppermute | solution.py:32
  101.2 8.6 %collective-permute-start.31 = (f32[64,1152]{1,0:T(8,128)S(1)}, f32[64,1152]{1,0:T(8,128)S(1)}, u32[]{:S(2)}, u32[]{:S(2)}) collective-permute-start(f32[64,1152]{1,0:T(8,128)S(1)} %slice.201), channel_id=1, source_target_pairs={{0,8},{1,9},{2,10},{3,11},{4,12},{5,13},{6,14},{7,15},{8,0},{9,1},... | collective-permute-start | bytes 884744 | tf_op jit(solution)/shard_map/ppermute | solution.py:32
  (13 other events, 63.0 us)

commit v3 on v2

--- a/solution.py
+++ b/solution.py
@@ -1,3 +1,4 @@
+import functools
 import itertools
 
 import jax
@@ -54,6 +55,10 @@
 
 def flip_second(bit, v):
     return permute(lambda y, z, c, x: (y ^ bit, z, c, x) if c == 0 else (y, z, c, x ^ bit), v)
+
+
+def add_up(messages):
+    return sum(m.astype(F32) for m in messages) * UP
 
 
 def split(sums):
@@ -67,6 +72,7 @@
 
 
 def join(codes):
+    codes = codes.astype(F32)
     return (codes[:, :128] + codes[:, 128:256] / 2048.0 + codes[:, 256:384] / 2048.0**2) / SHRINK
 
 
@@ -74,11 +80,15 @@
     return (sums * DOWN).astype(F16)
 
 
+def unit_rows(wide):
+    length = jnp.sqrt(jnp.sum(wide * wide, axis=-1, keepdims=True) + tiny_eps)
+    return wide / length, length
+
+
 def normalise_kernel(images, texts, img_low, txt_low):
     for src, dst in ((images, img_low), (texts, txt_low)):
-        wide = src[...].astype(F32)
-        length = jnp.sqrt(jnp.sum(wide * wide, axis=-1, keepdims=True) + tiny_eps)
-        dst[...] = (wide / length).astype(BF16)
+        unit, _ = unit_rows(src[...].astype(F32))
+        dst[...] = unit.astype(BF16)
 
 
 def fold_rows(value):
@@ -157,37 +167,46 @@
         )
 
 
-def project_kernel(images, texts, img_dir, txt_dir, grad_images, grad_texts):
-    for src, sums, dst in ((images, img_dir, grad_images), (texts, txt_dir, grad_texts)):
-        direction = sums[...]
-        wide = src[...].astype(F32)
-        length = jnp.sqrt(jnp.sum(wide * wide, axis=-1, keepdims=True) + tiny_eps)
-        unit = wide / length
-        along = jnp.sum(unit * direction, axis=-1, keepdims=True)
-        dst[...] = (direction - unit * along) / length
+def project_kernel(values, sums, grads):
+    unit, length = unit_rows(values[...].astype(F32))
+    direction = sums[...]
+    along = jnp.sum(unit * direction, axis=-1, keepdims=True)
+    grads[...] = (direction - unit * along) / length
+
+
+def finish_kernel(share, sc, images, img_dir, sums, grads, mean_loss, grad_log_scale, grad_bias):
+    project_kernel(images, img_dir, grads)
+    mean_loss[0] = sums[0, 0] * share
+    grad_bias[0] = sums[1, 0] * share
+    grad_log_scale[0] = sc[0] * (sums[2, 0] * share)
 
 
 def shards(images, texts, log_scale, bias):
     rows, d = images.shape
     arr = jax.ShapeDtypeStruct
+    small = pltpu.CompilerParams(vmem_limit_bytes=4 * 1024 * 1024)
     img_low, txt_low = pl.pallas_call(
-        normalise_kernel, out_shape=(arr((rows, d), BF16), arr((rows, d), BF16)), name="normalise"
+        normalise_kernel,
+        out_shape=(arr((rows, d), BF16), arr((rows, d), BF16)),
+        compiler_params=small,
+        name="normalise",
     )(images, texts)
+    pair = jnp.concatenate([img_low, sibling(img_low)], axis=0)
     scale = jnp.exp(log_scale)
     scalars = jnp.stack([scale, bias])
 
-    pair = jnp.concatenate([img_low, sibling(img_low)], axis=0)
-    r1 = along_z(1, pair)
+    pair, txt_low = lax.optimization_barrier((pair, txt_low))
     r2 = along_z(2, pair)
     a, b, c = first(1, txt_low), first(-1, txt_low), first(2, txt_low)
     block = jnp.concatenate([txt_low, a, b, c], axis=0)
     block, pair = lax.optimization_barrier((block, pair))
     ta, tb, tc = second(1, block), second(-1, block), second(2, block)
+    r1 = along_z(1, pair)
     q1, q2 = sibling(r1), sibling(r2)
-    r2, q1, q2 = lax.optimization_barrier((r2, q1, q2))
+    r2, q2 = lax.optimization_barrier((r2, q2))
     r3 = along_z(1, r2)
     r4 = along_z(2, r2[:64])
-    imgs = (pair, r1, r2, r3, r4, q1, q2, sibling(r3), sibling(r4))
+    imgs = (pair, r1, r3, r2, r4, q1, sibling(r3), q2, sibling(r4))
     txts = (block, ta, tb, tc)
 
     vmem = pl.BlockSpec(memory_space=pltpu.VMEM)
@@ -202,9 +221,9 @@
         cost_estimate=cost,
         name="pairs",
     )(scalars, *imgs, *txts)
+
     sums = sums + sibling(sums)
     w, sums = lax.optimization_barrier((w, sums))
-
     keep, send = pl.pallas_call(
         image_kernel,
         in_specs=[vmem] * 2,
@@ -214,10 +233,8 @@
         cost_estimate=cost,
         name="images",
     )(w, y)
-    sums = sums + flip_z(1, sums)
-    got = sibling(send)
-    w, sums, keep = lax.optimization_barrier((w, sums, keep))
-
+    sums = sums + flip_z(4, sums)
+    w, keep = lax.optimization_barrier((w, keep))
     t_own, t_back, t_fore, t_over = pl.pallas_call(
         text_kernel,
         in_specs=[vmem] * 2,
@@ -227,37 +244,45 @@
         cost_estimate=cost,
         name="texts",
     )(w, x)
-    sums = sums + flip_z(2, sums) + flip_z(4, sums) + flip_z(6, sums)
-
-    chain = keep[128:] + got
-    g3 = along_z(-1, low(chain[256:384]))
-    g4 = along_z(-2, low(chain[384:448]))
 
     codes = split(sums)
     out = [jnp.concatenate([low(v), codes], axis=0) for v in (t_back, t_fore, t_over)]
-    back = [second(k, v).astype(F32) for k, v in zip((-1, 1, 2), out)]
-    c2 = chain[128:256] + (g3.astype(F32) + jnp.pad(g4.astype(F32), ((0, 64), (0, 0)))) * UP
-    c2, back[0], back[1], back[2] = lax.optimization_barrier((c2, *back))
-    t_sum = t_own + (back[0][:256] + back[1][:256] + back[2][:256]) * UP
+    back = [second(k, v) for k, v in zip((-1, 1, 2), out)]
+
+    chain = keep[128:] + sibling(send)
+    z1 = along_z(-1, low(chain[:256]))
+    z4 = along_z(-2, low(chain[384:]))
+
+    c2 = low(chain[256:384] + (z1[128:].astype(F32) + jnp.pad(z4.astype(F32), ((0, 64), (0, 0)))) * UP)
+    *back, _, _ = lax.optimization_barrier((*back, z1, z4))
+    z2 = along_z(-2, c2)
+    t_sum = t_own + add_up(v[:256] for v in back)
     sums = sums + sum(join(v[256:]) for v in back)
     codes = split(sums)
     out = [jnp.concatenate([low(t_sum[k * 64 : k * 64 + 64]), codes], axis=0) for k in (1, 2, 3)]
-    back = [first(k, v).astype(F32) for k, v in zip((-1, 1, 2), out)]
-    txt_dir = t_sum[:64] + (back[0][:64] + back[1][:64] + back[2][:64]) * UP
+    back = [first(k, v) for k, v in zip((-1, 1, 2), out)]
+
+    mine = keep[:128] + add_up((z1[:128], z2))
+    img_dir = mine[:64] + sibling(mine[64:])
+
+    txt_dir = t_sum[:64] + add_up(v[:64] for v in back)
     sums = sums + sum(join(v[64:]) for v in back)
-
-    g1 = along_z(-1, low(chain[0:128]))
-    g2 = along_z(-2, low(c2))
-    mine = keep[:128] + (g1.astype(F32) + g2.astype(F32)) * UP
-    img_dir = mine[:64] + sibling(mine[64:])
-
-    grad_images, grad_texts = pl.pallas_call(
-        project_kernel, out_shape=(arr((rows, d), F32), arr((rows, d), F32)), name="project"
-    )(images, texts, img_dir, txt_dir)
-
+    sums = sums + flip_z(1, sums) + flip_z(2, sums) + flip_z(3, sums)
+
+    project = pl.pallas_call(project_kernel, out_shape=arr((rows, d), F32), compiler_params=small, name="project")
+    grad_texts = project(texts, txt_dir)
     total = float(rows * 256)
-    count = total * total
-    return (sums[0, 0] / count, grad_images, grad_texts, scale * sums[2, 0] / count, sums[1, 0] / count)
+    one = pl.BlockSpec(memory_space=pltpu.SMEM)
+    grad_images, *means = pl.pallas_call(
+        functools.partial(finish_kernel, 1.0 / (total * total)),
+        in_specs=[one] + [vmem] * 3,
+        out_specs=[vmem] + [one] * 3,
+        out_shape=[arr((rows, d), F32)] + [arr((1,), F32)] * 3,
+        compiler_params=small,
+        name="finish",
+    )(scalars, images, img_dir, sums)
+    mean_loss, grad_log_scale, grad_bias = (m.reshape(()) for m in means)
+    return (mean_loss, grad_images, grad_texts, grad_log_scale, grad_bias)
 
 
 def solution(mesh):

time: 117 us -> 101 us (0.86)
  other arithmetic: 8.44 us -> 2.41 us
  between operations: 7.57 us -> 2.42 us
  starting transfers between devices: 53.6 us -> 49.3 us
  Pallas kernels: 16.3 us -> 14.9 us
    ppermute x32 -> x31, starting transfers between devices: 53.6 us -> 49.3 us  [permute(): return lax.ppermute(value, AXES, pairs)]
    add x6 -> x5, other arithmetic: 3.64 us -> 0.84 us  [the longest x1 0.32 us: shards(): t_sum = t_own + add_up((v[:256] for v in back))]
    pallas_call x1, Pallas kernels: 1.82 us -> 0.16 us  [shards(): pl.pallas_call(normalise_kernel, out_shape=(arr((rows, d), BF16), arr((ro...]
    convert_element_type x6, other arithmetic: 2 us -> 0.68 us  [low(): return (sums * DOWN).astype(F16)]
    unnamed x11 -> x12, local copies, waits for them, and re-layouts: 2.65 us -> 3.5 us
    ppermute x32 -> x31, waiting for transfers between devices: 27.1 us -> 27.8 us  [permute(): return lax.ppermute(value, AXES, pairs)]
    pallas_call x1 -> x2, Pallas kernels: 2.25 us -> 2.44 us  [the longest x1 1.49 us: shards(): pl.pallas_call(functools.partial(finish_kernel, 1.0 / (total * total)), i...]
  transfers between devices with their start and end apart: 32 -> 31, of which waited for: 11 -> 15; matrix products, arithmetic and copies ran while one was open for 7% -> 2% of each run, Pallas kernels for 5% -> 4%
where the time goes in v3:
time: 101 us; the launch traced here: 100 us
  starting transfers between devices  49.3 us (49%)
  waiting for transfers between devices  27.8 us (28%)
  Pallas kernels  14.9 us (15%)
  local copies, waits for them, and re-layouts  3.54 us (4%)
  between operations  2.42 us (2%)
  other arithmetic  2.41 us (2%)
    ppermute x31, starting transfers between devices, permute(): return lax.ppermute(value, AXES, pairs)  49.3 us
    ppermute x31, waiting for transfers between devices, permute(): return lax.ppermute(value, AXES, pairs)  27.8 us
    pallas_call x1, Pallas kernels, shards(): pl.pallas_call(pair_kernel, in_specs=[pl.BlockSpec(memory_space=pltpu.SME...  6.43 us
    unnamed x12, local copies, waits for them, and re-layouts  3.5 us
    pallas_call x1, Pallas kernels, shards(): pl.pallas_call(text_kernel, in_specs=[vmem] * 2, out_specs=[vmem] * 4, ou...  2.94 us
    pallas_call x1, Pallas kernels, shards(): pl.pallas_call(image_kernel, in_specs=[vmem] * 2, out_specs=[vmem] * 2, o...  2.89 us
  transfers between devices with their start and end apart: 31, of which 15 were waited for; matrix products, arithmetic and copies ran while one was open for 2% of the time, Pallas kernels for 4%

profile of v3, /device:TPU:1, one launch (start us, length us, event | category | flops | bytes accessed | tf_op | source)
XLA Modules:
  0.0 100.3 jit_solution(10800948540307912411)
XLA Ops:
  2.6 3.3 %collective-permute-start = (bf16[64,1152]{1,0:T(8,128)(2,1)S(1)}, bf16[64,1152]{1,0:T(8,128)(2,1)S(1)}, u32[]{:S(2)}, u32[]{:S(2)}) collective-permute-start(bf16[64,1152]{1,0:T(8,128)(2,1)S(1)} %get-tuple-element.34), channel_id=1, source_target_pairs={{0,8},{1,9},{2,10},{3,11},{4,12},{5,13},{6,14},{7,15},{8,0},{9,1},... | collective-permute-start | bytes 442376 | tf_op jit(solution)/shard_map/ppermute | solution.py:33
  7.0 4.4 %collective-permute-start.5 = (bf16[128,1152]{1,0:T(8,128)(2,1)S(1)}, bf16[128,1152]{1,0:T(8,128)(2,1)S(1)}, u32[]{:S(2)}, u32[]{:S(2)}) collective-permute-start(bf16[128,1152]{1,0:T(8,128)(2,1)S(1)} %pad_maximum_fusion.4.refs_0_), channel_id=1, source_target_pairs={{0,32},{1,33},{2,34},{3,35},{4,36},{5,37},{6,38},{7,39},{8,41},{9,... | collective-permute-start | bytes 884744 | tf_op jit(solution)/shard_map/ppermute | solution.py:33
  11.3 2.9 %collective-permute-start.3 = (bf16[64,1152]{1,0:T(8,128)(2,1)S(1)}, bf16[64,1152]{1,0:T(8,128)(2,1)S(1)}, u32[]{:S(2)}, u32[]{:S(2)}) collective-permute-start(bf16[64,1152]{1,0:T(8,128)(2,1)S(1)} %get-tuple-element.36), channel_id=1, source_target_pairs={{0,4},{1,5},{2,6},{3,7},{4,0},{5,1},{6,2},{7,3},{8,136},{9,137},{1... | collective-permute-start | bytes 442376 | tf_op jit(solution)/shard_map/ppermute | solution.py:33
  17.3 1.8 %collective-permute-done.2 = bf16[64,1152]{1,0:T(8,128)(2,1)S(1)} collective-permute-done((bf16[64,1152]{1,0:T(8,128)(2,1)S(1)}, bf16[64,1152]{1,0:T(8,128)(2,1)S(1)}, u32[]{:S(2)}, u32[]{:S(2)}) %collective-permute-start.2) | collective-permute-done | bytes 147488 | tf_op jit(solution)/shard_map/ppermute | solution.py:33
  20.3 1.6 %collective-permute-start.4 = (bf16[128,1152]{1,0:T(8,128)(2,1)S(1)}, bf16[128,1152]{1,0:T(8,128)(2,1)S(1)}, u32[]{:S(2)}, u32[]{:S(2)}) collective-permute-start(bf16[128,1152]{1,0:T(8,128)(2,1)S(1)} %pad_maximum_fusion.4.refs_0_), channel_id=1, source_target_pairs={{0,16},{1,17},{2,18},{3,19},{4,20},{5,21},{6,22},{7,23},{8,57},{9,... | collective-permute-start | bytes 884744 | tf_op jit(solution)/shard_map/ppermute | solution.py:33
  24.6 1.5 %collective-permute-start.14 = (bf16[256,1152]{1,0:T(8,128)(2,1)S(1)}, bf16[256,1152]{1,0:T(8,128)(2,1)S(1)}, u32[]{:S(2)}, u32[]{:S(2)}) collective-permute-start(bf16[256,1152]{1,0:T(8,128)(2,1)S(1)} %pad_maximum_fusion.3.refs_9_), channel_id=1, source_target_pairs={{0,128},{1,129},{2,130},{3,131},{4,132},{5,133},{6,134},{7,135},{8... | collective-permute-start | bytes 1769480 | tf_op jit(solution)/shard_map/ppermute | solution.py:33
  27.1 2.4 %collective-permute-start.7 = (bf16[128,1152]{1,0:T(8,128)(2,1)S(1)}, bf16[128,1152]{1,0:T(8,128)(2,1)}, u32[]{:S(2)}, u32[]{:S(2)}) collective-permute-start(bf16[128,1152]{1,0:T(8,128)(2,1)S(1)} %collective-permute-done.5.refs_3_), channel_id=1, source_target_pairs={{0,16},{1,17},{2,18},{3,19},{4,20},{5,21},{6,22},{7,23},{8,57},{9,... | collective-permute-start | bytes 884744 | tf_op jit(solution)/shard_map/ppermute | solution.py:33
  29.5 3.3 %collective-permute-done.8.refs_4_ = bf16[64,1152]{1,0:T(8,128)(2,1)} collective-permute-done((bf16[64,1152]{1,0:T(8,128)(2,1)S(1)}, bf16[64,1152]{1,0:T(8,128)(2,1)}, u32[]{:S(2)}, u32[]{:S(2)}) %collective-permute-start.8) | collective-permute-done | bytes 147488 | tf_op jit(solution)/shard_map/ppermute | solution.py:33
  32.8 2.0 %collective-permute-start.9 = (bf16[128,1152]{1,0:T(8,128)(2,1)S(1)}, bf16[128,1152]{1,0:T(8,128)(2,1)S(1)}, u32[]{:S(2)}, u32[]{:S(2)}) collective-permute-start(bf16[128,1152]{1,0:T(8,128)(2,1)S(1)} %collective-permute-done.4.refs_1_), channel_id=1, source_target_pairs={{0,8},{1,9},{2,10},{3,11},{4,12},{5,13},{6,14},{7,15},{8,0},{9,1},... | collective-permute-start | bytes 884744 | tf_op jit(solution)/shard_map/ppermute | solution.py:33
  36.1 3.4 %collective-permute-start.10 = (bf16[128,1152]{1,0:T(8,128)(2,1)}, bf16[128,1152]{1,0:T(8,128)(2,1)}, u32[]{:S(2)}, u32[]{:S(2)}) collective-permute-start(bf16[128,1152]{1,0:T(8,128)(2,1)} %collective-permute-done.7.refs_2_), channel_id=1, source_target_pairs={{0,8},{1,9},{2,10},{3,11},{4,12},{5,13},{6,14},{7,15},{8,0},{9,1},... | collective-permute-start | bytes 884744 | tf_op jit(solution)/shard_map/ppermute | solution.py:33
  42.9 6.4 %pairs.1 = (bf16[1024,1024]{1,0:T(8,128)(2,1)S(1)}, bf16[1024,1152]{1,0:T(8,128)(2,1)S(1)}, bf16[1024,1152]{1,0:T(8,128)(2,1)S(1)}, f32[8,128]{1,0:T(8,128)S(1)}) custom-call(f32[2]{0:T(128)S(1)} %pad_maximum_fusion.8.sc, bf16[128,1152]{1,0:T(8,128)(2,1)S(1)} %pad_maximum_fusion.4.refs_0_, bf16[128,1152]{1,0:T(8,128)(2,1)S(1)} %collective-permute-done.4.refs_1_, ...), custom_call_target="tpu_custom_call" | custom-call | flops 2415919104 | bytes 7000000 | tf_op jit(solution)/shard_map/pairs/pallas_call | solution.py:215
  50.6 2.9 %images.4 = (f32[576,1152]{1,0:T(8,128)S(1)}, f32[448,1152]{1,0:T(8,128)S(1)}) custom-call(bf16[1024,1024]{1,0:T(8,128)(2,1)S(1)} %get-tuple-element.50.w_ref, bf16[1024,1152]{1,0:T(8,128)(2,1)S(1)} %get-tuple-element.45.y_ref), custom_call_target="tpu_custom_call" | custom-call | flops 2415919104 | bytes 7000000 | tf_op jit(solution)/shard_map/images/pallas_call | solution.py:227
  53.8 2.3 %collective-permute-start.21 = (f32[8,128]{1,0:T(8,128)S(1)}, f32[8,128]{1,0:T(8,128)S(1)}, u32[]{:S(2)}, u32[]{:S(2)}) collective-permute-start(f32[8,128]{1,0:T(8,128)S(1)} %add.115), channel_id=1, source_target_pairs={{0,1},{1,0},{2,3},{3,2},{4,5},{5,4},{6,7},{7,6},{8,9},{9,8},{10,11... | collective-permute-start | bytes 12296 | tf_op jit(solution)/shard_map/ppermute | solution.py:33
  56.1 2.9 %texts.3 = (f32[256,1152]{1,0:T(8,128)S(1)}, f32[256,1152]{1,0:T(8,128)S(1)}, f32[256,1152]{1,0:T(8,128)S(1)}, f32[256,1152]{1,0:T(8,128)S(1)}) custom-call(bf16[1024,1024]{1,0:T(8,128)(2,1)S(1)} %get-tuple-element.50.w_ref, bf16[1024,1152]{1,0:T(8,128)(2,1)S(1)} %get-tuple-element.51.x_ref), custom_call_target="tpu_custom_call" | custom-call | flops 2415919104 | bytes 7000000 | tf_op jit(solution)/shard_map/texts/pallas_call | solution.py:238
  60.7 1.7 %collective-permute-start.22 = (f16[264,1152]{1,0:T(8,128)(2,1)S(1)}, f16[264,1152]{1,0:T(8,128)(2,1)S(1)}, u32[]{:S(2)}, u32[]{:S(2)}) collective-permute-start(f16[264,1152]{1,0:T(8,128)(2,1)S(1)} %get-tuple-element.75), channel_id=1, source_target_pairs={{0,192},{1,193},{2,194},{3,195},{4,196},{5,197},{6,198},{7,199},{8... | collective-permute-start | bytes 1824776 | tf_op jit(solution)/shard_map/ppermute | solution.py:33
  62.4 1.7 %collective-permute-start.24 = (f16[264,1152]{1,0:T(8,128)(2,1)S(1)}, f16[264,1152]{1,0:T(8,128)(2,1)S(1)}, u32[]{:S(2)}, u32[]{:S(2)}) collective-permute-start(f16[264,1152]{1,0:T(8,128)(2,1)S(1)} %get-tuple-element.73), channel_id=1, source_target_pairs={{0,128},{1,129},{2,130},{3,131},{4,132},{5,133},{6,134},{7,135},{8... | collective-permute-start | bytes 1824776 | tf_op jit(solution)/shard_map/ppermute | solution.py:33
  64.7 2.9 %collective-permute-start.18 = (f16[64,1152]{1,0:T(8,128)(2,1)S(1)}, f16[64,1152]{1,0:T(8,128)(2,1)S(1)}, u32[]{:S(2)}, u32[]{:S(2)}) collective-permute-start(f16[64,1152]{1,0:T(8,128)(2,1)S(1)} %fusion.6), channel_id=1, source_target_pairs={{0,33},{1,32},{2,35},{3,34},{4,37},{5,36},{6,39},{7,38},{8,40},{9,... | collective-permute-start | bytes 442376 | tf_op jit(solution)/shard_map/ppermute | solution.py:33
  67.6 8.4 %collective-permute-done.22 = f16[264,1152]{1,0:T(8,128)(2,1)S(1)} collective-permute-done((f16[264,1152]{1,0:T(8,128)(2,1)S(1)}, f16[264,1152]{1,0:T(8,128)(2,1)S(1)}, u32[]{:S(2)}, u32[]{:S(2)}) %collective-permute-start.22) | collective-permute-done | bytes 608288 | tf_op jit(solution)/shard_map/ppermute | solution.py:33
  75.9 3.4 %collective-permute-done.23 = f16[264,1152]{1,0:T(8,128)(2,1)S(1)} collective-permute-done((f16[264,1152]{1,0:T(8,128)(2,1)S(1)}, f16[264,1152]{1,0:T(8,128)(2,1)S(1)}, u32[]{:S(2)}, u32[]{:S(2)}) %collective-permute-start.23) | collective-permute-done | bytes 608288 | tf_op jit(solution)/shard_map/ppermute | solution.py:33
  80.0 1.7 %collective-permute-start.27 = (f16[72,1152]{1,0:T(8,128)(2,1)S(1)}, f16[72,1152]{1,0:T(8,128)(2,1)S(1)}, u32[]{:S(2)}, u32[]{:S(2)}) collective-permute-start(f16[72,1152]{1,0:T(8,128)(2,1)S(1)} %get-tuple-element.72), channel_id=1, source_target_pairs={{0,4},{1,5},{2,6},{3,7},{4,0},{5,1},{6,2},{7,3},{8,136},{9,137},{1... | collective-permute-start | bytes 497672 | tf_op jit(solution)/shard_map/ppermute | solution.py:33
  82.6 2.1 %collective-permute-start.25 = (f16[72,1152]{1,0:T(8,128)(2,1)S(1)}, f16[72,1152]{1,0:T(8,128)(2,1)S(1)}, u32[]{:S(2)}, u32[]{:S(2)}) collective-permute-start(f16[72,1152]{1,0:T(8,128)(2,1)S(1)} %get-tuple-element.70), channel_id=1, source_target_pairs={{0,6},{1,7},{2,0},{3,1},{4,2},{5,3},{6,4},{7,5},{8,200},{9,201},{1... | collective-permute-start | bytes 497672 | tf_op jit(solution)/shard_map/ppermute | solution.py:33
  85.8 2.1 %collective-permute-done.26 = f16[72,1152]{1,0:T(8,128)(2,1)S(1)} collective-permute-done((f16[72,1152]{1,0:T(8,128)(2,1)S(1)}, f16[72,1152]{1,0:T(8,128)(2,1)S(1)}, u32[]{:S(2)}, u32[]{:S(2)}) %collective-permute-start.26) | collective-permute-done | bytes 165920 | tf_op jit(solution)/shard_map/ppermute | solution.py:33
  87.9 2.7 %collective-permute-start.30 = (f32[8,128]{1,0:T(8,128)S(1)}, f32[8,128]{1,0:T(8,128)S(1)}, u32[]{:S(2)}, u32[]{:S(2)}) collective-permute-start(f32[8,128]{1,0:T(8,128)S(1)} %fusion.28), channel_id=1, source_target_pairs={{0,48},{1,49},{2,50},{3,51},{4,52},{5,53},{6,54},{7,55},{8,56},{9,... | collective-permute-start | bytes 12296 | tf_op jit(solution)/shard_map/ppermute | solution.py:33
  92.8 4.6 %collective-permute-start.20 = (f32[64,1152]{1,0:T(8,128)S(1)}, f32[64,1152]{1,0:T(8,128)S(1)}, u32[]{:S(2)}, u32[]{:S(2)}) collective-permute-start(f32[64,1152]{1,0:T(8,128)S(1)} %slice.182), channel_id=1, source_target_pairs={{0,8},{1,9},{2,10},{3,11},{4,12},{5,13},{6,14},{7,15},{8,0},{9,1},... | collective-permute-start | bytes 884744 | tf_op jit(solution)/shard_map/ppermute | solution.py:33
  (89 shorter events, 25.4 us)
Async XLA Ops:
  7.0 9.9 %collective-permute-start.5 = (bf16[128,1152]{1,0:T(8,128)(2,1)S(1)}, bf16[128,1152]{1,0:T(8,128)(2,1)S(1)}, u32[]{:S(2)}, u32[]{:S(2)}) collective-permute-start(bf16[128,1152]{1,0:T(8,128)(2,1)S(1)} %pad_maximum_fusion.4.refs_0_), channel_id=1, source_target_pairs={{0,32},{1,33},{2,34},{3,35},{4,36},{5,37},{6,38},{7,39},{8,41},{9,... | collective-permute-start | bytes 884744 | tf_op jit(solution)/shard_map/ppermute | solution.py:33
  11.3 5.9 %collective-permute-start.3 = (bf16[64,1152]{1,0:T(8,128)(2,1)S(1)}, bf16[64,1152]{1,0:T(8,128)(2,1)S(1)}, u32[]{:S(2)}, u32[]{:S(2)}) collective-permute-start(bf16[64,1152]{1,0:T(8,128)(2,1)S(1)} %get-tuple-element.36), channel_id=1, source_target_pairs={{0,4},{1,5},{2,6},{3,7},{4,0},{5,1},{6,2},{7,3},{8,136},{9,137},{1... | collective-permute-start | bytes 442376 | tf_op jit(solution)/shard_map/ppermute | solution.py:33
  16.9 9.2 %collective-permute-start.6 = (bf16[128,1152]{1,0:T(8,128)(2,1)S(1)}, bf16[128,1152]{1,0:T(8,128)(2,1)S(1)}, u32[]{:S(2)}, u32[]{:S(2)}) collective-permute-start(bf16[128,1152]{1,0:T(8,128)(2,1)S(1)} %collective-permute-done.5.refs_3_), channel_id=1, source_target_pairs={{0,8},{1,9},{2,10},{3,11},{4,12},{5,13},{6,14},{7,15},{8,0},{9,1},... | collective-permute-start | bytes 884744 | tf_op jit(solution)/shard_map/ppermute | solution.py:33
  20.3 6.8 %collective-permute-start.4 = (bf16[128,1152]{1,0:T(8,128)(2,1)S(1)}, bf16[128,1152]{1,0:T(8,128)(2,1)S(1)}, u32[]{:S(2)}, u32[]{:S(2)}) collective-permute-start(bf16[128,1152]{1,0:T(8,128)(2,1)S(1)} %pad_maximum_fusion.4.refs_0_), channel_id=1, source_target_pairs={{0,16},{1,17},{2,18},{3,19},{4,20},{5,21},{6,22},{7,23},{8,57},{9,... | collective-permute-start | bytes 884744 | tf_op jit(solution)/shard_map/ppermute | solution.py:33
  21.9 19.8 %collective-permute-start.12 = (bf16[256,1152]{1,0:T(8,128)(2,1)S(1)}, bf16[256,1152]{1,0:T(8,128)(2,1)S(1)}, u32[]{:S(2)}, u32[]{:S(2)}) collective-permute-start(bf16[256,1152]{1,0:T(8,128)(2,1)S(1)} %pad_maximum_fusion.3.refs_9_), channel_id=1, source_target_pairs={{0,64},{1,65},{2,66},{3,67},{4,68},{5,69},{6,70},{7,71},{8,10},{9,... | collective-permute-start | bytes 1769480 | tf_op jit(solution)/shard_map/ppermute | solution.py:33
  23.1 18.5 %collective-permute-start.13 = (bf16[256,1152]{1,0:T(8,128)(2,1)S(1)}, bf16[256,1152]{1,0:T(8,128)(2,1)S(1)}, u32[]{:S(2)}, u32[]{:S(2)}) collective-permute-start(bf16[256,1152]{1,0:T(8,128)(2,1)S(1)} %pad_maximum_fusion.3.refs_9_), channel_id=1, source_target_pairs={{0,192},{1,193},{2,194},{3,195},{4,196},{5,197},{6,198},{7,199},{8... | collective-permute-start | bytes 1769480 | tf_op jit(solution)/shard_map/ppermute | solution.py:33
  24.6 17.1 %collective-permute-start.14 = (bf16[256,1152]{1,0:T(8,128)(2,1)S(1)}, bf16[256,1152]{1,0:T(8,128)(2,1)S(1)}, u32[]{:S(2)}, u32[]{:S(2)}) collective-permute-start(bf16[256,1152]{1,0:T(8,128)(2,1)S(1)} %pad_maximum_fusion.3.refs_9_), channel_id=1, source_target_pairs={{0,128},{1,129},{2,130},{3,131},{4,132},{5,133},{6,134},{7,135},{8... | collective-permute-start | bytes 1769480 | tf_op jit(solution)/shard_map/ppermute | solution.py:33
  26.1 6.7 %collective-permute-start.8 = (bf16[64,1152]{1,0:T(8,128)(2,1)S(1)}, bf16[64,1152]{1,0:T(8,128)(2,1)}, u32[]{:S(2)}, u32[]{:S(2)}) collective-permute-start(bf16[64,1152]{1,0:T(8,128)(2,1)S(1)} %slice.132), channel_id=1, source_target_pairs={{0,32},{1,33},{2,34},{3,35},{4,36},{5,37},{6,38},{7,39},{8,41},{9,... | collective-permute-start | bytes 442376 | tf_op jit(solution)/shard_map/ppermute | solution.py:33
  27.1 9.0 %collective-permute-start.7 = (bf16[128,1152]{1,0:T(8,128)(2,1)S(1)}, bf16[128,1152]{1,0:T(8,128)(2,1)}, u32[]{:S(2)}, u32[]{:S(2)}) collective-permute-start(bf16[128,1152]{1,0:T(8,128)(2,1)S(1)} %collective-permute-done.5.refs_3_), channel_id=1, source_target_pairs={{0,16},{1,17},{2,18},{3,19},{4,20},{5,21},{6,22},{7,23},{8,57},{9,... | collective-permute-start | bytes 884744 | tf_op jit(solution)/shard_map/ppermute | solution.py:33
  32.8 6.7 %collective-permute-start.9 = (bf16[128,1152]{1,0:T(8,128)(2,1)S(1)}, bf16[128,1152]{1,0:T(8,128)(2,1)S(1)}, u32[]{:S(2)}, u32[]{:S(2)}) collective-permute-start(bf16[128,1152]{1,0:T(8,128)(2,1)S(1)} %collective-permute-done.4.refs_1_), channel_id=1, source_target_pairs={{0,8},{1,9},{2,10},{3,11},{4,12},{5,13},{6,14},{7,15},{8,0},{9,1},... | collective-permute-start | bytes 884744 | tf_op jit(solution)/shard_map/ppermute | solution.py:33
  36.1 5.8 %collective-permute-start.10 = (bf16[128,1152]{1,0:T(8,128)(2,1)}, bf16[128,1152]{1,0:T(8,128)(2,1)}, u32[]{:S(2)}, u32[]{:S(2)}) collective-permute-start(bf16[128,1152]{1,0:T(8,128)(2,1)} %collective-permute-done.7.refs_2_), channel_id=1, source_target_pairs={{0,8},{1,9},{2,10},{3,11},{4,12},{5,13},{6,14},{7,15},{8,0},{9,1},... | collective-permute-start | bytes 884744 | tf_op jit(solution)/shard_map/ppermute | solution.py:33
  53.5 10.6 %collective-permute-start.16 = (f32[448,1152]{1,0:T(8,128)S(1)}, f32[448,1152]{1,0:T(8,128)S(1)}, u32[]{:S(2)}, u32[]{:S(2)}) collective-permute-start(f32[448,1152]{1,0:T(8,128)S(1)} %get-tuple-element.48), channel_id=1, source_target_pairs={{0,8},{1,9},{2,10},{3,11},{4,12},{5,13},{6,14},{7,15},{8,0},{9,1},... | collective-permute-start | bytes 6193160 | tf_op jit(solution)/shard_map/ppermute | solution.py:33
  53.8 6.4 %collective-permute-start.21 = (f32[8,128]{1,0:T(8,128)S(1)}, f32[8,128]{1,0:T(8,128)S(1)}, u32[]{:S(2)}, u32[]{:S(2)}) collective-permute-start(f32[8,128]{1,0:T(8,128)S(1)} %add.115), channel_id=1, source_target_pairs={{0,1},{1,0},{2,3},{3,2},{4,5},{5,4},{6,7},{7,6},{8,9},{9,8},{10,11... | collective-permute-start | bytes 12296 | tf_op jit(solution)/shard_map/ppermute | solution.py:33
  60.7 15.2 %collective-permute-start.22 = (f16[264,1152]{1,0:T(8,128)(2,1)S(1)}, f16[264,1152]{1,0:T(8,128)(2,1)S(1)}, u32[]{:S(2)}, u32[]{:S(2)}) collective-permute-start(f16[264,1152]{1,0:T(8,128)(2,1)S(1)} %get-tuple-element.75), channel_id=1, source_target_pairs={{0,192},{1,193},{2,194},{3,195},{4,196},{5,197},{6,198},{7,199},{8... | collective-permute-start | bytes 1824776 | tf_op jit(solution)/shard_map/ppermute | solution.py:33
  62.4 17.0 %collective-permute-start.23 = (f16[264,1152]{1,0:T(8,128)(2,1)S(1)}, f16[264,1152]{1,0:T(8,128)(2,1)S(1)}, u32[]{:S(2)}, u32[]{:S(2)}) collective-permute-start(f16[264,1152]{1,0:T(8,128)(2,1)S(1)} %get-tuple-element.74), channel_id=1, source_target_pairs={{0,64},{1,65},{2,66},{3,67},{4,68},{5,69},{6,70},{7,71},{8,10},{9,... | collective-permute-start | bytes 1824776 | tf_op jit(solution)/shard_map/ppermute | solution.py:33
  62.4 17.0 %collective-permute-start.24 = (f16[264,1152]{1,0:T(8,128)(2,1)S(1)}, f16[264,1152]{1,0:T(8,128)(2,1)S(1)}, u32[]{:S(2)}, u32[]{:S(2)}) collective-permute-start(f16[264,1152]{1,0:T(8,128)(2,1)S(1)} %get-tuple-element.73), channel_id=1, source_target_pairs={{0,128},{1,129},{2,130},{3,131},{4,132},{5,133},{6,134},{7,135},{8... | collective-permute-start | bytes 1824776 | tf_op jit(solution)/shard_map/ppermute | solution.py:33
  64.5 14.8 %collective-permute-start.17 = (f16[256,1152]{1,0:T(8,128)(2,1)S(1)}, f16[256,1152]{1,0:T(8,128)(2,1)S(1)}, u32[]{:S(2)}, u32[]{:S(2)}) collective-permute-start(f16[256,1152]{1,0:T(8,128)(2,1)S(1)} %fusion), channel_id=1, source_target_pairs={{0,49},{1,48},{2,51},{3,50},{4,53},{5,52},{6,55},{7,54},{8,24},{9,... | collective-permute-start | bytes 1769480 | tf_op jit(solution)/shard_map/ppermute | solution.py:33
  64.7 14.7 %collective-permute-start.18 = (f16[64,1152]{1,0:T(8,128)(2,1)S(1)}, f16[64,1152]{1,0:T(8,128)(2,1)S(1)}, u32[]{:S(2)}, u32[]{:S(2)}) collective-permute-start(f16[64,1152]{1,0:T(8,128)(2,1)S(1)} %fusion.6), channel_id=1, source_target_pairs={{0,33},{1,32},{2,35},{3,34},{4,37},{5,36},{6,39},{7,38},{8,40},{9,... | collective-permute-start | bytes 442376 | tf_op jit(solution)/shard_map/ppermute | solution.py:33
  81.9 10.7 %collective-permute-start.19 = (f16[128,1152]{1,0:T(8,128)(2,1)S(1)}, f16[128,1152]{1,0:T(8,128)(2,1)S(1)}, u32[]{:S(2)}, u32[]{:S(2)}) collective-permute-start(f16[128,1152]{1,0:T(8,128)(2,1)S(1)} %fusion.2), channel_id=1, source_target_pairs={{0,33},{1,32},{2,35},{3,34},{4,37},{5,36},{6,39},{7,38},{8,40},{9,... | collective-permute-start | bytes 884744 | tf_op jit(solution)/shard_map/ppermute | solution.py:33
  82.0 5.9 %collective-permute-start.26 = (f16[72,1152]{1,0:T(8,128)(2,1)S(1)}, f16[72,1152]{1,0:T(8,128)(2,1)S(1)}, u32[]{:S(2)}, u32[]{:S(2)}) collective-permute-start(f16[72,1152]{1,0:T(8,128)(2,1)S(1)} %get-tuple-element.71), channel_id=1, source_target_pairs={{0,2},{1,3},{2,4},{3,5},{4,6},{5,7},{6,0},{7,1},{8,72},{9,73},{10,... | collective-permute-start | bytes 497672 | tf_op jit(solution)/shard_map/ppermute | solution.py:33
  87.9 10.5 %collective-permute-start.30 = (f32[8,128]{1,0:T(8,128)S(1)}, f32[8,128]{1,0:T(8,128)S(1)}, u32[]{:S(2)}, u32[]{:S(2)}) collective-permute-start(f32[8,128]{1,0:T(8,128)S(1)} %fusion.28), channel_id=1, source_target_pairs={{0,48},{1,49},{2,50},{3,51},{4,52},{5,53},{6,54},{7,55},{8,56},{9,... | collective-permute-start | bytes 12296 | tf_op jit(solution)/shard_map/ppermute | solution.py:33
  90.6 7.8 %collective-permute-start.29 = (f32[8,128]{1,0:T(8,128)S(1)}, f32[8,128]{1,0:T(8,128)S(1)}, u32[]{:S(2)}, u32[]{:S(2)}) collective-permute-start(f32[8,128]{1,0:T(8,128)S(1)} %fusion.28), channel_id=1, source_target_pairs={{0,32},{1,33},{2,34},{3,35},{4,36},{5,37},{6,38},{7,39},{8,40},{9,... | collective-permute-start | bytes 12296 | tf_op jit(solution)/shard_map/ppermute | solution.py:33
  91.0 7.4 %collective-permute-start.28 = (f32[8,128]{1,0:T(8,128)S(1)}, f32[8,128]{1,0:T(8,128)S(1)}, u32[]{:S(2)}, u32[]{:S(2)}) collective-permute-start(f32[8,128]{1,0:T(8,128)S(1)} %fusion.28), channel_id=1, source_target_pairs={{0,16},{1,17},{2,18},{3,19},{4,20},{5,21},{6,22},{7,23},{8,24},{9,... | collective-permute-start | bytes 12296 | tf_op jit(solution)/shard_map/ppermute | solution.py:33
  92.8 5.8 %collective-permute-start.20 = (f32[64,1152]{1,0:T(8,128)S(1)}, f32[64,1152]{1,0:T(8,128)S(1)}, u32[]{:S(2)}, u32[]{:S(2)}) collective-permute-start(f32[64,1152]{1,0:T(8,128)S(1)} %slice.182), channel_id=1, source_target_pairs={{0,8},{1,9},{2,10},{3,11},{4,12},{5,13},{6,14},{7,15},{8,0},{9,1},... | collective-permute-start | bytes 884744 | tf_op jit(solution)/shard_map/ppermute | solution.py:33
  (13 other events, 42.4 us)

commit v4 on v3

--- a/solution.py
+++ b/solution.py
@@ -116,7 +116,8 @@
     lay(imgs, x_ref)
     lay(txts, y_ref)
     scale = sc[0]
-    bias = sc[1]
+    slant = scale * LOG2E
+    offset = sc[1] * LOG2E
     lift = jnp.zeros((8, 256), F32)
     logs = jnp.zeros((8, 256), F32)
     slope_acc = jnp.zeros((8, 256), F32)
@@ -129,7 +130,7 @@
                 (((1,), (1,)), ((), ())),
                 preferred_element_type=F32,
             )
-            z = (scale * dots + bias) * LOG2E
+            z = slant * dots + offset
             if i == 0 and j == 0:
                 row = lax.broadcasted_iota(jnp.int32, (256, 256), 0)
                 col = lax.broadcasted_iota(jnp.int32, (256, 256), 1)
@@ -222,8 +223,7 @@
         name="pairs",
     )(scalars, *imgs, *txts)
 
-    sums = sums + sibling(sums)
-    w, sums = lax.optimization_barrier((w, sums))
+    sums = sums + flip_z(4, sums)
     keep, send = pl.pallas_call(
         image_kernel,
         in_specs=[vmem] * 2,
@@ -233,8 +233,8 @@
         cost_estimate=cost,
         name="images",
     )(w, y)
-    sums = sums + flip_z(4, sums)
-    w, keep = lax.optimization_barrier((w, keep))
+    w, keep, sums = lax.optimization_barrier((w, keep, sums))
+    sums = sums + sibling(sums)
     t_own, t_back, t_fore, t_over = pl.pallas_call(
         text_kernel,
         in_specs=[vmem] * 2,

time: 101 us -> 100 us (0.990)
  waiting for transfers between devices: 27.8 us -> 25 us
  starting transfers between devices: 49.3 us -> 51.4 us
    ppermute x31, waiting for transfers between devices: 27.8 us -> 25 us  [permute(): return lax.ppermute(value, AXES, pairs)]
    ppermute x31, starting transfers between devices: 49.3 us -> 51.4 us  [permute(): return lax.ppermute(value, AXES, pairs)]
  transfers between devices with their start and end apart: 31 -> 31, of which waited for: 15 -> 13; matrix products, arithmetic and copies ran while one was open for 2% -> 2% of each run, Pallas kernels for 4% -> 7%
where the time goes in v4:
time: 100 us; the launch traced here: 99.4 us
  starting transfers between devices  51.4 us (51%)
  waiting for transfers between devices  25 us (25%)
  Pallas kernels  14.6 us (15%)
  local copies, waits for them, and re-layouts  3.54 us (4%)
  other arithmetic  2.42 us (2%)
  between operations  2.41 us (2%)
    ppermute x31, starting transfers between devices, permute(): return lax.ppermute(value, AXES, pairs)  51.4 us
    ppermute x31, waiting for transfers between devices, permute(): return lax.ppermute(value, AXES, pairs)  25 us
    pallas_call x1, Pallas kernels, shards(): pl.pallas_call(pair_kernel, in_specs=[pl.BlockSpec(memory_space=pltpu.SME...  6.18 us
    unnamed x12, local copies, waits for them, and re-layouts  3.5 us
    pallas_call x1, Pallas kernels, shards(): pl.pallas_call(text_kernel, in_specs=[vmem] * 2, out_specs=[vmem] * 4, ou...  2.94 us
    pallas_call x1, Pallas kernels, shards(): pl.pallas_call(image_kernel, in_specs=[vmem] * 2, out_specs=[vmem] * 2, o...  2.89 us
  transfers between devices with their start and end apart: 31, of which 13 were waited for; matrix products, arithmetic and copies ran while one was open for 2% of the time, Pallas kernels for 7%

profile of v4, /device:TPU:1, one launch (start us, length us, event | category | flops | bytes accessed | tf_op | source)
XLA Modules:
  0.0 99.4 jit_solution(4354052620563851657)
XLA Ops:
  2.6 3.3 %collective-permute-start = (bf16[64,1152]{1,0:T(8,128)(2,1)S(1)}, bf16[64,1152]{1,0:T(8,128)(2,1)S(1)}, u32[]{:S(2)}, u32[]{:S(2)}) collective-permute-start(bf16[64,1152]{1,0:T(8,128)(2,1)S(1)} %get-tuple-element.33), channel_id=1, source_target_pairs={{0,8},{1,9},{2,10},{3,11},{4,12},{5,13},{6,14},{7,15},{8,0},{9,1},... | collective-permute-start | bytes 442376 | tf_op jit(solution)/shard_map/ppermute | solution.py:33
  7.0 4.4 %collective-permute-start.5 = (bf16[128,1152]{1,0:T(8,128)(2,1)S(1)}, bf16[128,1152]{1,0:T(8,128)(2,1)S(1)}, u32[]{:S(2)}, u32[]{:S(2)}) collective-permute-start(bf16[128,1152]{1,0:T(8,128)(2,1)S(1)} %pad_maximum_fusion.4.refs_0_), channel_id=1, source_target_pairs={{0,32},{1,33},{2,34},{3,35},{4,36},{5,37},{6,38},{7,39},{8,41},{9,... | collective-permute-start | bytes 884744 | tf_op jit(solution)/shard_map/ppermute | solution.py:33
  11.3 2.9 %collective-permute-start.3 = (bf16[64,1152]{1,0:T(8,128)(2,1)S(1)}, bf16[64,1152]{1,0:T(8,128)(2,1)S(1)}, u32[]{:S(2)}, u32[]{:S(2)}) collective-permute-start(bf16[64,1152]{1,0:T(8,128)(2,1)S(1)} %get-tuple-element.35), channel_id=1, source_target_pairs={{0,4},{1,5},{2,6},{3,7},{4,0},{5,1},{6,2},{7,3},{8,136},{9,137},{1... | collective-permute-start | bytes 442376 | tf_op jit(solution)/shard_map/ppermute | solution.py:33
  17.3 1.8 %collective-permute-done.2 = bf16[64,1152]{1,0:T(8,128)(2,1)S(1)} collective-permute-done((bf16[64,1152]{1,0:T(8,128)(2,1)S(1)}, bf16[64,1152]{1,0:T(8,128)(2,1)S(1)}, u32[]{:S(2)}, u32[]{:S(2)}) %collective-permute-start.2) | collective-permute-done | bytes 147488 | tf_op jit(solution)/shard_map/ppermute | solution.py:33
  20.3 1.6 %collective-permute-start.4 = (bf16[128,1152]{1,0:T(8,128)(2,1)S(1)}, bf16[128,1152]{1,0:T(8,128)(2,1)S(1)}, u32[]{:S(2)}, u32[]{:S(2)}) collective-permute-start(bf16[128,1152]{1,0:T(8,128)(2,1)S(1)} %pad_maximum_fusion.4.refs_0_), channel_id=1, source_target_pairs={{0,16},{1,17},{2,18},{3,19},{4,20},{5,21},{6,22},{7,23},{8,57},{9,... | collective-permute-start | bytes 884744 | tf_op jit(solution)/shard_map/ppermute | solution.py:33
  23.1 1.5 %collective-permute-start.13 = (bf16[256,1152]{1,0:T(8,128)(2,1)S(1)}, bf16[256,1152]{1,0:T(8,128)(2,1)S(1)}, u32[]{:S(2)}, u32[]{:S(2)}) collective-permute-start(bf16[256,1152]{1,0:T(8,128)(2,1)S(1)} %pad_maximum_fusion.3.refs_9_), channel_id=1, source_target_pairs={{0,192},{1,193},{2,194},{3,195},{4,196},{5,197},{6,198},{7,199},{8... | collective-permute-start | bytes 1769480 | tf_op jit(solution)/shard_map/ppermute | solution.py:33
  24.6 1.5 %collective-permute-start.14 = (bf16[256,1152]{1,0:T(8,128)(2,1)S(1)}, bf16[256,1152]{1,0:T(8,128)(2,1)S(1)}, u32[]{:S(2)}, u32[]{:S(2)}) collective-permute-start(bf16[256,1152]{1,0:T(8,128)(2,1)S(1)} %pad_maximum_fusion.3.refs_9_), channel_id=1, source_target_pairs={{0,128},{1,129},{2,130},{3,131},{4,132},{5,133},{6,134},{7,135},{8... | collective-permute-start | bytes 1769480 | tf_op jit(solution)/shard_map/ppermute | solution.py:33
  27.1 2.4 %collective-permute-start.7 = (bf16[128,1152]{1,0:T(8,128)(2,1)S(1)}, bf16[128,1152]{1,0:T(8,128)(2,1)}, u32[]{:S(2)}, u32[]{:S(2)}) collective-permute-start(bf16[128,1152]{1,0:T(8,128)(2,1)S(1)} %collective-permute-done.5.refs_3_), channel_id=1, source_target_pairs={{0,16},{1,17},{2,18},{3,19},{4,20},{5,21},{6,22},{7,23},{8,57},{9,... | collective-permute-start | bytes 884744 | tf_op jit(solution)/shard_map/ppermute | solution.py:33
  29.5 3.3 %collective-permute-done.8.refs_4_ = bf16[64,1152]{1,0:T(8,128)(2,1)} collective-permute-done((bf16[64,1152]{1,0:T(8,128)(2,1)S(1)}, bf16[64,1152]{1,0:T(8,128)(2,1)}, u32[]{:S(2)}, u32[]{:S(2)}) %collective-permute-start.8) | collective-permute-done | bytes 147488 | tf_op jit(solution)/shard_map/ppermute | solution.py:33
  32.8 2.0 %collective-permute-start.9 = (bf16[128,1152]{1,0:T(8,128)(2,1)S(1)}, bf16[128,1152]{1,0:T(8,128)(2,1)S(1)}, u32[]{:S(2)}, u32[]{:S(2)}) collective-permute-start(bf16[128,1152]{1,0:T(8,128)(2,1)S(1)} %collective-permute-done.4.refs_1_), channel_id=1, source_target_pairs={{0,8},{1,9},{2,10},{3,11},{4,12},{5,13},{6,14},{7,15},{8,0},{9,1},... | collective-permute-start | bytes 884744 | tf_op jit(solution)/shard_map/ppermute | solution.py:33
  36.1 3.4 %collective-permute-start.10 = (bf16[128,1152]{1,0:T(8,128)(2,1)}, bf16[128,1152]{1,0:T(8,128)(2,1)}, u32[]{:S(2)}, u32[]{:S(2)}) collective-permute-start(bf16[128,1152]{1,0:T(8,128)(2,1)} %collective-permute-done.7.refs_2_), channel_id=1, source_target_pairs={{0,8},{1,9},{2,10},{3,11},{4,12},{5,13},{6,14},{7,15},{8,0},{9,1},... | collective-permute-start | bytes 884744 | tf_op jit(solution)/shard_map/ppermute | solution.py:33
  42.9 6.2 %pairs.1 = (bf16[1024,1024]{1,0:T(8,128)(2,1)S(1)}, bf16[1024,1152]{1,0:T(8,128)(2,1)S(1)}, bf16[1024,1152]{1,0:T(8,128)(2,1)S(1)}, f32[8,128]{1,0:T(8,128)S(1)}) custom-call(f32[2]{0:T(128)S(1)} %pad_maximum_fusion.8.sc, bf16[128,1152]{1,0:T(8,128)(2,1)S(1)} %pad_maximum_fusion.4.refs_0_, bf16[128,1152]{1,0:T(8,128)(2,1)S(1)} %collective-permute-done.4.refs_1_, ...), custom_call_target="tpu_custom_call" | custom-call | flops 2415919104 | bytes 7000000 | tf_op jit(solution)/shard_map/pairs/pallas_call | solution.py:216
  49.1 2.4 %collective-permute-start.15 = (f32[8,128]{1,0:T(8,128)S(1)}, f32[8,128]{1,0:T(8,128)S(1)}, u32[]{:S(2)}, u32[]{:S(2)}) collective-permute-start(f32[8,128]{1,0:T(8,128)S(1)} %get-tuple-element.44), channel_id=1, source_target_pairs={{0,1},{1,0},{2,3},{3,2},{4,5},{5,4},{6,7},{7,6},{8,9},{9,8},{10,11... | collective-permute-start | bytes 12296 | tf_op jit(solution)/shard_map/ppermute | solution.py:33
  51.4 2.9 %images.4 = (f32[576,1152]{1,0:T(8,128)S(1)}, f32[448,1152]{1,0:T(8,128)S(1)}) custom-call(bf16[1024,1024]{1,0:T(8,128)(2,1)S(1)} %get-tuple-element.48.w_ref, bf16[1024,1152]{1,0:T(8,128)(2,1)S(1)} %get-tuple-element.42.y_ref), custom_call_target="tpu_custom_call" | custom-call | flops 2415919104 | bytes 7000000 | tf_op jit(solution)/shard_map/images/pallas_call | solution.py:227
  56.9 2.9 %texts.3 = (f32[256,1152]{1,0:T(8,128)S(1)}, f32[256,1152]{1,0:T(8,128)S(1)}, f32[256,1152]{1,0:T(8,128)S(1)}, f32[256,1152]{1,0:T(8,128)S(1)}) custom-call(bf16[1024,1024]{1,0:T(8,128)(2,1)S(1)} %get-tuple-element.48.w_ref, bf16[1024,1152]{1,0:T(8,128)(2,1)S(1)} %get-tuple-element.49.x_ref), custom_call_target="tpu_custom_call" | custom-call | flops 2415919104 | bytes 7000000 | tf_op jit(solution)/shard_map/texts/pallas_call | solution.py:238
  62.2 1.6 %collective-permute-start.24 = (f16[264,1152]{1,0:T(8,128)(2,1)S(1)}, f16[264,1152]{1,0:T(8,128)(2,1)S(1)}, u32[]{:S(2)}, u32[]{:S(2)}) collective-permute-start(f16[264,1152]{1,0:T(8,128)(2,1)S(1)} %get-tuple-element.71), channel_id=1, source_target_pairs={{0,128},{1,129},{2,130},{3,131},{4,132},{5,133},{6,134},{7,135},{8... | collective-permute-start | bytes 1824776 | tf_op jit(solution)/shard_map/ppermute | solution.py:33
  64.4 3.2 %collective-permute-start.18 = (f16[64,1152]{1,0:T(8,128)(2,1)S(1)}, f16[64,1152]{1,0:T(8,128)(2,1)S(1)}, u32[]{:S(2)}, u32[]{:S(2)}) collective-permute-start(f16[64,1152]{1,0:T(8,128)(2,1)S(1)} %fusion.6), channel_id=1, source_target_pairs={{0,33},{1,32},{2,35},{3,34},{4,37},{5,36},{6,39},{7,38},{8,40},{9,... | collective-permute-start | bytes 442376 | tf_op jit(solution)/shard_map/ppermute | solution.py:33
  67.6 2.4 %collective-permute-done.22 = f16[264,1152]{1,0:T(8,128)(2,1)S(1)} collective-permute-done((f16[264,1152]{1,0:T(8,128)(2,1)S(1)}, f16[264,1152]{1,0:T(8,128)(2,1)S(1)}, u32[]{:S(2)}, u32[]{:S(2)}) %collective-permute-start.22) | collective-permute-done | bytes 608288 | tf_op jit(solution)/shard_map/ppermute | solution.py:33
  70.0 9.0 %collective-permute-done.23 = f16[264,1152]{1,0:T(8,128)(2,1)S(1)} collective-permute-done((f16[264,1152]{1,0:T(8,128)(2,1)S(1)}, f16[264,1152]{1,0:T(8,128)(2,1)S(1)}, u32[]{:S(2)}, u32[]{:S(2)}) %collective-permute-start.23) | collective-permute-done | bytes 608288 | tf_op jit(solution)/shard_map/ppermute | solution.py:33
  82.7 2.0 %collective-permute-start.25 = (f16[72,1152]{1,0:T(8,128)(2,1)S(1)}, f16[72,1152]{1,0:T(8,128)(2,1)S(1)}, u32[]{:S(2)}, u32[]{:S(2)}) collective-permute-start(f16[72,1152]{1,0:T(8,128)(2,1)S(1)} %get-tuple-element.68), channel_id=1, source_target_pairs={{0,6},{1,7},{2,0},{3,1},{4,2},{5,3},{6,4},{7,5},{8,200},{9,201},{1... | collective-permute-start | bytes 497672 | tf_op jit(solution)/shard_map/ppermute | solution.py:33
  85.8 1.7 %collective-permute-done.26 = f16[72,1152]{1,0:T(8,128)(2,1)S(1)} collective-permute-done((f16[72,1152]{1,0:T(8,128)(2,1)S(1)}, f16[72,1152]{1,0:T(8,128)(2,1)S(1)}, u32[]{:S(2)}, u32[]{:S(2)}) %collective-permute-start.26) | collective-permute-done | bytes 165920 | tf_op jit(solution)/shard_map/ppermute | solution.py:33
  87.6 2.8 %collective-permute-start.30 = (f32[8,128]{1,0:T(8,128)S(1)}, f32[8,128]{1,0:T(8,128)S(1)}, u32[]{:S(2)}, u32[]{:S(2)}) collective-permute-start(f32[8,128]{1,0:T(8,128)S(1)} %fusion.28), channel_id=1, source_target_pairs={{0,48},{1,49},{2,50},{3,51},{4,52},{5,53},{6,54},{7,55},{8,56},{9,... | collective-permute-start | bytes 12296 | tf_op jit(solution)/shard_map/ppermute | solution.py:33
  91.6 4.9 %collective-permute-start.20 = (f32[64,1152]{1,0:T(8,128)S(1)}, f32[64,1152]{1,0:T(8,128)S(1)}, u32[]{:S(2)}, u32[]{:S(2)}) collective-permute-start(f32[64,1152]{1,0:T(8,128)S(1)} %slice.182), channel_id=1, source_target_pairs={{0,8},{1,9},{2,10},{3,11},{4,12},{5,13},{6,14},{7,15},{8,0},{9,1},... | collective-permute-start | bytes 884744 | tf_op jit(solution)/shard_map/ppermute | solution.py:33
  97.7 1.5 %finish.1 = (f32[64,1152]{1,0:T(8,128)}, f32[1]{0:T(128)}, f32[1]{0:T(128)}, f32[1]{0:T(128)}) custom-call(f32[2]{0:T(128)S(1)} %pad_maximum_fusion.8.sc, bf16[64,1152]{1,0:T(8,128)(2,1)S(1)} %copy-done.3, f32[64,1152]{1,0:T(8,128)S(1)} %slice_add_fusion.3.img_dir, f32[8,128]{1,0:T(8,128)S(1)} %add_add_fusion.sums), custom_call_target="tpu_custom_call" | custom-call | tf_op jit(solution)/shard_map/finish/pallas_call | solution.py:276
  (89 shorter events, 25.4 us)
Async XLA Ops:
  7.0 9.9 %collective-permute-start.5 = (bf16[128,1152]{1,0:T(8,128)(2,1)S(1)}, bf16[128,1152]{1,0:T(8,128)(2,1)S(1)}, u32[]{:S(2)}, u32[]{:S(2)}) collective-permute-start(bf16[128,1152]{1,0:T(8,128)(2,1)S(1)} %pad_maximum_fusion.4.refs_0_), channel_id=1, source_target_pairs={{0,32},{1,33},{2,34},{3,35},{4,36},{5,37},{6,38},{7,39},{8,41},{9,... | collective-permute-start | bytes 884744 | tf_op jit(solution)/shard_map/ppermute | solution.py:33
  11.3 5.9 %collective-permute-start.3 = (bf16[64,1152]{1,0:T(8,128)(2,1)S(1)}, bf16[64,1152]{1,0:T(8,128)(2,1)S(1)}, u32[]{:S(2)}, u32[]{:S(2)}) collective-permute-start(bf16[64,1152]{1,0:T(8,128)(2,1)S(1)} %get-tuple-element.35), channel_id=1, source_target_pairs={{0,4},{1,5},{2,6},{3,7},{4,0},{5,1},{6,2},{7,3},{8,136},{9,137},{1... | collective-permute-start | bytes 442376 | tf_op jit(solution)/shard_map/ppermute | solution.py:33
  16.9 9.2 %collective-permute-start.6 = (bf16[128,1152]{1,0:T(8,128)(2,1)S(1)}, bf16[128,1152]{1,0:T(8,128)(2,1)S(1)}, u32[]{:S(2)}, u32[]{:S(2)}) collective-permute-start(bf16[128,1152]{1,0:T(8,128)(2,1)S(1)} %collective-permute-done.5.refs_3_), channel_id=1, source_target_pairs={{0,8},{1,9},{2,10},{3,11},{4,12},{5,13},{6,14},{7,15},{8,0},{9,1},... | collective-permute-start | bytes 884744 | tf_op jit(solution)/shard_map/ppermute | solution.py:33
  20.3 6.8 %collective-permute-start.4 = (bf16[128,1152]{1,0:T(8,128)(2,1)S(1)}, bf16[128,1152]{1,0:T(8,128)(2,1)S(1)}, u32[]{:S(2)}, u32[]{:S(2)}) collective-permute-start(bf16[128,1152]{1,0:T(8,128)(2,1)S(1)} %pad_maximum_fusion.4.refs_0_), channel_id=1, source_target_pairs={{0,16},{1,17},{2,18},{3,19},{4,20},{5,21},{6,22},{7,23},{8,57},{9,... | collective-permute-start | bytes 884744 | tf_op jit(solution)/shard_map/ppermute | solution.py:33
  21.9 19.8 %collective-permute-start.12 = (bf16[256,1152]{1,0:T(8,128)(2,1)S(1)}, bf16[256,1152]{1,0:T(8,128)(2,1)S(1)}, u32[]{:S(2)}, u32[]{:S(2)}) collective-permute-start(bf16[256,1152]{1,0:T(8,128)(2,1)S(1)} %pad_maximum_fusion.3.refs_9_), channel_id=1, source_target_pairs={{0,64},{1,65},{2,66},{3,67},{4,68},{5,69},{6,70},{7,71},{8,10},{9,... | collective-permute-start | bytes 1769480 | tf_op jit(solution)/shard_map/ppermute | solution.py:33
  23.1 18.5 %collective-permute-start.13 = (bf16[256,1152]{1,0:T(8,128)(2,1)S(1)}, bf16[256,1152]{1,0:T(8,128)(2,1)S(1)}, u32[]{:S(2)}, u32[]{:S(2)}) collective-permute-start(bf16[256,1152]{1,0:T(8,128)(2,1)S(1)} %pad_maximum_fusion.3.refs_9_), channel_id=1, source_target_pairs={{0,192},{1,193},{2,194},{3,195},{4,196},{5,197},{6,198},{7,199},{8... | collective-permute-start | bytes 1769480 | tf_op jit(solution)/shard_map/ppermute | solution.py:33
  24.6 17.1 %collective-permute-start.14 = (bf16[256,1152]{1,0:T(8,128)(2,1)S(1)}, bf16[256,1152]{1,0:T(8,128)(2,1)S(1)}, u32[]{:S(2)}, u32[]{:S(2)}) collective-permute-start(bf16[256,1152]{1,0:T(8,128)(2,1)S(1)} %pad_maximum_fusion.3.refs_9_), channel_id=1, source_target_pairs={{0,128},{1,129},{2,130},{3,131},{4,132},{5,133},{6,134},{7,135},{8... | collective-permute-start | bytes 1769480 | tf_op jit(solution)/shard_map/ppermute | solution.py:33
  26.1 6.7 %collective-permute-start.8 = (bf16[64,1152]{1,0:T(8,128)(2,1)S(1)}, bf16[64,1152]{1,0:T(8,128)(2,1)}, u32[]{:S(2)}, u32[]{:S(2)}) collective-permute-start(bf16[64,1152]{1,0:T(8,128)(2,1)S(1)} %slice.132), channel_id=1, source_target_pairs={{0,32},{1,33},{2,34},{3,35},{4,36},{5,37},{6,38},{7,39},{8,41},{9,... | collective-permute-start | bytes 442376 | tf_op jit(solution)/shard_map/ppermute | solution.py:33
  27.1 9.0 %collective-permute-start.7 = (bf16[128,1152]{1,0:T(8,128)(2,1)S(1)}, bf16[128,1152]{1,0:T(8,128)(2,1)}, u32[]{:S(2)}, u32[]{:S(2)}) collective-permute-start(bf16[128,1152]{1,0:T(8,128)(2,1)S(1)} %collective-permute-done.5.refs_3_), channel_id=1, source_target_pairs={{0,16},{1,17},{2,18},{3,19},{4,20},{5,21},{6,22},{7,23},{8,57},{9,... | collective-permute-start | bytes 884744 | tf_op jit(solution)/shard_map/ppermute | solution.py:33
  32.8 6.7 %collective-permute-start.9 = (bf16[128,1152]{1,0:T(8,128)(2,1)S(1)}, bf16[128,1152]{1,0:T(8,128)(2,1)S(1)}, u32[]{:S(2)}, u32[]{:S(2)}) collective-permute-start(bf16[128,1152]{1,0:T(8,128)(2,1)S(1)} %collective-permute-done.4.refs_1_), channel_id=1, source_target_pairs={{0,8},{1,9},{2,10},{3,11},{4,12},{5,13},{6,14},{7,15},{8,0},{9,1},... | collective-permute-start | bytes 884744 | tf_op jit(solution)/shard_map/ppermute | solution.py:33
  36.1 5.8 %collective-permute-start.10 = (bf16[128,1152]{1,0:T(8,128)(2,1)}, bf16[128,1152]{1,0:T(8,128)(2,1)}, u32[]{:S(2)}, u32[]{:S(2)}) collective-permute-start(bf16[128,1152]{1,0:T(8,128)(2,1)} %collective-permute-done.7.refs_2_), channel_id=1, source_target_pairs={{0,8},{1,9},{2,10},{3,11},{4,12},{5,13},{6,14},{7,15},{8,0},{9,1},... | collective-permute-start | bytes 884744 | tf_op jit(solution)/shard_map/ppermute | solution.py:33
  49.1 6.5 %collective-permute-start.15 = (f32[8,128]{1,0:T(8,128)S(1)}, f32[8,128]{1,0:T(8,128)S(1)}, u32[]{:S(2)}, u32[]{:S(2)}) collective-permute-start(f32[8,128]{1,0:T(8,128)S(1)} %get-tuple-element.44), channel_id=1, source_target_pairs={{0,1},{1,0},{2,3},{3,2},{4,5},{5,4},{6,7},{7,6},{8,9},{9,8},{10,11... | collective-permute-start | bytes 12296 | tf_op jit(solution)/shard_map/ppermute | solution.py:33
  54.3 9.5 %collective-permute-start.16 = (f32[448,1152]{1,0:T(8,128)S(1)}, f32[448,1152]{1,0:T(8,128)S(1)}, u32[]{:S(2)}, u32[]{:S(2)}) collective-permute-start(f32[448,1152]{1,0:T(8,128)S(1)} %get-tuple-element.46), channel_id=1, source_target_pairs={{0,8},{1,9},{2,10},{3,11},{4,12},{5,13},{6,14},{7,15},{8,0},{9,1},... | collective-permute-start | bytes 6193160 | tf_op jit(solution)/shard_map/ppermute | solution.py:33
  60.7 9.3 %collective-permute-start.22 = (f16[264,1152]{1,0:T(8,128)(2,1)S(1)}, f16[264,1152]{1,0:T(8,128)(2,1)S(1)}, u32[]{:S(2)}, u32[]{:S(2)}) collective-permute-start(f16[264,1152]{1,0:T(8,128)(2,1)S(1)} %get-tuple-element.73), channel_id=1, source_target_pairs={{0,192},{1,193},{2,194},{3,195},{4,196},{5,197},{6,198},{7,199},{8... | collective-permute-start | bytes 1824776 | tf_op jit(solution)/shard_map/ppermute | solution.py:33
  62.1 17.0 %collective-permute-start.23 = (f16[264,1152]{1,0:T(8,128)(2,1)S(1)}, f16[264,1152]{1,0:T(8,128)(2,1)S(1)}, u32[]{:S(2)}, u32[]{:S(2)}) collective-permute-start(f16[264,1152]{1,0:T(8,128)(2,1)S(1)} %get-tuple-element.72), channel_id=1, source_target_pairs={{0,64},{1,65},{2,66},{3,67},{4,68},{5,69},{6,70},{7,71},{8,10},{9,... | collective-permute-start | bytes 1824776 | tf_op jit(solution)/shard_map/ppermute | solution.py:33
  62.2 16.8 %collective-permute-start.24 = (f16[264,1152]{1,0:T(8,128)(2,1)S(1)}, f16[264,1152]{1,0:T(8,128)(2,1)S(1)}, u32[]{:S(2)}, u32[]{:S(2)}) collective-permute-start(f16[264,1152]{1,0:T(8,128)(2,1)S(1)} %get-tuple-element.71), channel_id=1, source_target_pairs={{0,128},{1,129},{2,130},{3,131},{4,132},{5,133},{6,134},{7,135},{8... | collective-permute-start | bytes 1824776 | tf_op jit(solution)/shard_map/ppermute | solution.py:33
  64.2 14.8 %collective-permute-start.17 = (f16[256,1152]{1,0:T(8,128)(2,1)S(1)}, f16[256,1152]{1,0:T(8,128)(2,1)S(1)}, u32[]{:S(2)}, u32[]{:S(2)}) collective-permute-start(f16[256,1152]{1,0:T(8,128)(2,1)S(1)} %fusion), channel_id=1, source_target_pairs={{0,49},{1,48},{2,51},{3,50},{4,53},{5,52},{6,55},{7,54},{8,24},{9,... | collective-permute-start | bytes 1769480 | tf_op jit(solution)/shard_map/ppermute | solution.py:33
  64.4 14.7 %collective-permute-start.18 = (f16[64,1152]{1,0:T(8,128)(2,1)S(1)}, f16[64,1152]{1,0:T(8,128)(2,1)S(1)}, u32[]{:S(2)}, u32[]{:S(2)}) collective-permute-start(f16[64,1152]{1,0:T(8,128)(2,1)S(1)} %fusion.6), channel_id=1, source_target_pairs={{0,33},{1,32},{2,35},{3,34},{4,37},{5,36},{6,39},{7,38},{8,40},{9,... | collective-permute-start | bytes 442376 | tf_op jit(solution)/shard_map/ppermute | solution.py:33
  79.7 6.1 %collective-permute-start.27 = (f16[72,1152]{1,0:T(8,128)(2,1)S(1)}, f16[72,1152]{1,0:T(8,128)(2,1)S(1)}, u32[]{:S(2)}, u32[]{:S(2)}) collective-permute-start(f16[72,1152]{1,0:T(8,128)(2,1)S(1)} %get-tuple-element.70), channel_id=1, source_target_pairs={{0,4},{1,5},{2,6},{3,7},{4,0},{5,1},{6,2},{7,3},{8,136},{9,137},{1... | collective-permute-start | bytes 497672 | tf_op jit(solution)/shard_map/ppermute | solution.py:33
  81.2 10.2 %collective-permute-start.19 = (f16[128,1152]{1,0:T(8,128)(2,1)S(1)}, f16[128,1152]{1,0:T(8,128)(2,1)S(1)}, u32[]{:S(2)}, u32[]{:S(2)}) collective-permute-start(f16[128,1152]{1,0:T(8,128)(2,1)S(1)} %fusion.2), channel_id=1, source_target_pairs={{0,33},{1,32},{2,35},{3,34},{4,37},{5,36},{6,39},{7,38},{8,40},{9,... | collective-permute-start | bytes 884744 | tf_op jit(solution)/shard_map/ppermute | solution.py:33
  87.6 10.0 %collective-permute-start.30 = (f32[8,128]{1,0:T(8,128)S(1)}, f32[8,128]{1,0:T(8,128)S(1)}, u32[]{:S(2)}, u32[]{:S(2)}) collective-permute-start(f32[8,128]{1,0:T(8,128)S(1)} %fusion.28), channel_id=1, source_target_pairs={{0,48},{1,49},{2,50},{3,51},{4,52},{5,53},{6,54},{7,55},{8,56},{9,... | collective-permute-start | bytes 12296 | tf_op jit(solution)/shard_map/ppermute | solution.py:33
  90.3 7.2 %collective-permute-start.29 = (f32[8,128]{1,0:T(8,128)S(1)}, f32[8,128]{1,0:T(8,128)S(1)}, u32[]{:S(2)}, u32[]{:S(2)}) collective-permute-start(f32[8,128]{1,0:T(8,128)S(1)} %fusion.28), channel_id=1, source_target_pairs={{0,32},{1,33},{2,34},{3,35},{4,36},{5,37},{6,38},{7,39},{8,40},{9,... | collective-permute-start | bytes 12296 | tf_op jit(solution)/shard_map/ppermute | solution.py:33
  91.2 6.4 %collective-permute-start.28 = (f32[8,128]{1,0:T(8,128)S(1)}, f32[8,128]{1,0:T(8,128)S(1)}, u32[]{:S(2)}, u32[]{:S(2)}) collective-permute-start(f32[8,128]{1,0:T(8,128)S(1)} %fusion.28), channel_id=1, source_target_pairs={{0,16},{1,17},{2,18},{3,19},{4,20},{5,21},{6,22},{7,23},{8,24},{9,... | collective-permute-start | bytes 12296 | tf_op jit(solution)/shard_map/ppermute | solution.py:33
  91.6 6.2 %collective-permute-start.20 = (f32[64,1152]{1,0:T(8,128)S(1)}, f32[64,1152]{1,0:T(8,128)S(1)}, u32[]{:S(2)}, u32[]{:S(2)}) collective-permute-start(f32[64,1152]{1,0:T(8,128)S(1)} %slice.182), channel_id=1, source_target_pairs={{0,8},{1,9},{2,10},{3,11},{4,12},{5,13},{6,14},{7,15},{8,0},{9,1},... | collective-permute-start | bytes 884744 | tf_op jit(solution)/shard_map/ppermute | solution.py:33
  (13 other events, 45.9 us)

commit v5 on v4

--- a/solution.py
+++ b/solution.py
@@ -201,7 +201,8 @@
     a, b, c = first(1, txt_low), first(-1, txt_low), first(2, txt_low)
     block = jnp.concatenate([txt_low, a, b, c], axis=0)
     block, pair = lax.optimization_barrier((block, pair))
-    ta, tb, tc = second(1, block), second(-1, block), second(2, block)
+    tc = second(2, block)
+    ta, tb = second(1, block), second(-1, block)
     r1 = along_z(1, pair)
     q1, q2 = sibling(r1), sibling(r2)
     r2, q2 = lax.optimization_barrier((r2, q2))
@@ -247,9 +248,9 @@
 
     codes = split(sums)
     out = [jnp.concatenate([low(v), codes], axis=0) for v in (t_back, t_fore, t_over)]
-    back = [second(k, v) for k, v in zip((-1, 1, 2), out)]
-
-    chain = keep[128:] + sibling(send)
+    back = [second(k, v) for k, v in zip((2, -1, 1), (out[2], out[0], out[1]))]
+
+    chain = keep[128:] + sibling(low(send)).astype(F32) * UP
     z1 = along_z(-1, low(chain[:256]))
     z4 = along_z(-2, low(chain[384:]))
 

time: 100 us -> 99.8 us (level)
  transfers between devices with their start and end apart: 31 -> 31, of which waited for: 13 -> 15; matrix products, arithmetic and copies ran while one was open for 2% -> 2% of each run, Pallas kernels for 7% -> 7%
where the time goes in v5:
time: 99.8 us; the launch traced here: 99.6 us
  starting transfers between devices  52.3 us (52%)
  waiting for transfers between devices  24.2 us (24%)
  Pallas kernels  14.6 us (15%)
  local copies, waits for them, and re-layouts  3.54 us (4%)
  other arithmetic  2.58 us (3%)
  between operations  2.4 us (2%)
    ppermute x31, starting transfers between devices, permute(): return lax.ppermute(value, AXES, pairs)  52.3 us
    ppermute x31, waiting for transfers between devices, permute(): return lax.ppermute(value, AXES, pairs)  24.2 us
    pallas_call x1, Pallas kernels, shards(): pl.pallas_call(pair_kernel, in_specs=[pl.BlockSpec(memory_space=pltpu.SME...  6.16 us
    unnamed x12, local copies, waits for them, and re-layouts  3.5 us
    pallas_call x1, Pallas kernels, shards(): pl.pallas_call(text_kernel, in_specs=[vmem] * 2, out_specs=[vmem] * 4, ou...  2.95 us
    pallas_call x1, Pallas kernels, shards(): pl.pallas_call(image_kernel, in_specs=[vmem] * 2, out_specs=[vmem] * 2, o...  2.89 us
  transfers between devices with their start and end apart: 31, of which 15 were waited for; matrix products, arithmetic and copies ran while one was open for 2% of the time, Pallas kernels for 7%

profile of v5, /device:TPU:1, one launch (start us, length us, event | category | flops | bytes accessed | tf_op | source)
XLA Modules:
  0.0 99.6 jit_solution(17403684571464374692)
XLA Ops:
  2.6 3.3 %collective-permute-start = (bf16[64,1152]{1,0:T(8,128)(2,1)S(1)}, bf16[64,1152]{1,0:T(8,128)(2,1)S(1)}, u32[]{:S(2)}, u32[]{:S(2)}) collective-permute-start(bf16[64,1152]{1,0:T(8,128)(2,1)S(1)} %get-tuple-element.33), channel_id=1, source_target_pairs={{0,8},{1,9},{2,10},{3,11},{4,12},{5,13},{6,14},{7,15},{8,0},{9,1},... | collective-permute-start | bytes 442376 | tf_op jit(solution)/shard_map/ppermute | solution.py:33
  7.0 4.4 %collective-permute-start.5 = (bf16[128,1152]{1,0:T(8,128)(2,1)S(1)}, bf16[128,1152]{1,0:T(8,128)(2,1)S(1)}, u32[]{:S(2)}, u32[]{:S(2)}) collective-permute-start(bf16[128,1152]{1,0:T(8,128)(2,1)S(1)} %pad_maximum_fusion.4.refs_0_), channel_id=1, source_target_pairs={{0,32},{1,33},{2,34},{3,35},{4,36},{5,37},{6,38},{7,39},{8,41},{9,... | collective-permute-start | bytes 884744 | tf_op jit(solution)/shard_map/ppermute | solution.py:33
  11.3 2.9 %collective-permute-start.3 = (bf16[64,1152]{1,0:T(8,128)(2,1)S(1)}, bf16[64,1152]{1,0:T(8,128)(2,1)S(1)}, u32[]{:S(2)}, u32[]{:S(2)}) collective-permute-start(bf16[64,1152]{1,0:T(8,128)(2,1)S(1)} %get-tuple-element.35), channel_id=1, source_target_pairs={{0,4},{1,5},{2,6},{3,7},{4,0},{5,1},{6,2},{7,3},{8,136},{9,137},{1... | collective-permute-start | bytes 442376 | tf_op jit(solution)/shard_map/ppermute | solution.py:33
  17.3 1.8 %collective-permute-done.2 = bf16[64,1152]{1,0:T(8,128)(2,1)S(1)} collective-permute-done((bf16[64,1152]{1,0:T(8,128)(2,1)S(1)}, bf16[64,1152]{1,0:T(8,128)(2,1)S(1)}, u32[]{:S(2)}, u32[]{:S(2)}) %collective-permute-start.2) | collective-permute-done | bytes 147488 | tf_op jit(solution)/shard_map/ppermute | solution.py:33
  20.3 1.6 %collective-permute-start.4 = (bf16[128,1152]{1,0:T(8,128)(2,1)S(1)}, bf16[128,1152]{1,0:T(8,128)(2,1)S(1)}, u32[]{:S(2)}, u32[]{:S(2)}) collective-permute-start(bf16[128,1152]{1,0:T(8,128)(2,1)S(1)} %pad_maximum_fusion.4.refs_0_), channel_id=1, source_target_pairs={{0,16},{1,17},{2,18},{3,19},{4,20},{5,21},{6,22},{7,23},{8,57},{9,... | collective-permute-start | bytes 884744 | tf_op jit(solution)/shard_map/ppermute | solution.py:33
  23.1 1.5 %collective-permute-start.13 = (bf16[256,1152]{1,0:T(8,128)(2,1)S(1)}, bf16[256,1152]{1,0:T(8,128)(2,1)S(1)}, u32[]{:S(2)}, u32[]{:S(2)}) collective-permute-start(bf16[256,1152]{1,0:T(8,128)(2,1)S(1)} %pad_maximum_fusion.3.refs_9_), channel_id=1, source_target_pairs={{0,192},{1,193},{2,194},{3,195},{4,196},{5,197},{6,198},{7,199},{8... | collective-permute-start | bytes 1769480 | tf_op jit(solution)/shard_map/ppermute | solution.py:33
  24.6 1.5 %collective-permute-start.14 = (bf16[256,1152]{1,0:T(8,128)(2,1)S(1)}, bf16[256,1152]{1,0:T(8,128)(2,1)S(1)}, u32[]{:S(2)}, u32[]{:S(2)}) collective-permute-start(bf16[256,1152]{1,0:T(8,128)(2,1)S(1)} %pad_maximum_fusion.3.refs_9_), channel_id=1, source_target_pairs={{0,128},{1,129},{2,130},{3,131},{4,132},{5,133},{6,134},{7,135},{8... | collective-permute-start | bytes 1769480 | tf_op jit(solution)/shard_map/ppermute | solution.py:33
  27.1 2.4 %collective-permute-start.7 = (bf16[128,1152]{1,0:T(8,128)(2,1)S(1)}, bf16[128,1152]{1,0:T(8,128)(2,1)}, u32[]{:S(2)}, u32[]{:S(2)}) collective-permute-start(bf16[128,1152]{1,0:T(8,128)(2,1)S(1)} %collective-permute-done.5.refs_3_), channel_id=1, source_target_pairs={{0,16},{1,17},{2,18},{3,19},{4,20},{5,21},{6,22},{7,23},{8,57},{9,... | collective-permute-start | bytes 884744 | tf_op jit(solution)/shard_map/ppermute | solution.py:33
  29.5 3.3 %collective-permute-done.8.refs_4_ = bf16[64,1152]{1,0:T(8,128)(2,1)} collective-permute-done((bf16[64,1152]{1,0:T(8,128)(2,1)S(1)}, bf16[64,1152]{1,0:T(8,128)(2,1)}, u32[]{:S(2)}, u32[]{:S(2)}) %collective-permute-start.8) | collective-permute-done | bytes 147488 | tf_op jit(solution)/shard_map/ppermute | solution.py:33
  32.8 2.0 %collective-permute-start.9 = (bf16[128,1152]{1,0:T(8,128)(2,1)S(1)}, bf16[128,1152]{1,0:T(8,128)(2,1)S(1)}, u32[]{:S(2)}, u32[]{:S(2)}) collective-permute-start(bf16[128,1152]{1,0:T(8,128)(2,1)S(1)} %collective-permute-done.4.refs_1_), channel_id=1, source_target_pairs={{0,8},{1,9},{2,10},{3,11},{4,12},{5,13},{6,14},{7,15},{8,0},{9,1},... | collective-permute-start | bytes 884744 | tf_op jit(solution)/shard_map/ppermute | solution.py:33
  36.1 3.4 %collective-permute-start.10 = (bf16[128,1152]{1,0:T(8,128)(2,1)}, bf16[128,1152]{1,0:T(8,128)(2,1)}, u32[]{:S(2)}, u32[]{:S(2)}) collective-permute-start(bf16[128,1152]{1,0:T(8,128)(2,1)} %collective-permute-done.7.refs_2_), channel_id=1, source_target_pairs={{0,8},{1,9},{2,10},{3,11},{4,12},{5,13},{6,14},{7,15},{8,0},{9,1},... | collective-permute-start | bytes 884744 | tf_op jit(solution)/shard_map/ppermute | solution.py:33
  42.9 6.2 %pairs.1 = (bf16[1024,1024]{1,0:T(8,128)(2,1)S(1)}, bf16[1024,1152]{1,0:T(8,128)(2,1)S(1)}, bf16[1024,1152]{1,0:T(8,128)(2,1)S(1)}, f32[8,128]{1,0:T(8,128)S(1)}) custom-call(f32[2]{0:T(128)S(1)} %pad_maximum_fusion.8.sc, bf16[128,1152]{1,0:T(8,128)(2,1)S(1)} %pad_maximum_fusion.4.refs_0_, bf16[128,1152]{1,0:T(8,128)(2,1)S(1)} %collective-permute-done.4.refs_1_, ...), custom_call_target="tpu_custom_call" | custom-call | flops 2415919104 | bytes 7000000 | tf_op jit(solution)/shard_map/pairs/pallas_call | solution.py:217
  49.1 2.4 %collective-permute-start.15 = (f32[8,128]{1,0:T(8,128)S(1)}, f32[8,128]{1,0:T(8,128)S(1)}, u32[]{:S(2)}, u32[]{:S(2)}) collective-permute-start(f32[8,128]{1,0:T(8,128)S(1)} %get-tuple-element.44), channel_id=1, source_target_pairs={{0,1},{1,0},{2,3},{3,2},{4,5},{5,4},{6,7},{7,6},{8,9},{9,8},{10,11... | collective-permute-start | bytes 12296 | tf_op jit(solution)/shard_map/ppermute | solution.py:33
  51.4 2.9 %images.4 = (f32[576,1152]{1,0:T(8,128)S(1)}, f32[448,1152]{1,0:T(8,128)S(1)}) custom-call(bf16[1024,1024]{1,0:T(8,128)(2,1)S(1)} %get-tuple-element.48.w_ref, bf16[1024,1152]{1,0:T(8,128)(2,1)S(1)} %get-tuple-element.42.y_ref), custom_call_target="tpu_custom_call" | custom-call | flops 2415919104 | bytes 7000000 | tf_op jit(solution)/shard_map/images/pallas_call | solution.py:228
  56.9 3.0 %texts.3 = (f32[256,1152]{1,0:T(8,128)S(1)}, f32[256,1152]{1,0:T(8,128)S(1)}, f32[256,1152]{1,0:T(8,128)S(1)}, f32[256,1152]{1,0:T(8,128)S(1)}) custom-call(bf16[1024,1024]{1,0:T(8,128)(2,1)S(1)} %get-tuple-element.48.w_ref, bf16[1024,1152]{1,0:T(8,128)(2,1)S(1)} %get-tuple-element.49.x_ref), custom_call_target="tpu_custom_call" | custom-call | flops 2415919104 | bytes 7000000 | tf_op jit(solution)/shard_map/texts/pallas_call | solution.py:239
  60.7 1.6 %collective-permute-start.22 = (f16[264,1152]{1,0:T(8,128)(2,1)S(1)}, f16[264,1152]{1,0:T(8,128)(2,1)S(1)}, u32[]{:S(2)}, u32[]{:S(2)}) collective-permute-start(f16[264,1152]{1,0:T(8,128)(2,1)S(1)} %get-tuple-element.73), channel_id=1, source_target_pairs={{0,128},{1,129},{2,130},{3,131},{4,132},{5,133},{6,134},{7,135},{8... | collective-permute-start | bytes 1824776 | tf_op jit(solution)/shard_map/ppermute | solution.py:33
  64.4 3.2 %collective-permute-start.18 = (f16[64,1152]{1,0:T(8,128)(2,1)S(1)}, f16[64,1152]{1,0:T(8,128)(2,1)S(1)}, u32[]{:S(2)}, u32[]{:S(2)}) collective-permute-start(f16[64,1152]{1,0:T(8,128)(2,1)S(1)} %fusion.6), channel_id=1, source_target_pairs={{0,33},{1,32},{2,35},{3,34},{4,37},{5,36},{6,39},{7,38},{8,40},{9,... | collective-permute-start | bytes 442376 | tf_op jit(solution)/shard_map/ppermute | solution.py:33
  67.6 4.0 %collective-permute-done.22 = f16[264,1152]{1,0:T(8,128)(2,1)S(1)} collective-permute-done((f16[264,1152]{1,0:T(8,128)(2,1)S(1)}, f16[264,1152]{1,0:T(8,128)(2,1)S(1)}, u32[]{:S(2)}, u32[]{:S(2)}) %collective-permute-start.22) | collective-permute-done | bytes 608288 | tf_op jit(solution)/shard_map/ppermute | solution.py:33
  71.6 5.4 %collective-permute-done.23 = f16[264,1152]{1,0:T(8,128)(2,1)S(1)} collective-permute-done((f16[264,1152]{1,0:T(8,128)(2,1)S(1)}, f16[264,1152]{1,0:T(8,128)(2,1)S(1)}, u32[]{:S(2)}, u32[]{:S(2)}) %collective-permute-start.23) | collective-permute-done | bytes 608288 | tf_op jit(solution)/shard_map/ppermute | solution.py:33
  81.1 1.5 %collective-permute-start.26 = (f16[72,1152]{1,0:T(8,128)(2,1)S(1)}, f16[72,1152]{1,0:T(8,128)(2,1)S(1)}, u32[]{:S(2)}, u32[]{:S(2)}) collective-permute-start(f16[72,1152]{1,0:T(8,128)(2,1)S(1)} %get-tuple-element.69), channel_id=1, source_target_pairs={{0,2},{1,3},{2,4},{3,5},{4,6},{5,7},{6,0},{7,1},{8,72},{9,73},{10,... | collective-permute-start | bytes 497672 | tf_op jit(solution)/shard_map/ppermute | solution.py:33
  84.8 1.8 %collective-permute-done.26 = f16[72,1152]{1,0:T(8,128)(2,1)S(1)} collective-permute-done((f16[72,1152]{1,0:T(8,128)(2,1)S(1)}, f16[72,1152]{1,0:T(8,128)(2,1)S(1)}, u32[]{:S(2)}, u32[]{:S(2)}) %collective-permute-start.26) | collective-permute-done | bytes 165920 | tf_op jit(solution)/shard_map/ppermute | solution.py:33
  87.2 3.5 %collective-permute-start.30 = (f32[8,128]{1,0:T(8,128)S(1)}, f32[8,128]{1,0:T(8,128)S(1)}, u32[]{:S(2)}, u32[]{:S(2)}) collective-permute-start(f32[8,128]{1,0:T(8,128)S(1)} %fusion.28), channel_id=1, source_target_pairs={{0,48},{1,49},{2,50},{3,51},{4,52},{5,53},{6,54},{7,55},{8,56},{9,... | collective-permute-start | bytes 12296 | tf_op jit(solution)/shard_map/ppermute | solution.py:33
  91.2 5.5 %collective-permute-start.20 = (f32[64,1152]{1,0:T(8,128)S(1)}, f32[64,1152]{1,0:T(8,128)S(1)}, u32[]{:S(2)}, u32[]{:S(2)}) collective-permute-start(f32[64,1152]{1,0:T(8,128)S(1)} %slice.182), channel_id=1, source_target_pairs={{0,8},{1,9},{2,10},{3,11},{4,12},{5,13},{6,14},{7,15},{8,0},{9,1},... | collective-permute-start | bytes 884744 | tf_op jit(solution)/shard_map/ppermute | solution.py:33
  98.0 1.5 %finish.1 = (f32[64,1152]{1,0:T(8,128)}, f32[1]{0:T(128)}, f32[1]{0:T(128)}, f32[1]{0:T(128)}) custom-call(f32[2]{0:T(128)S(1)} %pad_maximum_fusion.8.sc, bf16[64,1152]{1,0:T(8,128)(2,1)S(1)} %copy-done.3, f32[64,1152]{1,0:T(8,128)S(1)} %slice_add_fusion.2.img_dir, f32[8,128]{1,0:T(8,128)S(1)} %add_add_fusion.sums), custom_call_target="tpu_custom_call" | custom-call | tf_op jit(solution)/shard_map/finish/pallas_call | solution.py:277
  (90 shorter events, 26.7 us)
Async XLA Ops:
  7.0 9.9 %collective-permute-start.5 = (bf16[128,1152]{1,0:T(8,128)(2,1)S(1)}, bf16[128,1152]{1,0:T(8,128)(2,1)S(1)}, u32[]{:S(2)}, u32[]{:S(2)}) collective-permute-start(bf16[128,1152]{1,0:T(8,128)(2,1)S(1)} %pad_maximum_fusion.4.refs_0_), channel_id=1, source_target_pairs={{0,32},{1,33},{2,34},{3,35},{4,36},{5,37},{6,38},{7,39},{8,41},{9,... | collective-permute-start | bytes 884744 | tf_op jit(solution)/shard_map/ppermute | solution.py:33
  11.3 5.9 %collective-permute-start.3 = (bf16[64,1152]{1,0:T(8,128)(2,1)S(1)}, bf16[64,1152]{1,0:T(8,128)(2,1)S(1)}, u32[]{:S(2)}, u32[]{:S(2)}) collective-permute-start(bf16[64,1152]{1,0:T(8,128)(2,1)S(1)} %get-tuple-element.35), channel_id=1, source_target_pairs={{0,4},{1,5},{2,6},{3,7},{4,0},{5,1},{6,2},{7,3},{8,136},{9,137},{1... | collective-permute-start | bytes 442376 | tf_op jit(solution)/shard_map/ppermute | solution.py:33
  16.9 9.2 %collective-permute-start.6 = (bf16[128,1152]{1,0:T(8,128)(2,1)S(1)}, bf16[128,1152]{1,0:T(8,128)(2,1)S(1)}, u32[]{:S(2)}, u32[]{:S(2)}) collective-permute-start(bf16[128,1152]{1,0:T(8,128)(2,1)S(1)} %collective-permute-done.5.refs_3_), channel_id=1, source_target_pairs={{0,8},{1,9},{2,10},{3,11},{4,12},{5,13},{6,14},{7,15},{8,0},{9,1},... | collective-permute-start | bytes 884744 | tf_op jit(solution)/shard_map/ppermute | solution.py:33
  20.3 6.8 %collective-permute-start.4 = (bf16[128,1152]{1,0:T(8,128)(2,1)S(1)}, bf16[128,1152]{1,0:T(8,128)(2,1)S(1)}, u32[]{:S(2)}, u32[]{:S(2)}) collective-permute-start(bf16[128,1152]{1,0:T(8,128)(2,1)S(1)} %pad_maximum_fusion.4.refs_0_), channel_id=1, source_target_pairs={{0,16},{1,17},{2,18},{3,19},{4,20},{5,21},{6,22},{7,23},{8,57},{9,... | collective-permute-start | bytes 884744 | tf_op jit(solution)/shard_map/ppermute | solution.py:33
  21.9 19.8 %collective-permute-start.12 = (bf16[256,1152]{1,0:T(8,128)(2,1)S(1)}, bf16[256,1152]{1,0:T(8,128)(2,1)S(1)}, u32[]{:S(2)}, u32[]{:S(2)}) collective-permute-start(bf16[256,1152]{1,0:T(8,128)(2,1)S(1)} %pad_maximum_fusion.3.refs_9_), channel_id=1, source_target_pairs={{0,64},{1,65},{2,66},{3,67},{4,68},{5,69},{6,70},{7,71},{8,10},{9,... | collective-permute-start | bytes 1769480 | tf_op jit(solution)/shard_map/ppermute | solution.py:33
  23.1 18.5 %collective-permute-start.13 = (bf16[256,1152]{1,0:T(8,128)(2,1)S(1)}, bf16[256,1152]{1,0:T(8,128)(2,1)S(1)}, u32[]{:S(2)}, u32[]{:S(2)}) collective-permute-start(bf16[256,1152]{1,0:T(8,128)(2,1)S(1)} %pad_maximum_fusion.3.refs_9_), channel_id=1, source_target_pairs={{0,192},{1,193},{2,194},{3,195},{4,196},{5,197},{6,198},{7,199},{8... | collective-permute-start | bytes 1769480 | tf_op jit(solution)/shard_map/ppermute | solution.py:33
  24.6 17.1 %collective-permute-start.14 = (bf16[256,1152]{1,0:T(8,128)(2,1)S(1)}, bf16[256,1152]{1,0:T(8,128)(2,1)S(1)}, u32[]{:S(2)}, u32[]{:S(2)}) collective-permute-start(bf16[256,1152]{1,0:T(8,128)(2,1)S(1)} %pad_maximum_fusion.3.refs_9_), channel_id=1, source_target_pairs={{0,128},{1,129},{2,130},{3,131},{4,132},{5,133},{6,134},{7,135},{8... | collective-permute-start | bytes 1769480 | tf_op jit(solution)/shard_map/ppermute | solution.py:33
  26.1 6.7 %collective-permute-start.8 = (bf16[64,1152]{1,0:T(8,128)(2,1)S(1)}, bf16[64,1152]{1,0:T(8,128)(2,1)}, u32[]{:S(2)}, u32[]{:S(2)}) collective-permute-start(bf16[64,1152]{1,0:T(8,128)(2,1)S(1)} %slice.132), channel_id=1, source_target_pairs={{0,32},{1,33},{2,34},{3,35},{4,36},{5,37},{6,38},{7,39},{8,41},{9,... | collective-permute-start | bytes 442376 | tf_op jit(solution)/shard_map/ppermute | solution.py:33
  27.1 9.0 %collective-permute-start.7 = (bf16[128,1152]{1,0:T(8,128)(2,1)S(1)}, bf16[128,1152]{1,0:T(8,128)(2,1)}, u32[]{:S(2)}, u32[]{:S(2)}) collective-permute-start(bf16[128,1152]{1,0:T(8,128)(2,1)S(1)} %collective-permute-done.5.refs_3_), channel_id=1, source_target_pairs={{0,16},{1,17},{2,18},{3,19},{4,20},{5,21},{6,22},{7,23},{8,57},{9,... | collective-permute-start | bytes 884744 | tf_op jit(solution)/shard_map/ppermute | solution.py:33
  32.8 6.7 %collective-permute-start.9 = (bf16[128,1152]{1,0:T(8,128)(2,1)S(1)}, bf16[128,1152]{1,0:T(8,128)(2,1)S(1)}, u32[]{:S(2)}, u32[]{:S(2)}) collective-permute-start(bf16[128,1152]{1,0:T(8,128)(2,1)S(1)} %collective-permute-done.4.refs_1_), channel_id=1, source_target_pairs={{0,8},{1,9},{2,10},{3,11},{4,12},{5,13},{6,14},{7,15},{8,0},{9,1},... | collective-permute-start | bytes 884744 | tf_op jit(solution)/shard_map/ppermute | solution.py:33
  36.1 5.8 %collective-permute-start.10 = (bf16[128,1152]{1,0:T(8,128)(2,1)}, bf16[128,1152]{1,0:T(8,128)(2,1)}, u32[]{:S(2)}, u32[]{:S(2)}) collective-permute-start(bf16[128,1152]{1,0:T(8,128)(2,1)} %collective-permute-done.7.refs_2_), channel_id=1, source_target_pairs={{0,8},{1,9},{2,10},{3,11},{4,12},{5,13},{6,14},{7,15},{8,0},{9,1},... | collective-permute-start | bytes 884744 | tf_op jit(solution)/shard_map/ppermute | solution.py:33
  49.1 6.5 %collective-permute-start.15 = (f32[8,128]{1,0:T(8,128)S(1)}, f32[8,128]{1,0:T(8,128)S(1)}, u32[]{:S(2)}, u32[]{:S(2)}) collective-permute-start(f32[8,128]{1,0:T(8,128)S(1)} %get-tuple-element.44), channel_id=1, source_target_pairs={{0,1},{1,0},{2,3},{3,2},{4,5},{5,4},{6,7},{7,6},{8,9},{9,8},{10,11... | collective-permute-start | bytes 12296 | tf_op jit(solution)/shard_map/ppermute | solution.py:33
  54.5 9.3 %collective-permute-start.16 = (f16[448,1152]{1,0:T(8,128)(2,1)S(1)}, f16[448,1152]{1,0:T(8,128)(2,1)S(1)}, u32[]{:S(2)}, u32[]{:S(2)}) collective-permute-start(f16[448,1152]{1,0:T(8,128)(2,1)S(1)} %multiply_convert_fusion), channel_id=1, source_target_pairs={{0,8},{1,9},{2,10},{3,11},{4,12},{5,13},{6,14},{7,15},{8,0},{9,1},... | collective-permute-start | bytes 3096584 | tf_op jit(solution)/shard_map/ppermute | solution.py:33
  60.7 10.9 %collective-permute-start.22 = (f16[264,1152]{1,0:T(8,128)(2,1)S(1)}, f16[264,1152]{1,0:T(8,128)(2,1)S(1)}, u32[]{:S(2)}, u32[]{:S(2)}) collective-permute-start(f16[264,1152]{1,0:T(8,128)(2,1)S(1)} %get-tuple-element.73), channel_id=1, source_target_pairs={{0,128},{1,129},{2,130},{3,131},{4,132},{5,133},{6,134},{7,135},{8... | collective-permute-start | bytes 1824776 | tf_op jit(solution)/shard_map/ppermute | solution.py:33
  62.4 14.6 %collective-permute-start.23 = (f16[264,1152]{1,0:T(8,128)(2,1)S(1)}, f16[264,1152]{1,0:T(8,128)(2,1)S(1)}, u32[]{:S(2)}, u32[]{:S(2)}) collective-permute-start(f16[264,1152]{1,0:T(8,128)(2,1)S(1)} %get-tuple-element.72), channel_id=1, source_target_pairs={{0,192},{1,193},{2,194},{3,195},{4,196},{5,197},{6,198},{7,199},{8... | collective-permute-start | bytes 1824776 | tf_op jit(solution)/shard_map/ppermute | solution.py:33
  63.7 14.4 %collective-permute-start.24 = (f16[264,1152]{1,0:T(8,128)(2,1)S(1)}, f16[264,1152]{1,0:T(8,128)(2,1)S(1)}, u32[]{:S(2)}, u32[]{:S(2)}) collective-permute-start(f16[264,1152]{1,0:T(8,128)(2,1)S(1)} %get-tuple-element.71), channel_id=1, source_target_pairs={{0,64},{1,65},{2,66},{3,67},{4,68},{5,69},{6,70},{7,71},{8,10},{9,... | collective-permute-start | bytes 1824776 | tf_op jit(solution)/shard_map/ppermute | solution.py:33
  64.2 13.8 %collective-permute-start.17 = (f16[256,1152]{1,0:T(8,128)(2,1)S(1)}, f16[256,1152]{1,0:T(8,128)(2,1)S(1)}, u32[]{:S(2)}, u32[]{:S(2)}) collective-permute-start(f16[256,1152]{1,0:T(8,128)(2,1)S(1)} %fusion), channel_id=1, source_target_pairs={{0,49},{1,48},{2,51},{3,50},{4,53},{5,52},{6,55},{7,54},{8,24},{9,... | collective-permute-start | bytes 1769480 | tf_op jit(solution)/shard_map/ppermute | solution.py:33
  64.4 13.7 %collective-permute-start.18 = (f16[64,1152]{1,0:T(8,128)(2,1)S(1)}, f16[64,1152]{1,0:T(8,128)(2,1)S(1)}, u32[]{:S(2)}, u32[]{:S(2)}) collective-permute-start(f16[64,1152]{1,0:T(8,128)(2,1)S(1)} %fusion.6), channel_id=1, source_target_pairs={{0,33},{1,32},{2,35},{3,34},{4,37},{5,36},{6,39},{7,38},{8,40},{9,... | collective-permute-start | bytes 442376 | tf_op jit(solution)/shard_map/ppermute | solution.py:33
  78.7 6.1 %collective-permute-start.27 = (f16[72,1152]{1,0:T(8,128)(2,1)S(1)}, f16[72,1152]{1,0:T(8,128)(2,1)S(1)}, u32[]{:S(2)}, u32[]{:S(2)}) collective-permute-start(f16[72,1152]{1,0:T(8,128)(2,1)S(1)} %get-tuple-element.70), channel_id=1, source_target_pairs={{0,4},{1,5},{2,6},{3,7},{4,0},{5,1},{6,2},{7,3},{8,136},{9,137},{1... | collective-permute-start | bytes 497672 | tf_op jit(solution)/shard_map/ppermute | solution.py:33
  80.1 10.9 %collective-permute-start.19 = (f16[128,1152]{1,0:T(8,128)(2,1)S(1)}, f16[128,1152]{1,0:T(8,128)(2,1)S(1)}, u32[]{:S(2)}, u32[]{:S(2)}) collective-permute-start(f16[128,1152]{1,0:T(8,128)(2,1)S(1)} %fusion.2), channel_id=1, source_target_pairs={{0,33},{1,32},{2,35},{3,34},{4,37},{5,36},{6,39},{7,38},{8,40},{9,... | collective-permute-start | bytes 884744 | tf_op jit(solution)/shard_map/ppermute | solution.py:33
  87.2 10.6 %collective-permute-start.30 = (f32[8,128]{1,0:T(8,128)S(1)}, f32[8,128]{1,0:T(8,128)S(1)}, u32[]{:S(2)}, u32[]{:S(2)}) collective-permute-start(f32[8,128]{1,0:T(8,128)S(1)} %fusion.28), channel_id=1, source_target_pairs={{0,48},{1,49},{2,50},{3,51},{4,52},{5,53},{6,54},{7,55},{8,56},{9,... | collective-permute-start | bytes 12296 | tf_op jit(solution)/shard_map/ppermute | solution.py:33
  90.6 7.1 %collective-permute-start.29 = (f32[8,128]{1,0:T(8,128)S(1)}, f32[8,128]{1,0:T(8,128)S(1)}, u32[]{:S(2)}, u32[]{:S(2)}) collective-permute-start(f32[8,128]{1,0:T(8,128)S(1)} %fusion.28), channel_id=1, source_target_pairs={{0,32},{1,33},{2,34},{3,35},{4,36},{5,37},{6,38},{7,39},{8,40},{9,... | collective-permute-start | bytes 12296 | tf_op jit(solution)/shard_map/ppermute | solution.py:33
  90.6 7.1 %collective-permute-start.28 = (f32[8,128]{1,0:T(8,128)S(1)}, f32[8,128]{1,0:T(8,128)S(1)}, u32[]{:S(2)}, u32[]{:S(2)}) collective-permute-start(f32[8,128]{1,0:T(8,128)S(1)} %fusion.28), channel_id=1, source_target_pairs={{0,16},{1,17},{2,18},{3,19},{4,20},{5,21},{6,22},{7,23},{8,24},{9,... | collective-permute-start | bytes 12296 | tf_op jit(solution)/shard_map/ppermute | solution.py:33
  91.2 6.7 %collective-permute-start.20 = (f32[64,1152]{1,0:T(8,128)S(1)}, f32[64,1152]{1,0:T(8,128)S(1)}, u32[]{:S(2)}, u32[]{:S(2)}) collective-permute-start(f32[64,1152]{1,0:T(8,128)S(1)} %slice.182), channel_id=1, source_target_pairs={{0,8},{1,9},{2,10},{3,11},{4,12},{5,13},{6,14},{7,15},{8,0},{9,1},... | collective-permute-start | bytes 884744 | tf_op jit(solution)/shard_map/ppermute | solution.py:33
  (13 other events, 46.6 us)
